TPU v7x, 128 devices: a whole 4x4x4 slice. The times are simulated.
128 devices in a mesh: dp: 32 (over x_lo, y, z), tensor: 4 (over x_hi, core).
Axes of the slice: x: 4 (x_hi: 2, x_lo: 2; x = x_hi * 2 + x_lo), y: 4, z: 4, core: 2. Of those that a mesh axis runs over, the one named last changes fastest.
Arguments:
- layer_input: bfloat16 [16384, 2048], P(('dp', 'tensor')), may hold values from -6 to 6
- cotangent: bfloat16 [16384, 2048], P(('dp', 'tensor')), may hold values from -6 to 6
- lengths: int32 [32], P('dp'), may hold values from 385 to 512
- expert_ids: int32 [16384, 8], P('dp'), may hold values from 0 to 9, all different within a row; in each aligned block of 512 rows (0 to 511, 512 to 1023, ...) at most 448 rows name the same one
- gains: bfloat16 [4, 2048], P(None, ('dp', 'tensor')), may hold values from 0.5 to 1.5
- w_qkv: bfloat16 [3, 2048, 2048], P(None, 'dp', 'tensor'), may hold values from -0.125 to 0.125
- w_out: bfloat16 [2048, 2048], P('tensor', 'dp'), may hold values from -1.75 to 1.75
- w_router: bfloat16 [2048, 10], P(('dp', 'tensor')), may hold values from -0.0625 to 0.0625
- w_gate_up: bfloat16 [10, 2, 2048, 1024], P(None, None, 'dp', 'tensor'), may hold values from -0.125 to 0.125
- w_down: bfloat16 [10, 1024, 2048], P(None, 'tensor', 'dp'), may hold values from -0.75 to 0.75
Outputs:
- output: bfloat16 [16384, 2048], P(('dp', 'tensor'))
- input_grad: float32 [16384, 2048], P(('dp', 'tensor'))
- gains_grad: float32 [4, 2048], P(None, ('dp', 'tensor'))
- qkv_grad: float32 [3, 2048, 2048], P(None, 'dp', 'tensor')
- out_grad: float32 [2048, 2048], P('tensor', 'dp')
- router_grad: float32 [2048, 10], P(('dp', 'tensor'))
- gate_up_grad: float32 [10, 2, 2048, 1024], P(None, None, 'dp', 'tensor')
- down_grad: float32 [10, 1024, 2048], P(None, 'tensor', 'dp')
Inputs may be any that keep to these rules, and one draw needn't show every extreme that they name: `expert_ids`: within the 512 rows of one sequence no expert is named by more than 448 rows, a bound that some block reaches.
All inputs are finite; a program needn't handle non-finite values.
Results may differ from a plain program's by a relative error of at most 0.03.
Values may be sent and summed in bfloat16 or wider, within the bound.
A program may use at most 320 MiB of HBM per device.

v0:
```python
import jax
import jax.numpy as jnp
from jax import lax
from jax.sharding import Mesh
from jax.sharding import PartitionSpec as P

HD = 128
TOPK = 8
E = 10
DP = ("dp_0", "dp_1", "dp_2")
DP_TENSOR = ("dp_0", "dp_1", "dp_2", "tensor")


epsilon = 1e-06
theta = 10000.0
precise = lax.Precision.HIGHEST


def joined_along(parts, dim):
    parts = jnp.moveaxis(parts, 0, dim)
    lengths = parts.shape
    return parts.reshape(*lengths[:dim], lengths[dim] * lengths[dim + 1], *lengths[dim + 2 :])


def copy_for_each(x, axis):
    devices = lax.axis_size(axis)
    return lax.all_to_all(jnp.broadcast_to(x[None], (devices, *x.shape)), axis, 0, 0, tiled=True)


def collect(x, axis, dim):
    return joined_along(copy_for_each(x, axis), dim)


def split_up(x, dim, devices):
    before, after = (x.shape[:dim], x.shape[dim + 1 :])
    return jnp.moveaxis(x.reshape(*before, devices, -1, *after), dim, 0)


def summed_on_arrival(x, axis, dim):
    devices = lax.axis_size(axis)
    parts = lax.all_to_all(split_up(x, dim, devices), axis, 0, 0, tiled=True)
    return jnp.sum(parts.astype(jnp.float32), axis=0)


def rows_first(arrays, axis, dims):
    turned = [jnp.moveaxis(a, dim, 0) for a, dim in zip(arrays, dims)]
    widths = [t[0].size for t in turned]
    both = jnp.concatenate([t.reshape(-1, w) for t, w in zip(turned, widths)], axis=1)
    whole = lax.all_gather(both, axis, axis=0, tiled=True)
    parts = jnp.split(whole, [sum(widths[:k]) for k in range(1, len(widths))], axis=1)
    return tuple(
        (
            jnp.moveaxis(b.reshape(-1, *t.shape[1:]), 0, dim)
            for b, t, dim in zip(parts, turned, dims)
        )
    )


def of_everyone(x, axis):
    everything = copy_for_each(x, axis)
    return jnp.sum(everything, axis=0)


def own_block(parts, axes, sequence):
    lengths = [lax.axis_size(a) for a in axes]
    parts = parts.reshape(*lengths, *parts.shape[1:])
    parts = parts.transpose(*sequence, *range(len(axes), parts.ndim))
    parts = parts.reshape(-1, *parts.shape[len(axes) :])
    for k in sequence:
        parts = lax.psum_scatter(parts, axes[k], scatter_dimension=0, tiled=True)
    return parts[0]


def summed_rows(x, axes, sequence, dim):
    devices = lax.axis_size(axes)
    return own_block(split_up(x, dim, devices), axes, sequence)


def one_scatter(arrays, axis, dims):
    devices = lax.axis_size(axis)
    parts = [split_up(a, dim, devices) for a, dim in zip(arrays, dims)]
    lines = jnp.concatenate([b.reshape(devices, -1) for b in parts], axis=1)
    rows = max(16, -(-lines.shape[1] // 1024) * 8)
    lines = jnp.pad(lines, ((0, 0), (0, rows * 128 - lines.shape[1]))).reshape(-1, 128)
    ravelled, at, finished = (lax.psum_scatter(lines, axis, tiled=True).reshape(-1), 0, [])
    for b in parts:
        part = b[0]
        finished.append(ravelled[at : at + part.size].reshape(part.shape))
        at += part.size
    return tuple(finished)


def rms_scale(value, gain):
    return value * lax.rsqrt(jnp.mean(value * value, axis=-1, keepdims=True) + epsilon) * gain


def rotary(length_all, head_dim):
    half_dim = head_dim // 2
    freqs = theta ** (-(jnp.arange(half_dim, dtype=jnp.float32) * 2.0 / head_dim))
    angles = jnp.arange(length_all, dtype=jnp.float32)[:, None] * freqs[None, :]
    return (jnp.cos(angles), jnp.sin(angles))


def head_post(projected, gain, cos_table, sin_table, factor):
    row_count = projected.shape[0]
    head_count = gain.shape[0] // HD
    shaped = projected.reshape(row_count, head_count, HD)
    normed = rms_scale(shaped, gain.reshape(head_count, HD))
    first = normed[..., : HD // 2]
    second = normed[..., HD // 2 :]
    cos_part = cos_table[:, None, :]
    sin_part = sin_table[:, None, :]
    turned = jnp.concatenate(
        [first * cos_part - second * sin_part, second * cos_part + first * sin_part], axis=-1
    )
    return (turned * factor).reshape(row_count, head_count * HD)


def route_tables(expert_ids, length, capacity):
    seq_len = expert_ids.shape[0]
    flat_ids = expert_ids.reshape(-1)
    route_index = jnp.arange(seq_len * TOPK, dtype=jnp.int32)
    token_index = route_index // TOPK
    live_route = token_index < length
    matches = (
        (flat_ids[:, None] == jnp.arange(E, dtype=jnp.int32)[None, :]) & live_route[:, None]
    ).astype(jnp.int32)
    before = jnp.cumsum(matches, axis=0) - matches
    place = jnp.sum(before * matches, axis=1)
    target = jnp.where(live_route, flat_ids * capacity + place, E * capacity)
    slot_token = jnp.zeros((E * capacity,), jnp.int32).at[target].set(token_index, mode="drop")
    slot_route = (
        jnp.full((E * capacity,), seq_len * TOPK, jnp.int32)
        .at[target]
        .set(route_index, mode="drop")
    )
    return (slot_token.reshape(E, capacity), slot_route.reshape(E, capacity))


def gated(gate_value, up_value):
    return jax.nn.silu(gate_value) * up_value


def gather_rows(value):
    return collect(value, "tensor", 0)


def scatter_rows(value):
    return summed_on_arrival(value.astype(jnp.bfloat16), "tensor", 0)


def attention_weights(w_qkv, w_out):
    return rows_first((w_qkv, w_out), DP, (1, 1))


def expert_weights(gate_up, down):
    return rows_first((gate_up, down), DP, (1, 1))


def local(
    layer_input, cotangent, lengths, expert_ids, gains, w_qkv, w_out, w_router, w_gate_up, w_down
):
    full_float = jnp.float32
    half_float = jnp.bfloat16
    tok_dev = layer_input.shape[0]
    groups = lax.axis_size("tensor")
    member = lax.axis_index("tensor")
    seq_len = tok_dev * groups
    capacity = seq_len - seq_len // 8
    length = lengths[0]
    own_rows = member * tok_dev
    all_gains, router = rows_first((gains, w_router), DP_TENSOR, (1, 0))
    gain_f = all_gains.astype(full_float)
    local_width = w_qkv.shape[2]
    head_start = member * local_width
    q_gain = lax.dynamic_slice_in_dim(gain_f[2], head_start, local_width)
    k_gain = lax.dynamic_slice_in_dim(gain_f[3], head_start, local_width)
    live = (jnp.arange(seq_len, dtype=jnp.int32) < length).astype(full_float)
    cos_table, sin_table = rotary(seq_len, HD)

    def post_query(projected, gain):
        return head_post(projected, gain, cos_table, sin_table, HD ** (-0.5))

    def post_key(projected, gain):
        return head_post(projected, gain, cos_table, sin_table, 1.0)

    input_float = layer_input.astype(full_float)
    normed_in = rms_scale(input_float, gain_f[0]).astype(half_float)
    gathered_in = gather_rows(normed_in)
    cot_all = gather_rows(cotangent)
    qkv_full, out_full = attention_weights(w_qkv, w_out)
    project = jnp.einsum("sd,cdf->csf", gathered_in, qkv_full, preferred_element_type=full_float)
    queries = post_query(project[0], q_gain).astype(half_float)
    keys = post_key(project[1], k_gain).astype(half_float)
    values = project[2].astype(half_float)
    head_count = local_width // HD
    key_heads = keys.reshape(seq_len, head_count, HD)
    value_heads = values.reshape(seq_len, head_count, HD)
    block = min(512, seq_len)
    blocks = seq_len // block
    query_blocks = queries.reshape(blocks, block, head_count, HD)

    def attend(query_block):
        scores = jnp.einsum(
            "qhd,khd->hqk", query_block, key_heads, preferred_element_type=full_float
        )
        highest = jnp.max(scores, axis=-1, keepdims=True)
        weights = jnp.exp(scores - highest) * live[None, None, :]
        total = jnp.sum(weights, axis=-1, keepdims=True)
        probs = (weights / total).astype(half_float)
        result = jnp.einsum("hqk,khd->qhd", probs, value_heads, preferred_element_type=full_float)
        return (result.astype(half_float), highest[..., 0] + jnp.log(total[..., 0]))

    attended_blocks, log_total = lax.map(attend, query_blocks)
    attended = attended_blocks.reshape(seq_len, local_width)
    branch = scatter_rows(jnp.dot(attended, out_full, preferred_element_type=full_float))
    state = input_float + branch
    normed_mid = rms_scale(state, gain_f[1]).astype(half_float)
    gathered_mid = gather_rows(normed_mid)
    logits = jnp.dot(gathered_mid, router, preferred_element_type=full_float)
    picks = (expert_ids[:, :, None] == jnp.arange(E, dtype=jnp.int32)[None, None, :]).astype(
        full_float
    )
    chosen = jnp.sum(logits[:, None, :] * picks, axis=-1)
    soft = jax.nn.softmax(chosen, axis=-1)
    gates = soft * live[:, None]
    slot_token, slot_route = route_tables(expert_ids, length, capacity)
    gate_pad = jnp.concatenate([gates.reshape(-1), jnp.zeros((1,), full_float)])
    slot_gate = gate_pad[slot_route]

    def expert_forward(mixed, pieces):
        gate_up, down, tokens, weight = pieces
        gate_up_full, down_full = expert_weights(gate_up, down)
        rows_in = gathered_mid[tokens]
        pre = jnp.einsum("cd,gdf->gcf", rows_in, gate_up_full, preferred_element_type=full_float)
        inner = gated(pre[0], pre[1]).astype(half_float)
        produced = jnp.dot(inner, down_full, preferred_element_type=full_float)
        intersection = jnp.sum(produced * cot_all[tokens].astype(full_float), axis=1)
        mixed = mixed.at[tokens].add(weight[:, None] * produced)
        saved = (pre, gate_up_full, down_full)
        return (mixed, (saved, intersection))

    mixed_all, (saved, intersections) = lax.scan(
        expert_forward,
        jnp.zeros((seq_len, layer_input.shape[1]), full_float),
        (w_gate_up, w_down, slot_token, slot_gate),
    )
    mixed = scatter_rows(mixed_all)
    output = (state + mixed).astype(half_float)
    intersection_all = of_everyone(intersections, "tensor")
    route_grad = (
        jnp.zeros((seq_len * TOPK + 1,), full_float)
        .at[slot_route.reshape(-1)]
        .add(intersection_all.reshape(-1))
    )
    soft_grad = route_grad[: seq_len * TOPK].reshape(seq_len, TOPK) * live[:, None]
    chosen_grad = soft * (soft_grad - jnp.sum(soft * soft_grad, axis=-1, keepdims=True))
    logit_grad = jnp.sum(chosen_grad[:, :, None] * picks, axis=1)
    own_logit_grad = lax.dynamic_slice_in_dim(logit_grad, own_rows, tok_dev)
    router_grad = jnp.dot(normed_mid.astype(full_float).T, own_logit_grad, precision=precise)
    mid_from_router = jnp.dot(own_logit_grad, router.astype(full_float).T, precision=precise)
    back_inputs = (saved[0], saved[1], saved[2], slot_token, slot_gate)

    def expert_backward(moved, pieces):
        pre, gate_up, down, tokens, weight = pieces
        gate_up_full, down_full = (gate_up, down)
        rows_in = gathered_mid[tokens]
        produced_grad = (weight[:, None] * cot_all[tokens].astype(full_float)).astype(half_float)
        inner_grad = jnp.einsum(
            "cd,fd->cf", produced_grad, down_full, preferred_element_type=full_float
        )
        inner, pullback = jax.vjp(gated, pre[0], pre[1])
        gate_grad, up_grad = pullback(inner_grad)
        pre_grad = jnp.stack([gate_grad, up_grad]).astype(half_float)
        down_grad = jnp.einsum(
            "cf,cd->fd", inner.astype(half_float), produced_grad, preferred_element_type=full_float
        )
        gate_up_grad = jnp.einsum(
            "cd,gcf->gdf", rows_in, pre_grad, preferred_element_type=full_float
        )
        rows_grad = jnp.einsum(
            "gcf,gdf->cd", pre_grad, gate_up_full, preferred_element_type=full_float
        )
        moved = moved.at[tokens].add(rows_grad)
        sent = (gate_up_grad, down_grad)
        return (moved, sent)

    moved_all, sent_all = lax.scan(
        expert_backward, jnp.zeros((seq_len, layer_input.shape[1]), full_float), back_inputs
    )
    gate_up_out, down_out = (
        summed_rows(sent_all[0].astype(jnp.bfloat16), DP, (1, 2, 0), 2).astype(jnp.float32),
        summed_rows(sent_all[1].astype(jnp.bfloat16), DP, (1, 2, 0), 2).astype(jnp.float32),
    )
    mid_grad = scatter_rows(moved_all) + mid_from_router
    mid_pull = jax.vjp(rms_scale, state, gain_f[1])[1]
    state_from_mid, mid_gain_grad = mid_pull(mid_grad)
    state_grad = cotangent.astype(full_float) + state_from_mid
    branch_grad = gather_rows(state_grad.astype(half_float))
    qkv_again, out_again = attention_weights(w_qkv, w_out)
    attended_grad = jnp.einsum(
        "sd,fd->sf", branch_grad, out_again, preferred_element_type=full_float
    ).astype(half_float)
    out_proj_grad = jnp.einsum(
        "sf,sd->fd", attended, branch_grad, preferred_element_type=full_float
    )
    grad_blocks = attended_grad.reshape(blocks, block, head_count, HD)

    def attend_back(carry, pieces):
        key_grad, value_grad = carry
        query_block, out_block, log_block = pieces
        scores = jnp.einsum(
            "qhd,khd->hqk", query_block, key_heads, preferred_element_type=full_float
        )
        probs = jnp.exp(scores - log_block[..., None]) * live[None, None, :]
        prob_grad = jnp.einsum(
            "qhd,khd->hqk", out_block, value_heads, preferred_element_type=full_float
        )
        inner_sum = jnp.sum(probs * prob_grad, axis=-1, keepdims=True)
        score_grad = (probs * (prob_grad - inner_sum)).astype(half_float)
        query_grad = jnp.einsum(
            "hqk,khd->qhd", score_grad, key_heads, preferred_element_type=full_float
        )
        key_grad = key_grad + jnp.einsum(
            "hqk,qhd->khd", score_grad, query_block, preferred_element_type=full_float
        )
        value_grad = value_grad + jnp.einsum(
            "hqk,qhd->khd", probs.astype(half_float), out_block, preferred_element_type=full_float
        )
        return ((key_grad, value_grad), query_grad)

    zero_heads = jnp.zeros((seq_len, head_count, HD), full_float)
    (key_grad, value_grad), query_grad = lax.scan(
        attend_back, (zero_heads, zero_heads), (query_blocks, grad_blocks, log_total)
    )
    query_pull = jax.vjp(post_query, project[0], q_gain)[1]
    query_proj_grad, q_gain_grad = query_pull(query_grad.reshape(seq_len, local_width))
    key_pull = jax.vjp(post_key, project[1], k_gain)[1]
    key_proj_grad, k_gain_grad = key_pull(key_grad.reshape(seq_len, local_width))
    proj_grad = jnp.stack(
        [query_proj_grad, key_proj_grad, value_grad.reshape(seq_len, local_width)]
    ).astype(half_float)
    qkv_weight_grad = jnp.einsum(
        "sd,csf->cdf", gathered_in, proj_grad, preferred_element_type=full_float
    )
    in_part = jnp.einsum("csf,cdf->sd", proj_grad, qkv_again, preferred_element_type=full_float)
    in_grad = scatter_rows(in_part)
    in_pull = jax.vjp(rms_scale, input_float, gain_f[0])[1]
    input_from_norm, in_gain_grad = in_pull(in_grad)
    input_grad = state_grad + input_from_norm
    head_grads = lax.dynamic_update_slice(
        jnp.zeros((2, gain_f.shape[1]), full_float),
        jnp.stack([q_gain_grad, k_gain_grad]),
        (jnp.zeros((), jnp.int32), head_start),
    )
    gain_grads = jnp.concatenate([jnp.stack([in_gain_grad, mid_gain_grad]), head_grads], axis=0)
    gains_out, router_out = one_scatter((gain_grads, router_grad), DP_TENSOR, (1, 0))
    qkv_out, out_proj_out = tuple(
        (
            part.astype(jnp.float32)
            for part in one_scatter(
                (qkv_weight_grad.astype(jnp.bfloat16), out_proj_grad.astype(jnp.bfloat16)),
                DP,
                (1, 1),
            )
        )
    )
    return (output, input_grad, gains_out, qkv_out, out_proj_out, router_out, gate_up_out, down_out)


def solution(mesh):
    split = Mesh(
        mesh.devices.reshape(2, 4, 4, mesh.shape["tensor"]), ("dp_0", "dp_1", "dp_2", "tensor")
    )
    placed = (
        P(DP_TENSOR, None),
        P(DP_TENSOR, None),
        P(DP),
        P(DP, None),
        P(None, DP_TENSOR),
        P(None, DP, "tensor"),
        P("tensor", DP),
        P(DP_TENSOR, None),
        P(None, None, DP, "tensor"),
        P(None, "tensor", DP),
    )
    return jax.shard_map(
        local,
        mesh=split,
        in_specs=placed,
        out_specs=(
            P(DP_TENSOR, None),
            P(DP_TENSOR, None),
            P(None, DP_TENSOR),
            P(None, DP, "tensor"),
            P("tensor", DP),
            P(DP_TENSOR, None),
            P(None, None, DP, "tensor"),
            P(None, "tensor", DP),
        ),
        check_vma=False,
    )
```

profile of v0, /device:TPU:1, one launch (start us, length us, event | category | flops | bytes accessed | tf_op | source)
XLA Modules:
  0.0 4076.5 jit_solution(348578323022258838)
XLA Ops:
  11.3 182.6 %all_gather.11 = bf16[2048,14]{1,0:T(8,128)(2,1)S(1)} all-gather(bf16[16,14]{1,0:T(8,128)(2,1)S(1)} %pad_maximum_fusion.14), channel_id=1, replica_groups=mesh['dp_0'=2,'dp_1'=4,'dp_2'=4,'tensor'=4] {'dp_0','dp_1','dp_2','tensor'}, dimensions={0}, use_global_device_ids=true | all-gather | bytes 57792 | tf_op jit(solution)/shard_map/all_gather | solution.py:49
  253.7 29.5 all_to_all.45
  287.4 16.4 all-to-all-start.2
  310.2 20.0 all-to-all-done.2
  337.3 15.5 scatter_custom_fusion.3
  353.0 15.5 scatter_custom_fusion.2
  370.4 23.5 gather_fusion.4
  396.5 1902.9 %while.7 = (s32[]{:T(128)}, f32[512,2048]{1,0:T(8,128)}, f32[10,2,448,256]{3,2,1,0:T(8,128)}, bf16[10,2,2048,256]{3,2,1,0:T(8,128)(2,1)}, bf16[10,256,2048]{1,2,...) while((s32[]{:T(128)}, f32[512,2048]{1,0:T(8,128)}, ...), condition=%wide.region_18.19_spmd, body=%wide.region_15.18_spmd.sunk | while | flops 1414760320 | bytes 80797464 | solution.py:243
  409.2 121.5 %all-gather.5.cloned.1.call-done = bf16[2048,768]{1,0:T(8,128)(2,1)} async-done(((bf16[64,768]{1,0:T(8,128)(2,1)}), bf16[2048,768]{1,0:T(8,128)(2,1)}) %all-gather.5.cloned.1.call-update) | async-done | bytes 3145744 | tf_op jit(solution)/shard_map/while/body/eval_jaxpr/all_gather | solution.py:49
  550.7 11.9 scatter_custom_fusion.15
  577.7 145.9 %all-gather.5.cloned.1.call-done = bf16[2048,768]{1,0:T(8,128)(2,1)} async-done(((bf16[64,768]{1,0:T(8,128)(2,1)}), bf16[2048,768]{1,0:T(8,128)(2,1)}) %all-gather.5.cloned.1.call-update) | async-done | bytes 3145744 | tf_op jit(solution)/shard_map/while/body/eval_jaxpr/all_gather | solution.py:49
  743.6 11.9 scatter_custom_fusion.15
  770.6 145.6 %all-gather.5.cloned.1.call-done = bf16[2048,768]{1,0:T(8,128)(2,1)} async-done(((bf16[64,768]{1,0:T(8,128)(2,1)}), bf16[2048,768]{1,0:T(8,128)(2,1)}) %all-gather.5.cloned.1.call-update) | async-done | bytes 3145744 | tf_op jit(solution)/shard_map/while/body/eval_jaxpr/all_gather | solution.py:49
  936.2 11.9 scatter_custom_fusion.15
  963.2 145.6 %all-gather.5.cloned.1.call-done = bf16[2048,768]{1,0:T(8,128)(2,1)} async-done(((bf16[64,768]{1,0:T(8,128)(2,1)}), bf16[2048,768]{1,0:T(8,128)(2,1)}) %all-gather.5.cloned.1.call-update) | async-done | bytes 3145744 | tf_op jit(solution)/shard_map/while/body/eval_jaxpr/all_gather | solution.py:49
  1128.7 11.9 scatter_custom_fusion.15
  1155.7 145.5 %all-gather.5.cloned.1.call-done = bf16[2048,768]{1,0:T(8,128)(2,1)} async-done(((bf16[64,768]{1,0:T(8,128)(2,1)}), bf16[2048,768]{1,0:T(8,128)(2,1)}) %all-gather.5.cloned.1.call-update) | async-done | bytes 3145744 | tf_op jit(solution)/shard_map/while/body/eval_jaxpr/all_gather | solution.py:49
  1321.2 11.9 scatter_custom_fusion.15
  1348.1 145.9 %all-gather.5.cloned.1.call-done = bf16[2048,768]{1,0:T(8,128)(2,1)} async-done(((bf16[64,768]{1,0:T(8,128)(2,1)}), bf16[2048,768]{1,0:T(8,128)(2,1)}) %all-gather.5.cloned.1.call-update) | async-done | bytes 3145744 | tf_op jit(solution)/shard_map/while/body/eval_jaxpr/all_gather | solution.py:49
  1514.0 11.9 scatter_custom_fusion.15
  1541.0 145.9 %all-gather.5.cloned.1.call-done = bf16[2048,768]{1,0:T(8,128)(2,1)} async-done(((bf16[64,768]{1,0:T(8,128)(2,1)}), bf16[2048,768]{1,0:T(8,128)(2,1)}) %all-gather.5.cloned.1.call-update) | async-done | bytes 3145744 | tf_op jit(solution)/shard_map/while/body/eval_jaxpr/all_gather | solution.py:49
  1706.9 11.9 scatter_custom_fusion.15
  1733.8 145.9 %all-gather.5.cloned.1.call-done = bf16[2048,768]{1,0:T(8,128)(2,1)} async-done(((bf16[64,768]{1,0:T(8,128)(2,1)}), bf16[2048,768]{1,0:T(8,128)(2,1)}) %all-gather.5.cloned.1.call-update) | async-done | bytes 3145744 | tf_op jit(solution)/shard_map/while/body/eval_jaxpr/all_gather | solution.py:49
  1899.7 11.9 scatter_custom_fusion.15
  1926.7 145.6 %all-gather.5.cloned.1.call-done = bf16[2048,768]{1,0:T(8,128)(2,1)} async-done(((bf16[64,768]{1,0:T(8,128)(2,1)}), bf16[2048,768]{1,0:T(8,128)(2,1)}) %all-gather.5.cloned.1.call-update) | async-done | bytes 3145744 | tf_op jit(solution)/shard_map/while/body/eval_jaxpr/all_gather | solution.py:49
  2092.2 11.9 scatter_custom_fusion.15
  2119.2 145.9 %all-gather.5.cloned.1.call-done = bf16[2048,768]{1,0:T(8,128)(2,1)} async-done(((bf16[64,768]{1,0:T(8,128)(2,1)}), bf16[2048,768]{1,0:T(8,128)(2,1)}) %all-gather.5.cloned.1.call-update) | async-done | bytes 3145744 | tf_op jit(solution)/shard_map/while/body/eval_jaxpr/all_gather | solution.py:49
  2285.1 11.9 scatter_custom_fusion.15
  2301.9 444.7 %while.8 = (s32[]{:T(128)}, f32[512,2048]{1,0:T(8,128)}, bf16[10,2,2048,256]{3,2,1,0:T(8,128)(2,1)}, bf16[10,256,2048]{1,2,0:T(8,128)(2,1)}, s32[10,448]{1,0:T(8...) while((s32[]{:T(128)}, f32[512,2048]{1,0:T(8,128)}, ...), condition=%wide.region_22.23_spmd, body=%wide.region_20.22_spmd.sunk | while | flops 2827749632 | bytes 43342752 | solution.py:288
  2330.9 11.8 scatter_custom_fusion.17
  2375.3 11.8 scatter_custom_fusion.17
  2419.8 11.8 scatter_custom_fusion.17
  2464.2 11.8 scatter_custom_fusion.17
  2508.6 11.8 scatter_custom_fusion.17
  2553.1 11.8 scatter_custom_fusion.17
  2597.5 11.8 scatter_custom_fusion.17
  2641.9 11.8 scatter_custom_fusion.17
  2686.3 11.8 scatter_custom_fusion.17
  2756.9 17.6 copy.286
  2774.5 100.4 %reduce-scatter.19.cloned.1.call-done = bf16[8,10,256,64]{2,3,1,0:T(8,128)(2,1)} async-done(((bf16[32,10,256,64]{2,3,1,0:T(8,128)(2,1)}), bf16[8,10,256,64]{2,3,1,0:T(8,128)(2,1)}) %reduce-scatter.19.cloned.1.call-update) | async-done | bytes 2621456 | tf_op jit(solution)/shard_map/reduce_scatter | solution.py:70
  2890.3 32.0 scatter_custom_fusion.4
  2922.7 136.3 %reduce-scatter.13.cloned.1.call-done = bf16[8,10,2,64,256]{4,3,2,1,0:T(8,128)(2,1)} async-done(((bf16[32,10,2,64,256]{4,3,2,1,0:T(8,128)(2,1)}), bf16[8,10,2,64,256]{4,3,2,1,0:T(8,128)(2,1)}) %reduce-scatter.13.cloned.1.call-update) | async-done | bytes 5242896 | tf_op jit(solution)/shard_map/reduce_scatter | solution.py:70
  3069.4 26.4 all-to-all-done.7
  3221.1 26.1 all-to-all-done.4
  3251.0 588.1 %reduce-scatter.9.cloned.1.call-done = f32[16,128]{1,0:T(8,128)} async-done(((f32[2048,128]{1,0:T(8,128)}), f32[16,128]{1,0:T(8,128)}) %reduce-scatter.9.cloned.1.call-update) | async-done | bytes 8208 | tf_op jit(solution)/shard_map/reduce_scatter | solution.py:85
  3842.0 157.5 %reduce-scatter.11.cloned.1.call-done = bf16[1024,128]{1,0:T(8,128)(2,1)} async-done(((bf16[32768,128]{1,0:T(8,128)(2,1)}), bf16[1024,128]{1,0:T(8,128)(2,1)}) %reduce-scatter.11.cloned.1.call-update) | async-done | bytes 262160 | tf_op jit(solution)/shard_map/reduce_scatter | solution.py:85
  4003.0 35.3 reduce-scatter.23.cloned.1.call-done
  4040.2 27.3 reduce-scatter.17.cloned.1.call-done
  (722 shorter events, 950.3 us)
Async XLA Ops:
  7.2 200.5 %all-gather.3.cloned.1.call-start = ((), (), s32[]{:S(2)}) async-start(), calls=%async_computation.17 | async-start | bytes 8650752 | tf_op jit(solution)/shard_map/all_gather | solution.py:49
  193.8 174.8 %copy-start.19 = (bf16[2048,14]{1,0:T(8,128)(2,1)}, bf16[2048,14]{1,0:T(8,128)(2,1)S(1)}, u32[]{:S(2)}) copy-start(bf16[2048,14]{1,0:T(8,128)(2,1)S(1)} %all_gather.11) | copy-start | bytes 172036
  198.1 85.8 %copy-start.45 = (f32[2048]{0:T(1024)}, f32[2048]{0:T(1024)S(1)}, u32[]{:S(2)}) copy-start(f32[2048]{0:T(1024)S(1)} %get-tuple-element.416) | copy-start | bytes 24580
  199.9 30.4 all-to-all-start
  205.9 38.7 copy-start.67
  205.9 39.4 copy-start.65
  206.0 163.6 %copy-start.55 = (f32[512]{0:T(512)}, f32[512]{0:T(512)S(1)}, u32[]{:S(2)}) copy-start(f32[512]{0:T(512)S(1)} %fusion.94) | copy-start | bytes 6148
  207.7 38.1 copy-start.31
  285.8 18.1 copy-start.43
  287.4 42.8 %copy-start.20 = (bf16[128,2048]{1,0:T(8,128)(2,1)S(1)}, bf16[128,2048]{1,0:T(8,128)(2,1)}, u32[]{:S(2)}) copy-start(bf16[128,2048]{1,0:T(8,128)(2,1)} %param.15) | copy-start | bytes 1572868
  287.4 42.7 %all-to-all-start.2 = ((bf16[4,128,2048]{2,1,0:T(8,128)(2,1)}), bf16[4,128,2048]{2,1,0:T(8,128)(2,1)S(1)}, u32[]{:S(2)}, u32[]{:S(2)}) async-start(bf16[4,128,2048]{2,1,0:T(8,128)(2,1)} %broadcast_in_dim.97), calls=%async_computation.2 | async-start | bytes 4194304 | tf_op jit(solution)/shard_map/all_to_all | solution.py:27
  331.8 62.2 %all-to-all-start.3 = ((bf16[4,128,2048]{2,1,0:T(8,128)(2,1)}), bf16[4,128,2048]{2,1,0:T(8,128)(2,1)}, u32[]{:S(2)}, u32[]{:S(2)}) async-start(bf16[4,128,2048]{2,1,0:T(8,128)(2,1)} %broadcast_in_dim.99), calls=%async_computation.3 | async-start | bytes 4194304 | tf_op jit(solution)/shard_map/all_to_all | solution.py:27
  352.8 41.1 %copy-start.47 = (s32[4480]{0:T(1024)}, s32[4480]{0:T(1024)S(1)}, u32[]{:S(2)}) copy-start(s32[4480]{0:T(1024)S(1)} %scatter_custom_fusion.3) | copy-start | bytes 53764
  369.5 24.4 copy-start.63
  370.1 23.8 copy-start.71
  396.5 134.3 %all-gather.5.cloned.1.call-start = ((), (), s32[]{:S(2)}) async-start(), calls=%async_computation.26 | async-start | bytes 3244032 | tf_op jit(solution)/shard_map/while/body/eval_jaxpr/all_gather | solution.py:49
  565.0 158.6 %all-gather.5.cloned.1.call-start = ((), (), s32[]{:S(2)}) async-start(), calls=%async_computation.26 | async-start | bytes 3244032 | tf_op jit(solution)/shard_map/while/body/eval_jaxpr/all_gather | solution.py:49
  757.9 158.3 %all-gather.5.cloned.1.call-start = ((), (), s32[]{:S(2)}) async-start(), calls=%async_computation.26 | async-start | bytes 3244032 | tf_op jit(solution)/shard_map/while/body/eval_jaxpr/all_gather | solution.py:49
  950.5 158.3 %all-gather.5.cloned.1.call-start = ((), (), s32[]{:S(2)}) async-start(), calls=%async_computation.26 | async-start | bytes 3244032 | tf_op jit(solution)/shard_map/while/body/eval_jaxpr/all_gather | solution.py:49
  1143.0 158.3 %all-gather.5.cloned.1.call-start = ((), (), s32[]{:S(2)}) async-start(), calls=%async_computation.26 | async-start | bytes 3244032 | tf_op jit(solution)/shard_map/while/body/eval_jaxpr/all_gather | solution.py:49
  1335.4 158.6 %all-gather.5.cloned.1.call-start = ((), (), s32[]{:S(2)}) async-start(), calls=%async_computation.26 | async-start | bytes 3244032 | tf_op jit(solution)/shard_map/while/body/eval_jaxpr/all_gather | solution.py:49
  1528.2 158.6 %all-gather.5.cloned.1.call-start = ((), (), s32[]{:S(2)}) async-start(), calls=%async_computation.26 | async-start | bytes 3244032 | tf_op jit(solution)/shard_map/while/body/eval_jaxpr/all_gather | solution.py:49
  1721.1 158.6 %all-gather.5.cloned.1.call-start = ((), (), s32[]{:S(2)}) async-start(), calls=%async_computation.26 | async-start | bytes 3244032 | tf_op jit(solution)/shard_map/while/body/eval_jaxpr/all_gather | solution.py:49
  1914.0 158.3 %all-gather.5.cloned.1.call-start = ((), (), s32[]{:S(2)}) async-start(), calls=%async_computation.26 | async-start | bytes 3244032 | tf_op jit(solution)/shard_map/while/body/eval_jaxpr/all_gather | solution.py:49
  2106.5 158.6 %all-gather.5.cloned.1.call-start = ((), (), s32[]{:S(2)}) async-start(), calls=%async_computation.26 | async-start | bytes 3244032 | tf_op jit(solution)/shard_map/while/body/eval_jaxpr/all_gather | solution.py:49
  2299.4 575.5 %reduce-scatter.19.cloned.1.call-start = ((), (), s32[]{:S(2)}) async-start(), calls=%async_computation.23 | async-start | bytes 13107200 | tf_op jit(solution)/shard_map/reduce_scatter | solution.py:70
  2756.8 302.2 %reduce-scatter.13.cloned.1.call-start = ((), (), s32[]{:S(2)}) async-start(), calls=%async_computation.20 | async-start | bytes 26214400 | tf_op jit(solution)/shard_map/reduce_scatter | solution.py:70
  2774.5 436.5 %reduce-scatter.21.cloned.1.call-start = ((), (), s32[]{:S(2)}) async-start(), calls=%async_computation.24 | async-start | bytes 3276800 | tf_op jit(solution)/shard_map/reduce_scatter | solution.py:70
  2875.6 10.0 all-to-all-start.6
  2884.4 38.3 copy-start.41
  2884.4 38.3 copy-start.56
  2884.4 38.3 copy-start.64
  2884.4 38.3 copy-start.72
  2885.6 173.5 %all-to-all-start.5 = ((bf16[4,128,2048]{2,1,0:T(8,128)(2,1)}), bf16[4,128,2048]{2,1,0:T(8,128)(2,1)S(1)}, u32[]{:S(2)}, u32[]{:S(2)}) async-start(bf16[4,128,2048]{2,1,0:T(8,128)(2,1)} %bitcast.54), calls=%async_computation.5 | async-start | bytes 4194304 | tf_op jit(solution)/shard_map/all_to_all | solution.py:41
  2890.2 168.8 %copy-start.44 = (s32[512,8]{0,1:T(8,128)S(1)}, s32[512,8]{0,1:T(8,128)}, u32[]{:S(2)}) copy-start(s32[512,8]{0,1:T(8,128)} %param.17) | copy-start | bytes 49156
  2890.2 330.1 %reduce-scatter.15.cloned.1.call-start = ((), (), s32[]{:S(2)}) async-start(), calls=%async_computation.21 | async-start | bytes 6553600 | tf_op jit(solution)/shard_map/reduce_scatter | solution.py:70
  3064.4 31.5 all-to-all-start.7
  3132.4 55.1 %all-to-all-start.8 = ((bf16[4,128,2048]{2,1,0:T(8,128)(2,1)}), bf16[4,128,2048]{2,1,0:T(8,128)(2,1)}, u32[]{:S(2)}, u32[]{:S(2)}) async-start(bf16[4,128,2048]{2,1,0:T(8,128)(2,1)} %bitcast.308), calls=%async_computation.8 | async-start | bytes 4194304 | tf_op jit(solution)/shard_map/all_to_all | solution.py:41
  3137.9 701.2 %reduce-scatter.9.cloned.1.call-start = ((), (), s32[]{:S(2)}) async-start(), calls=%async_computation.18 | async-start | bytes 1056768 | tf_op jit(solution)/shard_map/reduce_scatter | solution.py:85
  3181.2 9.4 copy-start.12
  3181.2 9.4 copy-start.50
  3181.2 9.4 copy-start.76
  3194.8 804.6 %reduce-scatter.11.cloned.1.call-start = ((), (), s32[]{:S(2)}) async-start(), calls=%async_computation.19 | async-start | bytes 8650752 | tf_op jit(solution)/shard_map/reduce_scatter | solution.py:85
  3211.0 827.3 %reduce-scatter.23.cloned.1.call-start = ((), (), s32[]{:S(2)}) async-start(), calls=%async_computation.25 | async-start | bytes 983040 | tf_op jit(solution)/shard_map/reduce_scatter | solution.py:70
  3215.4 33.9 copy-start.78
  3215.4 34.0 copy-start.22
  3215.4 31.7 all-to-all-start.4
  3220.3 847.2 %reduce-scatter.17.cloned.1.call-start = ((), (), s32[]{:S(2)}) async-start(), calls=%async_computation.22 | async-start | bytes 1966080 | tf_op jit(solution)/shard_map/reduce_scatter | solution.py:70
  (89 other events, 258.1 us)
Sparse Core Ops, SparseCore 0:
  10.2 151.5 all-gather.2
  399.6 131.1 all-gather.4
  568.0 155.4 all-gather.4
  760.6 155.4 all-gather.4
  953.2 155.4 all-gather.4
  1145.7 155.4 all-gather.4
  1338.5 155.4 all-gather.4
  1531.3 155.4 all-gather.4
  1724.2 155.4 all-gather.4
  1916.7 155.4 all-gather.4
  2109.5 155.4 all-gather.4
  2756.9 117.9 reduce-scatter.18
  2877.4 181.5 reduce-scatter.12
  3061.4 33.8 reduce-scatter.20
  3097.7 55.1 reduce-scatter.14
  3195.0 644.1 reduce-scatter.8
  3841.4 158.0 reduce-scatter.10
  4001.7 36.5 reduce-scatter.22
  4040.8 26.6 reduce-scatter.16
where the time goes:
time: 4080 us
  waiting for transfers between devices  2560 us (63%)
  local copies, waits for them, and re-layouts  648 us (16%)
  other arithmetic  329 us (8%)
  matrix products  258 us (6%)
  blocking collectives  212 us (5%)
  starting transfers between devices  51.1 us (1%)
    all_gather x11, waiting for transfers between devices, rows_first(): whole = lax.all_gather(both, axis, axis=0, tiled=True)  1430 us
    reduce_scatter x2, waiting for transfers between devices, one_scatter(): lax.psum_scatter(lines, axis, tiled=True).reshape(-1)  746 us
    reduce_scatter x6, waiting for transfers between devices, own_block(): parts = lax.psum_scatter(parts, axes[k], scatter_dimension=0, tiled=True)  299 us
    all_gather x1, blocking collectives, rows_first(): whole = lax.all_gather(both, axis, axis=0, tiled=True)  183 us
    scatter-add x10, other arithmetic, expert_forward(): mixed = mixed.at[tokens].add(weight[:, None] * produced)  119 us
    scatter-add x10, other arithmetic, expert_backward(): moved = moved.at[tokens].add(rows_grad)  118 us
  transfers between devices with their start and end apart: 27, of which 21 were waited for; matrix products, arithmetic and copies ran while one was open for 9% of the time, Pallas kernels for 0%

commit v1 on v0

v1 whole, which is shorter than its diff:
```python
import itertools

import jax
import jax.numpy as jnp
from jax import lax
from jax.sharding import Mesh
from jax.sharding import PartitionSpec as P

HD = 128
TOPK = 8
E = 10
D = 2048
SEQ = 512
BLK = 128
HALF_E = 5
FFS = 256
AXES = ("xl", "y", "z", "xh", "c")
SIZES = (2, 4, 4, 2, 2)
DP = ("xl", "y", "z")
DP_TENSOR = ("xl", "y", "z", "xh", "c")
epsilon = 1e-06
theta = 10000.0
precise = lax.Precision.HIGHEST
F32 = jnp.float32
BF16 = jnp.bfloat16


def shift(v, dx=0, dy=0, dz=0, dc=0):
    perm = []
    for xl, y, z, xh, c in itertools.product(*map(range, SIZES)):
        x = (xh * 2 + xl + dx) % 4
        to = (x % 2, (y + dy) % 4, (z + dz) % 4, x // 2, (c + dc) % 2)
        flat = lambda k: (((k[0] * 4 + k[1]) * 4 + k[2]) * 2 + k[3]) * 2 + k[4]
        perm.append((flat((xl, y, z, xh, c)), flat(to)))
    return lax.ppermute(v, AXES, perm)


def partner(v):
    perm = []
    for xl, y, z, xh, c in itertools.product(*map(range, SIZES)):
        flat = lambda k: (((k[0] * 4 + k[1]) * 4 + k[2]) * 2 + k[3]) * 2 + k[4]
        perm.append((flat((xl, y, z, xh, c)), flat((1 - xl, y, z, xh, c))))
    return lax.ppermute(v, AXES, perm)


def tied(value, *others):
    return lax.optimization_barrier((value, *others))[0]


def at(v, index, dim):
    return lax.dynamic_index_in_dim(v, index, dim, keepdims=False)


def ring_gather(v, axis, index, dim):
    shape = v.shape[:dim] + (4,) + v.shape[dim:]
    out = jnp.zeros(shape, v.dtype)
    out = lax.dynamic_update_index_in_dim(out, v, index, dim)
    for k in (1, 3, 2):
        got = shift(v, **{"d" + axis: k})
        out = lax.dynamic_update_index_in_dim(out, got, (index + 4 - k) % 4, dim)
    return out


def weight_gather(own, other, pos):
    own_a = ring_gather(own, "y", pos["y"], 0)
    other_a = ring_gather(other, "z", pos["z"], 0)
    return own_a, other_a


def weight_gather_end(own_a, other_a, pos):
    own_b = ring_gather(own_a, "z", pos["z"], 1)
    other_b = ring_gather(other_a, "y", pos["y"], 0)
    out = jnp.zeros((2,) + own_b.shape, own_b.dtype)
    out = lax.dynamic_update_index_in_dim(out, own_b, pos["xl"], 0)
    out = lax.dynamic_update_index_in_dim(out, other_b, 1 - pos["xl"], 0)
    return out.reshape(D, own_b.shape[-1])


def ring_scatter(v, axis, index, dim):
    total = at(v, index, dim).astype(F32)
    for k in (1, 3, 2):
        got = shift(at(v, (index + k) % 4, dim), **{"d" + axis: k})
        total = total + got.astype(F32)
    return total


def weight_scatter(grad, pos):
    parts = grad.reshape(2, 4, 4, 64, grad.shape[-1])
    own = at(parts, pos["xl"], 0)
    other = at(parts, 1 - pos["xl"], 0)
    own_a = ring_scatter(own, "z", pos["z"], 1).astype(BF16)
    other_a = ring_scatter(other, "y", pos["y"], 0).astype(BF16)
    own_b = ring_scatter(own_a, "y", pos["y"], 0)
    other_b = ring_scatter(other_a, "z", pos["z"], 0)
    return own_b, partner(other_b.astype(BF16)).astype(F32)


def token_gather(v, pos):
    mine = jnp.zeros((2, 2, 2) + v.shape, v.dtype)
    half = jnp.zeros((2, 2) + v.shape, v.dtype)
    zero = (0,) * v.ndim

    def put(buffer, block, dx):
        x = (pos["x"] + 4 - dx) % 4
        return lax.dynamic_update_slice(buffer, block[None, None], (x % 2, x // 2) + zero)

    half = put(half, v, 0)
    for k in (1, 3, 2):
        half = put(half, shift(v, dx=k), k)
    there = shift(half, dc=1)
    mine = lax.dynamic_update_index_in_dim(mine, half, pos["c"], 2)
    mine = lax.dynamic_update_index_in_dim(mine, there, 1 - pos["c"], 2)
    return mine.reshape(8 * v.shape[0], v.shape[1])


def token_scatter(v, pos, wire):
    parts = v.reshape(2, 2, 2, BLK, v.shape[1])
    got = shift(at(parts, 1 - pos["c"], 2).astype(wire), dc=1)
    half = (at(parts, pos["c"], 2).astype(F32) + got.astype(F32)).astype(wire)

    def pick(dx):
        x = (pos["x"] + dx) % 4
        return lax.dynamic_slice(half, (x % 2, x // 2, 0, 0), (1, 1, BLK, v.shape[1]))[0, 0]

    total = pick(0).astype(F32)
    for k in (1, 3, 2):
        total = total + shift(pick(k), dx=k).astype(F32)
    return total


def rms_scale(value, gain):
    return value * lax.rsqrt(jnp.mean(value * value, axis=-1, keepdims=True) + epsilon) * gain


def rotary(length_all, head_dim):
    half_dim = head_dim // 2
    freqs = theta ** (-(jnp.arange(half_dim, dtype=F32) * 2.0 / head_dim))
    angles = jnp.arange(length_all, dtype=F32)[:, None] * freqs[None, :]
    return (jnp.cos(angles), jnp.sin(angles))


def head_post(projected, gain, cos_table, sin_table, factor):
    normed = rms_scale(projected, gain)
    first = normed[..., : HD // 2]
    second = normed[..., HD // 2 :]
    cos_part = cos_table[None, :, None, :]
    sin_part = sin_table[None, :, None, :]
    turned = jnp.concatenate(
        [first * cos_part - second * sin_part, second * cos_part + first * sin_part], axis=-1
    )
    return turned * factor


def local(
    layer_input, cotangent, lengths, expert_ids, gains, w_qkv, w_out, w_router, w_gate_up, w_down
):
    pos = {a: lax.axis_index(a) for a in AXES}
    pos["x"] = pos["xh"] * 2 + pos["xl"]
    xl = pos["xl"]
    t = pos["xh"] * 2 + pos["c"]

    small = jnp.concatenate([gains.T, w_router], axis=1)
    small = jnp.pad(small, ((0, 0), (0, 128 - small.shape[1])))
    tiny = jnp.zeros((2, 2, 16, 128), BF16)
    tiny = lax.dynamic_update_slice(tiny, small[None, None], (pos["xh"], pos["c"], 0, 0))
    for dx, dc in ((0, 1), (2, 0), (2, 1)):
        got = shift(small, dx=dx, dc=dc)
        h = (pos["xh"] + dx // 2) % 2
        c = (pos["c"] + dc) % 2
        tiny = lax.dynamic_update_slice(tiny, got[None, None], (h, c, 0, 0))
    small = tiny.reshape(64, 128)
    out_rows = w_out.reshape(2, 256, 64).transpose(0, 2, 1)
    qkv_rows = w_qkv.reshape(3, 64, 2, 256).transpose(2, 1, 0, 3).reshape(2, 64, 768)
    att = jnp.concatenate([qkv_rows, out_rows], axis=2)
    att_own = jnp.concatenate([at(att, xl, 0), small], axis=1)
    att_give = jnp.concatenate([at(att, 1 - xl, 0), small], axis=1)
    att_other = partner(att_give)
    in_all = token_gather(layer_input, pos)
    att_a = weight_gather(att_own, att_other, pos)

    exp_rows = jnp.concatenate(
        [
            w_gate_up.reshape(2, HALF_E, 2, 64, FFS).transpose(0, 3, 1, 2, 4).reshape(2, 64, 2560),
            w_down.reshape(2, HALF_E, FFS, 64).transpose(0, 3, 1, 2).reshape(2, 64, 1280),
        ],
        axis=2,
    )
    exp_rows = tied(exp_rows, *att_a)
    att_full = weight_gather_end(*att_a, pos)
    exp_other = partner(at(exp_rows, 1 - xl, 0))
    exp_a = weight_gather(at(exp_rows, xl, 0), exp_other, pos)
    exp_a = lax.optimization_barrier((*exp_a, att_full))[:2]
    exp_full = weight_gather_end(*exp_a, pos)
    ids_other = partner(expert_ids)
    length_other = partner(jnp.broadcast_to(lengths, (8, 128)))[0, 0]
    cot_all = token_gather(tied(cotangent, in_all), pos)

    first = xl == 0
    length_both = jnp.stack(
        [jnp.where(first, lengths[0], length_other), jnp.where(first, length_other, lengths[0])]
    )
    ids_both = jnp.concatenate(
        [jnp.where(first, expert_ids, ids_other), jnp.where(first, ids_other, expert_ids)]
    )
    live = (jnp.arange(SEQ, dtype=jnp.int32)[None, :] < length_both[:, None]).astype(F32)

    w_qkv_all = att_full[:, :768]
    w_out_all = att_full[:, 768:1024]
    gain_f = att_full[:, 1024:1028].T.astype(F32)
    router = att_full[:, 1028:1038]
    head_start = t * 512 + xl * 256
    q_gain = lax.dynamic_slice_in_dim(gain_f[2], head_start, 256).reshape(2, HD)
    k_gain = lax.dynamic_slice_in_dim(gain_f[3], head_start, 256).reshape(2, HD)
    cos_table, sin_table = rotary(SEQ, HD)

    def post_query(projected, gain):
        return head_post(projected, gain, cos_table, sin_table, HD ** (-0.5))

    def post_key(projected, gain):
        return head_post(projected, gain, cos_table, sin_table, 1.0)

    in_float = in_all.astype(F32)
    in_scale = lax.rsqrt(jnp.mean(in_float * in_float, axis=-1, keepdims=True) + epsilon)
    normed_in = (in_float * in_scale * gain_f[0]).astype(BF16)
    project = jnp.dot(normed_in, w_qkv_all, preferred_element_type=F32)
    project = project.reshape(2, SEQ, 3, 2, HD)
    queries = post_query(project[:, :, 0], q_gain).astype(BF16)
    keys = post_key(project[:, :, 1], k_gain).astype(BF16)
    values = project[:, :, 2].astype(BF16)
    scores = jnp.einsum("sqhd,skhd->shqk", queries, keys, preferred_element_type=F32)
    highest = jnp.max(scores, axis=-1, keepdims=True)
    weights = jnp.exp(scores - highest) * live[:, None, None, :]
    probs = weights / jnp.sum(weights, axis=-1, keepdims=True)
    probs_low = probs.astype(BF16)
    attended = jnp.einsum("shqk,skhd->sqhd", probs_low, values, preferred_element_type=F32)
    attended = attended.astype(BF16).reshape(2 * SEQ, 256)
    branch = jnp.einsum("sf,df->sd", attended, w_out_all, preferred_element_type=F32)
    branch = token_scatter(branch, pos, BF16)
    input_float = layer_input.astype(F32)
    state = input_float + branch
    normed_mid = rms_scale(state, gain_f[1]).astype(BF16)
    mid_all = token_gather(normed_mid, pos)

    logits = jnp.dot(mid_all, router, preferred_element_type=F32)
    named = jnp.any(
        ids_both[:, :, None] == jnp.arange(E, dtype=jnp.int32)[None, None, :], axis=1
    )
    peak = jnp.max(jnp.where(named, logits, -jnp.inf), axis=-1, keepdims=True)
    soft = jnp.where(named, jnp.exp(jnp.where(named, logits - peak, 0.0)), 0.0)
    soft = soft / jnp.sum(soft, axis=-1, keepdims=True)
    live_rows = live.reshape(2 * SEQ, 1)
    gates = lax.dynamic_slice_in_dim(soft * live_rows, xl * HALF_E, HALF_E, axis=1)

    w_gu = exp_full[:, :2560]
    w_dn = exp_full[:, 2560:]
    hidden_grad = jnp.dot(cot_all, w_dn, preferred_element_type=F32).reshape(1024, HALF_E, FFS)
    pre = jnp.dot(mid_all, w_gu, preferred_element_type=F32).reshape(1024, HALF_E, 2, FFS)
    pre_gate = pre[:, :, 0]
    pre_up = pre[:, :, 1]
    sig = jax.nn.sigmoid(pre_gate)
    silu = pre_gate * sig
    inner = (silu * pre_up).astype(BF16).astype(F32)
    route_part = jnp.sum(inner * hidden_grad, axis=-1)
    gated_inner = (gates[:, :, None] * inner).astype(BF16).reshape(1024, HALF_E * FFS)
    inner_grad = gates[:, :, None] * hidden_grad
    gate_grad = inner_grad * pre_up * (sig + silu * (1.0 - sig))
    up_grad = inner_grad * silu
    pre_grad = jnp.stack([gate_grad, up_grad], axis=2).astype(BF16).reshape(1024, 2560)
    mid_part = jnp.einsum("sf,df->sd", pre_grad, w_gu, preferred_element_type=F32)

    route_wide = jnp.zeros((1024, E), F32)
    route_wide = lax.dynamic_update_slice(route_wide, route_part, (0, xl * HALF_E))
    route_grad = token_scatter(route_wide, pos, F32)
    own_start = xl * SEQ + t * BLK
    soft_own = lax.dynamic_slice_in_dim(soft, own_start, BLK)
    live_own = lax.dynamic_slice_in_dim(live_rows, own_start, BLK)
    soft_grad = route_grad * live_own
    logit_grad = soft_own * (soft_grad - jnp.sum(soft_own * soft_grad, axis=-1, keepdims=True))
    router_grad = jnp.dot(normed_mid.astype(F32).T, logit_grad, precision=precise)
    mid_from_router = jnp.dot(logit_grad, router.astype(F32).T, precision=precise)

    mid_grad = token_scatter(mid_part, pos, BF16) + mid_from_router
    mid_pull = jax.vjp(rms_scale, state, gain_f[1])[1]
    state_from_mid, mid_gain_grad = mid_pull(mid_grad)
    state_grad = cotangent.astype(F32) + state_from_mid
    branch_grad = token_gather(state_grad.astype(BF16), pos)

    mixed_part = jnp.einsum("sf,df->sd", gated_inner, w_dn, preferred_element_type=F32)
    mixed = token_scatter(mixed_part, pos, BF16)
    output = (state + mixed).astype(BF16)
    gu_grad = jnp.einsum("sd,sf->df", mid_all, pre_grad, preferred_element_type=F32).astype(BF16)
    dn_grad = jnp.einsum("sd,sf->df", cot_all, gated_inner, preferred_element_type=F32).astype(BF16)
    gu_sums = weight_scatter(gu_grad, pos)
    dn_sums = weight_scatter(dn_grad, pos)

    attended_grad = jnp.dot(branch_grad, w_out_all, preferred_element_type=F32).astype(BF16)
    out_grad = jnp.einsum("sd,sf->df", branch_grad, attended, preferred_element_type=F32)
    attended_grad = attended_grad.reshape(2, SEQ, 2, HD)
    prob_grad = jnp.einsum("sqhd,skhd->shqk", attended_grad, values, preferred_element_type=F32)
    inner_sum = jnp.sum(probs * prob_grad, axis=-1, keepdims=True)
    score_grad = (probs * (prob_grad - inner_sum)).astype(BF16)
    query_grad = jnp.einsum("shqk,skhd->sqhd", score_grad, keys, preferred_element_type=F32)
    key_grad = jnp.einsum("shqk,sqhd->skhd", score_grad, queries, preferred_element_type=F32)
    value_grad = jnp.einsum(
        "shqk,sqhd->skhd", probs_low, attended_grad, preferred_element_type=F32
    )
    query_proj, q_gain_grad = jax.vjp(post_query, project[:, :, 0], q_gain)[1](query_grad)
    key_proj, k_gain_grad = jax.vjp(post_key, project[:, :, 1], k_gain)[1](key_grad)
    proj_grad = jnp.stack([query_proj, key_proj, value_grad], axis=2).astype(BF16)
    proj_grad = proj_grad.reshape(1024, 768)
    in_part = jnp.einsum("sf,df->sd", proj_grad, w_qkv_all, preferred_element_type=F32)
    in_gain_grad = jnp.sum(in_part * (in_float * in_scale), axis=0)
    qkv_grad = jnp.einsum("sd,sf->df", normed_in, proj_grad, preferred_element_type=F32)
    in_grad = token_scatter(in_part, pos, BF16)
    in_pull = jax.vjp(lambda v: rms_scale(v, gain_f[0]), input_float)[1]
    input_grad = state_grad + in_pull(in_grad)[0]

    head_grads = lax.dynamic_update_slice(
        jnp.zeros((2, D), F32),
        jnp.stack([q_gain_grad.reshape(256), k_gain_grad.reshape(256)]),
        (0, head_start),
    )
    smalls = jnp.concatenate(
        [in_gain_grad[:, None], mid_gain_grad[:, None], head_grads.T, router_grad], axis=1
    )
    smalls = jnp.pad(smalls, ((0, 0), (0, 128 - smalls.shape[1])))
    att_grad = jnp.concatenate([qkv_grad, out_grad, smalls], axis=1).astype(BF16)
    att_own_sum, att_other_sum = weight_scatter(att_grad, pos)
    att_sums = jnp.zeros((2, 64, 1024), F32)
    att_sums = lax.dynamic_update_index_in_dim(att_sums, att_own_sum[:, :1024], xl, 0)
    att_sums = lax.dynamic_update_index_in_dim(att_sums, att_other_sum[:, :1024], 1 - xl, 0)
    qkv_out = att_sums[:, :, :768].reshape(2, 64, 3, 256).transpose(2, 1, 0, 3).reshape(3, 64, 512)
    out_out = att_sums[:, :, 768:].transpose(0, 2, 1).reshape(512, 64)
    small_sum = (att_own_sum + att_other_sum)[:, 1024:].reshape(2, 2, 16, 128)
    small_total = lax.dynamic_slice(small_sum, (pos["xh"], pos["c"], 0, 0), (1, 1, 16, 128))[0, 0]
    for dx, dc in ((0, 1), (2, 0), (2, 1)):
        h = (pos["xh"] + dx // 2) % 2
        c = (pos["c"] + dc) % 2
        give = lax.dynamic_slice(small_sum, (h, c, 0, 0), (1, 1, 16, 128))[0, 0]
        small_total = small_total + shift(give, dx=dx, dc=dc)
    gains_out = small_total[:, :4].T
    router_out = small_total[:, 4:14]

    def both(sums, width):
        joined = jnp.zeros((2, 64, width), F32)
        joined = lax.dynamic_update_index_in_dim(joined, sums[0], xl, 0)
        return lax.dynamic_update_index_in_dim(joined, sums[1], 1 - xl, 0)

    gate_up_out = both(gu_sums, 2560).reshape(2, 64, HALF_E, 2, FFS)
    gate_up_out = gate_up_out.transpose(0, 2, 3, 1, 4).reshape(E, 2, 64, FFS)
    down_out = both(dn_sums, 1280).reshape(2, 64, HALF_E, FFS)
    down_out = down_out.transpose(0, 2, 3, 1).reshape(E, FFS, 64)
    return (output, input_grad, gains_out, qkv_out, out_out, router_out, gate_up_out, down_out)


def solution(mesh):
    split = Mesh(mesh.devices.reshape(SIZES), AXES)
    placed = (
        P(DP_TENSOR, None),
        P(DP_TENSOR, None),
        P(DP),
        P(DP, None),
        P(None, DP_TENSOR),
        P(None, DP, ("xh", "c")),
        P(("xh", "c"), DP),
        P(DP_TENSOR, None),
        P(None, None, DP, ("xh", "c")),
        P(None, ("xh", "c"), DP),
    )
    return jax.shard_map(
        local,
        mesh=split,
        in_specs=placed,
        out_specs=(
            P(DP_TENSOR, None),
            P(DP_TENSOR, None),
            P(None, DP_TENSOR),
            P(None, DP, ("xh", "c")),
            P(("xh", "c"), DP),
            P(DP_TENSOR, None),
            P(None, None, DP, ("xh", "c")),
            P(None, ("xh", "c"), DP),
        ),
        check_vma=False,
    )
```

time: 4080 us -> 977 us (0.24)
  waiting for transfers between devices: 2560 us -> 228 us
  local copies, waits for them, and re-layouts: 648 us -> 329 us
  other arithmetic: 329 us -> 62.1 us
  blocking collectives: 212 us -> 0 us
  starting transfers between devices: 51.1 us -> 211 us
  matrix products: 258 us -> 128 us
    all_gather x11 -> x0, waiting for transfers between devices: 1430 us -> none  [rows_first(): whole = lax.all_gather(both, axis, axis=0, tiled=True)]
    reduce_scatter x8 -> x0, waiting for transfers between devices: 1040 us -> none  [the longest x2 746 us: one_scatter(): lax.psum_scatter(lines, axis, tiled=True).reshape(-1)]
    scatter-add x21 -> x0, other arithmetic: 270 us -> none  [the longest x10 119 us: expert_forward(): mixed = mixed.at[tokens].add(weight[:, None] * produced)]
    gather x42 -> x0, local copies, waits for them, and re-layouts: 228 us -> none  [the longest x10 70.5 us: expert_forward(): cot_all[tokens].astype(full_float)]
    ppermute x0 -> x109, waiting for transfers between devices: none -> 228 us  [the longest x102 221 us: shift(): return lax.ppermute(v, AXES, perm)]
    ppermute x0 -> x109, starting transfers between devices: none -> 211 us  [the longest x102 206 us: shift(): return lax.ppermute(v, AXES, perm)]
    all_gather x1 -> x0, blocking collectives: 183 us -> none  [rows_first(): whole = lax.all_gather(both, axis, axis=0, tiled=True)]
    dot_general x75 -> x20, matrix products: 258 us -> 123 us  [the longest x1 15.4 us: local(): jnp.einsum('sf,df->sd', pre_grad, w_gu, preferred_element_type=F32)]
  transfers between devices with their start and end apart: 27 -> 109, of which waited for: 21 -> 50; matrix products, arithmetic and copies ran while one was open for 9% -> 43% of each run, Pallas kernels for 0% -> 0%
where the time goes in v1:
time: 977 us; the launch traced here: 963 us
  local copies, waits for them, and re-layouts  329 us (34%)
  waiting for transfers between devices  228 us (23%)
  starting transfers between devices  211 us (22%)
  matrix products  128 us (13%)
  other arithmetic  62.1 us (6%)
    ppermute x102, waiting for transfers between devices, shift(): return lax.ppermute(v, AXES, perm)  221 us
    ppermute x102, starting transfers between devices, shift(): return lax.ppermute(v, AXES, perm)  206 us
    convert_element_type x3, local copies, waits for them, and re-layouts, local(): jnp.stack([gate_grad, up_grad], axis=2).astype(BF16).reshape(1024, 2560)  31.7 us
    dynamic_update_slice x24, local copies, waits for them, and re-layouts, ring_gather(): out = lax.dynamic_update_index_in_dim(out, got, (index + 4 - k) % 4, dim)  28.6 us
    dot_general x2, local copies, waits for them, and re-layouts, local(): jnp.dot(mid_all, w_gu, preferred_element_type=F32)  23.1 us
    unnamed x181, local copies, waits for them, and re-layouts  21.3 us
    mul x3, local copies, waits for them, and re-layouts, local(): gates[:, :, None] * inner  20.2 us
  transfers between devices with their start and end apart: 109, of which 50 were waited for; matrix products, arithmetic and copies ran while one was open for 43% of the time, Pallas kernels for 0%

profile of v1, /device:TPU:1, one launch (start us, length us, event | category | flops | bytes accessed | tf_op | source)
XLA Modules:
  0.0 963.3 jit_solution(16369228364611622324)
XLA Ops:
  22.4 5.7 collective-permute-done.5
  32.4 5.7 collective-permute-done.20
  114.0 22.2 %collective-permute-start.50 = (bf16[2,2,128,2048]{3,2,1,0:T(8,128)(2,1)}, bf16[2,2,128,2048]{3,2,1,0:T(8,128)(2,1)}, u32[]{:S(2)}, u32[]{:S(2)}) collective-permute-start(bf16[2,2,128,2048]{3,2,1,0:T(8,128)(2,1)} %bitcast_dynamic-update-slice_fusion.28), channel_id=1, source_target_pairs={{0,1},{1,0},{2,3},{3,2},{4,5},{5,4},{6,7},{7,6},{8,9},{9,8},{10,11... | collective-permute-start | bytes 6291464 | tf_op jit(solution)/shard_map/ppermute | solution.py:35
  178.0 5.2 collective-permute-start.40
  208.8 5.9 fusion.69
  216.3 6.4 copy.223
  232.4 24.0 %collective-permute-start.21 = (bf16[2,2,128,2048]{3,2,1,0:T(8,128)(2,1)S(1)}, bf16[2,2,128,2048]{3,2,1,0:T(8,128)(2,1)}, u32[]{:S(2)}, u32[]{:S(2)}) collective-permute-start(bf16[2,2,128,2048]{3,2,1,0:T(8,128)(2,1)S(1)} %fusion.31), channel_id=1, source_target_pairs={{0,1},{1,0},{2,3},{3,2},{4,5},{5,4},{6,7},{7,6},{8,9},{9,8},{10,11... | collective-permute-start | bytes 6291464 | tf_op jit(solution)/shard_map/ppermute | solution.py:35
  265.4 7.3 broadcast_in_dim.346
  272.8 7.2 constant_dynamic-update-slice_fusion.2
  292.7 7.2 constant_dynamic-update-slice_fusion.1
  304.8 10.6 %collective-permute-done.23 = bf16[128,2048]{1,0:T(8,128)(2,1)S(1)} collective-permute-done((bf16[128,2048]{1,0:T(8,128)(2,1)S(1)}, bf16[128,2048]{1,0:T(8,128)(2,1)S(1)}, u32[]{:S(2)}, u32[]{:S(2)}) %collective-permute-start.23) | collective-permute-done | bytes 524320 | tf_op jit(solution)/shard_map/ppermute | solution.py:35
  320.9 8.6 slice_bitcast_fusion
  333.7 9.7 %collective-permute-done.28 = bf16[128,2048]{1,0:T(8,128)(2,1)S(1)} collective-permute-done((bf16[128,2048]{1,0:T(8,128)(2,1)S(1)}, bf16[128,2048]{1,0:T(8,128)(2,1)S(1)}, u32[]{:S(2)}, u32[]{:S(2)}) %collective-permute-start.28) | collective-permute-done | bytes 524320 | tf_op jit(solution)/shard_map/ppermute | solution.py:35
  345.5 5.1 slice_bitcast_fusion.1
  350.6 8.1 copy.210
  358.7 14.5 %copy.201 = bf16[2560,2048]{1,0:T(8,128)(2,1)} copy(bf16[2560,2048]{0,1:T(8,128)(2,1)} %slice_bitcast_fusion) | data formatting | bytes 20971520 | tf_op jit(solution)/shard_map/dot_general | solution.py:257
  373.2 10.3 %fusion.167 = f32[1024,5,256]{0,2,1:T(8,128)} fusion(bf16[1024,2048,1]{1,0,2:T(8,128)(2,1)} %bitcast.682, bf16[5,256,2048]{2,1,0:T(8,128)(2,1)} %bitcast.670), kind=kOutput, calls=%fused_computation.419 | convolution fusion | flops 5368709120 | bytes 14680064 | tf_op jit(solution)/shard_map/dot_general | solution.py:256
  389.0 13.8 %fusion.166 = f32[1024,5,2,256]{0,3,2,1:T(8,128)S(1)} fusion(bf16[1024,2048,1,1]{1,0,3,2:T(8,128)(2,1)S(1)} %bitcast.647, bf16[5,2,256,2048]{3,2,1,0:T(8,128)(2,1)} %bitcast.662), kind=kOutput, calls=%fused_computation.418 | convolution fusion | flops 10737418240 | bytes 25165824 | tf_op jit(solution)/shard_map/dot_general | solution.py:257
  402.8 5.0 slice_bitcast_fusion.2
  411.3 5.2 fusion.15
  419.1 13.8 %copy.211 = bf16[1024,5,2,256]{3,2,1,0:T(2,128)(2,1)} copy(bf16[1024,5,2,256]{0,3,1,2:T(8,128)(2,1)} %maximum_convert_fusion) | data formatting | bytes 10485760 | tf_op jit(solution)/shard_map/convert_element_type | solution.py:268
  433.0 5.4 copy.230
  438.4 12.4 %convert_element_type.544 = bf16[2,2,2,128,2560]{4,3,2,1,0:T(8,128)(2,1)} reshape(bf16[1024,5,2,256]{3,2,1,0:T(2,128)(2,1)} %copy.211) | data formatting | bytes 10485760 | tf_op jit(solution)/shard_map/convert_element_type | solution.py:268
  450.8 15.4 %fusion.1 = f32[2,2,2,128,2048]{4,3,2,1,0:T(8,128)S(1)} fusion(bf16[2,2,2,128,2560]{4,3,2,1,0:T(8,128)(2,1)} %convert_element_type.544, bf16[2048,3840]{1,0:T(8,128)(2,1)} %bitcast.644), kind=kOutput, calls=%fused_computation.5 | convolution fusion | flops 10737418240 | bytes 24117248 | tf_op jit(solution)/shard_map/sf,df->sd/dot_general | solution.py:269
  474.4 8.2 mul.690
  482.7 8.9 copy.206
  491.5 8.1 squeeze.281
  499.6 8.8 copy.205
  508.4 8.1 squeeze.280
  516.5 8.8 copy.204
  525.4 14.7 %convolution_convert_fusion = bf16[2048,2560]{1,0:T(8,128)(2,1)S(1)} fusion(bf16[1024,2048]{1,0:T(8,128)(2,1)} %bitcast.648, bf16[1024,2560]{0,1:T(8,128)(2,1)} %bitcast.669), kind=kOutput, calls=%fused_computation.1 | convolution fusion | flops 10742661120 | bytes 19922944 | tf_op jit(solution)/shard_map/sd,sf->df/dot_general | solution.py:291
  540.1 9.4 convolution_convert_fusion.1
  556.0 20.2 %collective-permute-start.103 = (bf16[4,64,1280]{2,1,0:T(8,128)(2,1)}, bf16[4,64,1280]{2,1,0:T(8,128)(2,1)}, u32[]{:S(2)}, u32[]{:S(2)}) collective-permute-start(bf16[4,64,1280]{2,1,0:T(8,128)(2,1)} %get-tuple-element.90), channel_id=1, source_target_pairs={{0,48},{1,49},{2,50},{3,51},{4,52},{5,53},{6,54},{7,55},{8,56},{9,... | collective-permute-start | bytes 1966088 | tf_op jit(solution)/shard_map/ppermute | solution.py:35
  576.3 12.7 %fusion.12 = f32[2,2,2,128,2048]{4,3,2,1,0:T(8,128)} fusion(bf16[2048,3840]{1,0:T(8,128)(2,1)} %bitcast.645, f32[2,2,2,128,1280]{4,3,2,1,0:T(8,128)} %copy.206, f32[2,2,2,128,1280]{4,3,2,1,0:T(8,128)} %copy.205, f32[2,2,2,128,1280]{4,3,2,1,0:T(8,128)} %copy.204), kind=kOutput, calls=%fused_computation.23 | convolution fusion | flops 5380505600 | bytes 29360128 | tf_op jit(solution)/shard_map/sf,df->sd/dot_general | solution.py:288
  613.3 16.9 %collective-permute-done.97 = bf16[4,64,1280]{2,1,0:T(8,128)(2,1)S(1)} collective-permute-done((bf16[4,64,1280]{2,1,0:T(8,128)(2,1)S(1)}, bf16[4,64,1280]{2,1,0:T(8,128)(2,1)S(1)}, u32[]{:S(2)}, u32[]{:S(2)}) %collective-permute-start.97) | collective-permute-done | bytes 655392 | tf_op jit(solution)/shard_map/ppermute | solution.py:35
  646.6 7.0 collective-permute-done.54
  653.7 11.5 %collective-permute-done.53 = bf16[128,2048]{1,0:T(8,128)(2,1)S(1)} collective-permute-done((bf16[128,2048]{1,0:T(8,128)(2,1)S(1)}, bf16[128,2048]{1,0:T(8,128)(2,1)S(1)}, u32[]{:S(2)}, u32[]{:S(2)}) %collective-permute-start.53) | collective-permute-done | bytes 524320 | tf_op jit(solution)/shard_map/ppermute | solution.py:35
  679.2 7.5 collective-permute-done.45
  720.5 5.3 collective-permute-done.61
  733.2 7.3 collective-permute-done.90
  746.6 29.6 %collective-permute-done.84 = bf16[4,64,2560]{2,1,0:T(8,128)(2,1)S(1)} collective-permute-done((bf16[4,64,2560]{2,1,0:T(8,128)(2,1)}, bf16[4,64,2560]{2,1,0:T(8,128)(2,1)S(1)}, u32[]{:S(2)}, u32[]{:S(2)}) %collective-permute-start.84) | collective-permute-done | bytes 1310752 | tf_op jit(solution)/shard_map/ppermute | solution.py:35
  793.5 5.1 collective-permute-done.93
  818.0 6.4 copy.224
  829.7 5.0 copy.221
  839.6 5.1 reshape.598
  844.7 10.5 %multiply_reduce_fusion = (bf16[2048]{0:T(1024)(128)(2,1)S(1)}, f32[1024,2048]{1,0:T(8,128)}) fusion(f32[1024]{0:T(1024)S(1)} %bitcast.704, bf16[2,2,2,128,2048]{4,3,2,1,0:T(8,128)(2,1)} %bitcast_dynamic-update-slice_fusion.4, bf16[1024,768]{1,0:T(8,128)(2,1)} %convert_element_type.562, bf16[2048,1152]{1,0:T(8,128)(2,1)} %bitcast.655), kind=kOutput, calls=%fused_computation.12 | convolution fusion | flops 3229612032 | bytes 17309696 | tf_op jit(solution)/shard_map/sf,df->sd/dot_general | solution.py:311
  895.7 5.8 collective-permute-done.74
  945.4 10.8 %collective-permute-done.65 = bf16[128,2048]{1,0:T(8,128)(2,1)} collective-permute-done((bf16[128,2048]{1,0:T(8,128)(2,1)}, bf16[128,2048]{1,0:T(8,128)(2,1)}, u32[]{:S(2)}, u32[]{:S(2)}) %collective-permute-start.65) | collective-permute-done | bytes 524320 | tf_op jit(solution)/shard_map/ppermute | solution.py:35
  (607 shorter events, 481.6 us)
Async XLA Ops:
  0.6 81.7 %collective-permute-start.47 = (bf16[128,2048]{1,0:T(8,128)(2,1)}, bf16[128,2048]{1,0:T(8,128)(2,1)}, u32[]{:S(2)}, u32[]{:S(2)}) collective-permute-start(bf16[128,2048]{1,0:T(8,128)(2,1)} %param.11), channel_id=1, source_target_pairs={{0,64},{1,65},{2,66},{3,67},{4,68},{5,69},{6,70},{7,71},{8,72},{9,... | collective-permute-start | bytes 1572872 | tf_op jit(solution)/shard_map/ppermute | solution.py:35
  2.8 84.1 %collective-permute-start.48 = (bf16[128,2048]{1,0:T(8,128)(2,1)}, bf16[128,2048]{1,0:T(8,128)(2,1)}, u32[]{:S(2)}, u32[]{:S(2)}) collective-permute-start(bf16[128,2048]{1,0:T(8,128)(2,1)} %param.11), channel_id=1, source_target_pairs={{0,66},{1,67},{2,64},{3,65},{4,70},{5,71},{6,68},{7,69},{8,74},{9,... | collective-permute-start | bytes 1572872 | tf_op jit(solution)/shard_map/ppermute | solution.py:35
  4.1 88.3 %collective-permute-start.49 = (bf16[128,2048]{1,0:T(8,128)(2,1)}, bf16[128,2048]{1,0:T(8,128)(2,1)}, u32[]{:S(2)}, u32[]{:S(2)}) collective-permute-start(bf16[128,2048]{1,0:T(8,128)(2,1)} %param.11), channel_id=1, source_target_pairs={{0,2},{1,3},{2,0},{3,1},{4,6},{5,7},{6,4},{7,5},{8,10},{9,11},{10,... | collective-permute-start | bytes 1572872 | tf_op jit(solution)/shard_map/ppermute | solution.py:35
  28.2 57.6 %collective-permute-start = (bf16[128,2048]{1,0:T(8,128)(2,1)S(1)}, bf16[128,2048]{1,0:T(8,128)(2,1)}, u32[]{:S(2)}, u32[]{:S(2)}) collective-permute-start(bf16[128,2048]{1,0:T(8,128)(2,1)S(1)} %copy-done.13), channel_id=1, source_target_pairs={{0,64},{1,65},{2,66},{3,67},{4,68},{5,69},{6,70},{7,71},{8,72},{9,... | collective-permute-start | bytes 1572872 | tf_op jit(solution)/shard_map/ppermute | solution.py:35
  106.0 34.7 %collective-permute-start.17 = (bf16[4,64,1152]{2,1,0:T(8,128)(2,1)S(1)}, bf16[4,64,1152]{2,1,0:T(8,128)(2,1)S(1)}, u32[]{:S(2)}, u32[]{:S(2)}) collective-permute-start(bf16[4,64,1152]{2,1,0:T(8,128)(2,1)S(1)} %bitcast_dynamic-update-slice_fusion.47), channel_id=1, source_target_pairs={{0,16},{1,17},{2,18},{3,19},{4,20},{5,21},{6,22},{7,23},{8,24},{9,... | collective-permute-start | bytes 1769480 | tf_op jit(solution)/shard_map/ppermute | solution.py:35
  106.5 34.7 %collective-permute-start.18 = (bf16[4,64,1152]{2,1,0:T(8,128)(2,1)S(1)}, bf16[4,64,1152]{2,1,0:T(8,128)(2,1)S(1)}, u32[]{:S(2)}, u32[]{:S(2)}) collective-permute-start(bf16[4,64,1152]{2,1,0:T(8,128)(2,1)S(1)} %bitcast_dynamic-update-slice_fusion.47), channel_id=1, source_target_pairs={{0,48},{1,49},{2,50},{3,51},{4,52},{5,53},{6,54},{7,55},{8,56},{9,... | collective-permute-start | bytes 1769480 | tf_op jit(solution)/shard_map/ppermute | solution.py:35
  110.0 33.5 %collective-permute-start.19 = (bf16[4,64,1152]{2,1,0:T(8,128)(2,1)S(1)}, bf16[4,64,1152]{2,1,0:T(8,128)(2,1)S(1)}, u32[]{:S(2)}, u32[]{:S(2)}) collective-permute-start(bf16[4,64,1152]{2,1,0:T(8,128)(2,1)S(1)} %bitcast_dynamic-update-slice_fusion.47), channel_id=1, source_target_pairs={{0,32},{1,33},{2,34},{3,35},{4,36},{5,37},{6,38},{7,39},{8,40},{9,... | collective-permute-start | bytes 1769480 | tf_op jit(solution)/shard_map/ppermute | solution.py:35
  111.1 26.0 %collective-permute-start.33 = (bf16[64,3840]{1,0:T(8,128)(2,1)S(1)}, bf16[64,3840]{1,0:T(8,128)(2,1)}, u32[]{:S(2)}, u32[]{:S(2)}) collective-permute-start(bf16[64,3840]{1,0:T(8,128)(2,1)S(1)} %get-tuple-element.137), channel_id=1, source_target_pairs={{0,64},{1,65},{2,66},{3,67},{4,68},{5,69},{6,70},{7,71},{8,72},{9,... | collective-permute-start | bytes 1474568 | tf_op jit(solution)/shard_map/ppermute | solution.py:43
  114.0 111.3 %collective-permute-start.50 = (bf16[2,2,128,2048]{3,2,1,0:T(8,128)(2,1)}, bf16[2,2,128,2048]{3,2,1,0:T(8,128)(2,1)}, u32[]{:S(2)}, u32[]{:S(2)}) collective-permute-start(bf16[2,2,128,2048]{3,2,1,0:T(8,128)(2,1)} %bitcast_dynamic-update-slice_fusion.28), channel_id=1, source_target_pairs={{0,1},{1,0},{2,3},{3,2},{4,5},{5,4},{6,7},{7,6},{8,9},{9,8},{10,11... | collective-permute-start | bytes 6291464 | tf_op jit(solution)/shard_map/ppermute | solution.py:35
  137.0 40.9 %collective-permute-start.3 = (bf16[2,2,128,2048]{3,2,1,0:T(8,128)(2,1)S(1)}, bf16[2,2,128,2048]{3,2,1,0:T(8,128)(2,1)}, u32[]{:S(2)}, u32[]{:S(2)}) collective-permute-start(bf16[2,2,128,2048]{3,2,1,0:T(8,128)(2,1)S(1)} %bitcast_dynamic-update-slice_fusion.36), channel_id=1, source_target_pairs={{0,1},{1,0},{2,3},{3,2},{4,5},{5,4},{6,7},{7,6},{8,9},{9,8},{10,11... | collective-permute-start | bytes 6291464 | tf_op jit(solution)/shard_map/ppermute | solution.py:35
  164.4 63.6 %collective-permute-start.37 = (bf16[4,64,3840]{2,1,0:T(8,128)(2,1)}, bf16[4,64,3840]{2,1,0:T(8,128)(2,1)}, u32[]{:S(2)}, u32[]{:S(2)}) collective-permute-start(bf16[4,64,3840]{2,1,0:T(8,128)(2,1)} %bitcast_dynamic-update-slice_fusion.44), channel_id=1, source_target_pairs={{0,4},{1,5},{2,6},{3,7},{4,8},{5,9},{6,10},{7,11},{8,12},{9,13},{1... | collective-permute-start | bytes 5898248 | tf_op jit(solution)/shard_map/ppermute | solution.py:35
  165.0 67.3 %collective-permute-start.38 = (bf16[4,64,3840]{2,1,0:T(8,128)(2,1)}, bf16[4,64,3840]{2,1,0:T(8,128)(2,1)}, u32[]{:S(2)}, u32[]{:S(2)}) collective-permute-start(bf16[4,64,3840]{2,1,0:T(8,128)(2,1)} %bitcast_dynamic-update-slice_fusion.44), channel_id=1, source_target_pairs={{0,12},{1,13},{2,14},{3,15},{4,0},{5,1},{6,2},{7,3},{8,4},{9,5},{1... | collective-permute-start | bytes 5898248 | tf_op jit(solution)/shard_map/ppermute | solution.py:35
  167.0 92.4 %collective-permute-start.39 = (bf16[4,64,3840]{2,1,0:T(8,128)(2,1)}, bf16[4,64,3840]{2,1,0:T(8,128)(2,1)}, u32[]{:S(2)}, u32[]{:S(2)}) collective-permute-start(bf16[4,64,3840]{2,1,0:T(8,128)(2,1)} %bitcast_dynamic-update-slice_fusion.44), channel_id=1, source_target_pairs={{0,8},{1,9},{2,10},{3,11},{4,12},{5,13},{6,14},{7,15},{8,0},{9,1},... | collective-permute-start | bytes 5898248 | tf_op jit(solution)/shard_map/ppermute | solution.py:35
  178.0 84.5 %collective-permute-start.40 = (bf16[4,64,3840]{2,1,0:T(8,128)(2,1)}, bf16[4,64,3840]{2,1,0:T(8,128)(2,1)}, u32[]{:S(2)}, u32[]{:S(2)}) collective-permute-start(bf16[4,64,3840]{2,1,0:T(8,128)(2,1)} %bitcast_dynamic-update-slice_fusion.40), channel_id=1, source_target_pairs={{0,16},{1,17},{2,18},{3,19},{4,20},{5,21},{6,22},{7,23},{8,24},{9,... | collective-permute-start | bytes 5898248 | tf_op jit(solution)/shard_map/ppermute | solution.py:35
  225.4 54.6 %collective-permute-start.41 = (bf16[4,64,3840]{2,1,0:T(8,128)(2,1)}, bf16[4,64,3840]{2,1,0:T(8,128)(2,1)}, u32[]{:S(2)}, u32[]{:S(2)}) collective-permute-start(bf16[4,64,3840]{2,1,0:T(8,128)(2,1)} %bitcast_dynamic-update-slice_fusion.40), channel_id=1, source_target_pairs={{0,48},{1,49},{2,50},{3,51},{4,52},{5,53},{6,54},{7,55},{8,56},{9,... | collective-permute-start | bytes 5898248 | tf_op jit(solution)/shard_map/ppermute | solution.py:35
  228.0 55.0 %collective-permute-start.42 = (bf16[4,64,3840]{2,1,0:T(8,128)(2,1)}, bf16[4,64,3840]{2,1,0:T(8,128)(2,1)}, u32[]{:S(2)}, u32[]{:S(2)}) collective-permute-start(bf16[4,64,3840]{2,1,0:T(8,128)(2,1)} %bitcast_dynamic-update-slice_fusion.40), channel_id=1, source_target_pairs={{0,32},{1,33},{2,34},{3,35},{4,36},{5,37},{6,38},{7,39},{8,40},{9,... | collective-permute-start | bytes 5898248 | tf_op jit(solution)/shard_map/ppermute | solution.py:35
  232.4 53.6 %collective-permute-start.21 = (bf16[2,2,128,2048]{3,2,1,0:T(8,128)(2,1)S(1)}, bf16[2,2,128,2048]{3,2,1,0:T(8,128)(2,1)}, u32[]{:S(2)}, u32[]{:S(2)}) collective-permute-start(bf16[2,2,128,2048]{3,2,1,0:T(8,128)(2,1)S(1)} %fusion.31), channel_id=1, source_target_pairs={{0,1},{1,0},{2,3},{3,2},{4,5},{5,4},{6,7},{7,6},{8,9},{9,8},{10,11... | collective-permute-start | bytes 6291464 | tf_op jit(solution)/shard_map/ppermute | solution.py:35
  290.6 24.8 %collective-permute-start.23 = (bf16[128,2048]{1,0:T(8,128)(2,1)S(1)}, bf16[128,2048]{1,0:T(8,128)(2,1)S(1)}, u32[]{:S(2)}, u32[]{:S(2)}) collective-permute-start(bf16[128,2048]{1,0:T(8,128)(2,1)S(1)} %get-tuple-element.117), channel_id=1, source_target_pairs={{0,66},{1,67},{2,64},{3,65},{4,70},{5,71},{6,68},{7,69},{8,74},{9,... | collective-permute-start | bytes 1572872 | tf_op jit(solution)/shard_map/ppermute | solution.py:35
  343.4 40.9 %collective-permute-start.29 = (bf16[2,2,128,2048]{3,2,1,0:T(8,128)(2,1)S(1)}, bf16[2,2,128,2048]{3,2,1,0:T(8,128)(2,1)}, u32[]{:S(2)}, u32[]{:S(2)}) collective-permute-start(bf16[2,2,128,2048]{3,2,1,0:T(8,128)(2,1)S(1)} %bitcast_dynamic-update-slice_fusion.32), channel_id=1, source_target_pairs={{0,1},{1,0},{2,3},{3,2},{4,5},{5,4},{6,7},{7,6},{8,9},{9,8},{10,11... | collective-permute-start | bytes 6291464 | tf_op jit(solution)/shard_map/ppermute | solution.py:35
  468.0 169.1 %collective-permute-start.51 = (bf16[2,2,128,2048]{3,2,1,0:T(8,128)(2,1)}, bf16[2,2,128,2048]{3,2,1,0:T(8,128)(2,1)}, u32[]{:S(2)}, u32[]{:S(2)}) collective-permute-start(bf16[2,2,128,2048]{3,2,1,0:T(8,128)(2,1)} %fusion.32), channel_id=1, source_target_pairs={{0,1},{1,0},{2,3},{3,2},{4,5},{5,4},{6,7},{7,6},{8,9},{9,8},{10,11... | collective-permute-start | bytes 6291464 | tf_op jit(solution)/shard_map/ppermute | solution.py:35
  471.3 117.7 %collective-permute-start.55 = (f32[2,2,128,10]{2,3,1,0:T(8,128)S(1)}, f32[2,2,128,10]{2,3,1,0:T(8,128)S(1)}, u32[]{:S(2)}, u32[]{:S(2)}) collective-permute-start(f32[2,2,128,10]{2,3,1,0:T(8,128)S(1)} %bitcast.703), channel_id=1, source_target_pairs={{0,1},{1,0},{2,3},{3,2},{4,5},{5,4},{6,7},{7,6},{8,9},{9,8},{10,11... | collective-permute-start | bytes 61448 | tf_op jit(solution)/shard_map/ppermute | solution.py:35
  552.8 47.3 %collective-permute-start.104 = (bf16[4,64,1280]{2,1,0:T(8,128)(2,1)}, bf16[4,64,1280]{2,1,0:T(8,128)(2,1)}, u32[]{:S(2)}, u32[]{:S(2)}) collective-permute-start(bf16[4,64,1280]{2,1,0:T(8,128)(2,1)} %get-tuple-element.89), channel_id=1, source_target_pairs={{0,32},{1,33},{2,34},{3,35},{4,36},{5,37},{6,38},{7,39},{8,40},{9,... | collective-permute-start | bytes 1966088 | tf_op jit(solution)/shard_map/ppermute | solution.py:35
  556.0 48.9 %collective-permute-start.103 = (bf16[4,64,1280]{2,1,0:T(8,128)(2,1)}, bf16[4,64,1280]{2,1,0:T(8,128)(2,1)}, u32[]{:S(2)}, u32[]{:S(2)}) collective-permute-start(bf16[4,64,1280]{2,1,0:T(8,128)(2,1)} %get-tuple-element.90), channel_id=1, source_target_pairs={{0,48},{1,49},{2,50},{3,51},{4,52},{5,53},{6,54},{7,55},{8,56},{9,... | collective-permute-start | bytes 1966088 | tf_op jit(solution)/shard_map/ppermute | solution.py:35
  600.2 30.1 %collective-permute-start.97 = (bf16[4,64,1280]{2,1,0:T(8,128)(2,1)S(1)}, bf16[4,64,1280]{2,1,0:T(8,128)(2,1)S(1)}, u32[]{:S(2)}, u32[]{:S(2)}) collective-permute-start(bf16[4,64,1280]{2,1,0:T(8,128)(2,1)S(1)} %get-tuple-element.93), channel_id=1, source_target_pairs={{0,12},{1,13},{2,14},{3,15},{4,0},{5,1},{6,2},{7,3},{8,4},{9,5},{1... | collective-permute-start | bytes 1966088 | tf_op jit(solution)/shard_map/ppermute | solution.py:35
  604.9 25.6 %collective-permute-start.96 = (bf16[4,64,1280]{2,1,0:T(8,128)(2,1)S(1)}, bf16[4,64,1280]{2,1,0:T(8,128)(2,1)S(1)}, u32[]{:S(2)}, u32[]{:S(2)}) collective-permute-start(bf16[4,64,1280]{2,1,0:T(8,128)(2,1)S(1)} %get-tuple-element.91), channel_id=1, source_target_pairs={{0,4},{1,5},{2,6},{3,7},{4,8},{5,9},{6,10},{7,11},{8,12},{9,13},{1... | collective-permute-start | bytes 1966088 | tf_op jit(solution)/shard_map/ppermute | solution.py:35
  610.3 30.1 %collective-permute-start.43 = (bf16[2,2,128,2048]{3,2,1,0:T(8,128)(2,1)S(1)}, bf16[2,2,128,2048]{3,2,1,0:T(8,128)(2,1)S(1)}, u32[]{:S(2)}, u32[]{:S(2)}) collective-permute-start(bf16[2,2,128,2048]{3,2,1,0:T(8,128)(2,1)S(1)} %fusion.33), channel_id=1, source_target_pairs={{0,1},{1,0},{2,3},{3,2},{4,5},{5,4},{6,7},{7,6},{8,9},{9,8},{10,11... | collective-permute-start | bytes 6291464 | tf_op jit(solution)/shard_map/ppermute | solution.py:35
  640.4 24.8 %collective-permute-start.53 = (bf16[128,2048]{1,0:T(8,128)(2,1)S(1)}, bf16[128,2048]{1,0:T(8,128)(2,1)S(1)}, u32[]{:S(2)}, u32[]{:S(2)}) collective-permute-start(bf16[128,2048]{1,0:T(8,128)(2,1)S(1)} %get-tuple-element.111), channel_id=1, source_target_pairs={{0,66},{1,67},{2,64},{3,65},{4,70},{5,71},{6,68},{7,69},{8,74},{9,... | collective-permute-start | bytes 1572872 | tf_op jit(solution)/shard_map/ppermute | solution.py:35
  642.6 25.6 %collective-permute-start.52 = (bf16[128,2048]{1,0:T(8,128)(2,1)S(1)}, bf16[128,2048]{1,0:T(8,128)(2,1)S(1)}, u32[]{:S(2)}, u32[]{:S(2)}) collective-permute-start(bf16[128,2048]{1,0:T(8,128)(2,1)S(1)} %get-tuple-element.109), channel_id=1, source_target_pairs={{0,64},{1,65},{2,66},{3,67},{4,68},{5,69},{6,70},{7,71},{8,72},{9,... | collective-permute-start | bytes 1572872 | tf_op jit(solution)/shard_map/ppermute | solution.py:35
  643.6 32.5 %collective-permute-start.46 = (bf16[128,2048]{1,0:T(8,128)(2,1)S(1)}, bf16[128,2048]{1,0:T(8,128)(2,1)S(1)}, u32[]{:S(2)}, u32[]{:S(2)}) collective-permute-start(bf16[128,2048]{1,0:T(8,128)(2,1)S(1)} %get-tuple-element.113), channel_id=1, source_target_pairs={{0,2},{1,3},{2,0},{3,1},{4,6},{5,7},{6,4},{7,5},{8,10},{9,11},{10,... | collective-permute-start | bytes 1572872 | tf_op jit(solution)/shard_map/ppermute | solution.py:35
  645.5 41.1 %collective-permute-start.45 = (bf16[128,2048]{1,0:T(8,128)(2,1)S(1)}, bf16[128,2048]{1,0:T(8,128)(2,1)S(1)}, u32[]{:S(2)}, u32[]{:S(2)}) collective-permute-start(bf16[128,2048]{1,0:T(8,128)(2,1)S(1)} %get-tuple-element.114), channel_id=1, source_target_pairs={{0,66},{1,67},{2,64},{3,65},{4,70},{5,71},{6,68},{7,69},{8,74},{9,... | collective-permute-start | bytes 1572872 | tf_op jit(solution)/shard_map/ppermute | solution.py:35
  653.6 35.5 %collective-permute-start.44 = (bf16[128,2048]{1,0:T(8,128)(2,1)S(1)}, bf16[128,2048]{1,0:T(8,128)(2,1)S(1)}, u32[]{:S(2)}, u32[]{:S(2)}) collective-permute-start(bf16[128,2048]{1,0:T(8,128)(2,1)S(1)} %get-tuple-element.112), channel_id=1, source_target_pairs={{0,64},{1,65},{2,66},{3,67},{4,68},{5,69},{6,70},{7,71},{8,72},{9,... | collective-permute-start | bytes 1572872 | tf_op jit(solution)/shard_map/ppermute | solution.py:35
  665.2 51.1 %collective-permute-start.91 = (bf16[4,64,2560]{2,1,0:T(8,128)(2,1)}, bf16[4,64,2560]{2,1,0:T(8,128)(2,1)}, u32[]{:S(2)}, u32[]{:S(2)}) collective-permute-start(bf16[4,64,2560]{2,1,0:T(8,128)(2,1)} %get-tuple-element.79), channel_id=1, source_target_pairs={{0,32},{1,33},{2,34},{3,35},{4,36},{5,37},{6,38},{7,39},{8,40},{9,... | collective-permute-start | bytes 3932168 | tf_op jit(solution)/shard_map/ppermute | solution.py:35
  668.2 30.4 %collective-permute-start.101 = (bf16[64,1280]{1,0:T(8,128)(2,1)S(1)}, bf16[64,1280]{1,0:T(8,128)(2,1)S(1)}, u32[]{:S(2)}, u32[]{:S(2)}) collective-permute-start(bf16[64,1280]{1,0:T(8,128)(2,1)S(1)} %get-tuple-element.144), channel_id=1, source_target_pairs={{0,32},{1,33},{2,34},{3,35},{4,36},{5,37},{6,38},{7,39},{8,40},{9,... | collective-permute-start | bytes 491528 | tf_op jit(solution)/shard_map/ppermute | solution.py:35
  676.2 26.8 %collective-permute-start.100 = (bf16[64,1280]{1,0:T(8,128)(2,1)S(1)}, bf16[64,1280]{1,0:T(8,128)(2,1)S(1)}, u32[]{:S(2)}, u32[]{:S(2)}) collective-permute-start(bf16[64,1280]{1,0:T(8,128)(2,1)S(1)} %get-tuple-element.145), channel_id=1, source_target_pairs={{0,48},{1,49},{2,50},{3,51},{4,52},{5,53},{6,54},{7,55},{8,56},{9,... | collective-permute-start | bytes 491528 | tf_op jit(solution)/shard_map/ppermute | solution.py:35
  709.8 30.7 %collective-permute-start.90 = (bf16[4,64,2560]{2,1,0:T(8,128)(2,1)}, bf16[4,64,2560]{2,1,0:T(8,128)(2,1)}, u32[]{:S(2)}, u32[]{:S(2)}) collective-permute-start(bf16[4,64,2560]{2,1,0:T(8,128)(2,1)} %get-tuple-element.80), channel_id=1, source_target_pairs={{0,48},{1,49},{2,50},{3,51},{4,52},{5,53},{6,54},{7,55},{8,56},{9,... | collective-permute-start | bytes 3932168 | tf_op jit(solution)/shard_map/ppermute | solution.py:35
  716.3 30.4 %collective-permute-start.89 = (bf16[4,64,2560]{2,1,0:T(8,128)(2,1)}, bf16[4,64,2560]{2,1,0:T(8,128)(2,1)S(1)}, u32[]{:S(2)}, u32[]{:S(2)}) collective-permute-start(bf16[4,64,2560]{2,1,0:T(8,128)(2,1)} %get-tuple-element.78), channel_id=1, source_target_pairs={{0,16},{1,17},{2,18},{3,19},{4,20},{5,21},{6,22},{7,23},{8,24},{9,... | collective-permute-start | bytes 3932168 | tf_op jit(solution)/shard_map/ppermute | solution.py:35
  716.3 30.4 %collective-permute-start.85 = (bf16[4,64,2560]{2,1,0:T(8,128)(2,1)}, bf16[4,64,2560]{2,1,0:T(8,128)(2,1)S(1)}, u32[]{:S(2)}, u32[]{:S(2)}) collective-permute-start(bf16[4,64,2560]{2,1,0:T(8,128)(2,1)} %get-tuple-element.82), channel_id=1, source_target_pairs={{0,8},{1,9},{2,10},{3,11},{4,12},{5,13},{6,14},{7,15},{8,0},{9,1},... | collective-permute-start | bytes 3932168 | tf_op jit(solution)/shard_map/ppermute | solution.py:35
  718.4 57.8 %collective-permute-start.84 = (bf16[4,64,2560]{2,1,0:T(8,128)(2,1)}, bf16[4,64,2560]{2,1,0:T(8,128)(2,1)S(1)}, u32[]{:S(2)}, u32[]{:S(2)}) collective-permute-start(bf16[4,64,2560]{2,1,0:T(8,128)(2,1)} %get-tuple-element.83), channel_id=1, source_target_pairs={{0,12},{1,13},{2,14},{3,15},{4,0},{5,1},{6,2},{7,3},{8,4},{9,5},{1... | collective-permute-start | bytes 3932168 | tf_op jit(solution)/shard_map/ppermute | solution.py:35
  725.7 51.1 %collective-permute-start.83 = (bf16[4,64,2560]{2,1,0:T(8,128)(2,1)}, bf16[4,64,2560]{2,1,0:T(8,128)(2,1)S(1)}, u32[]{:S(2)}, u32[]{:S(2)}) collective-permute-start(bf16[4,64,2560]{2,1,0:T(8,128)(2,1)} %get-tuple-element.81), channel_id=1, source_target_pairs={{0,4},{1,5},{2,6},{3,7},{4,8},{5,9},{6,10},{7,11},{8,12},{9,13},{1... | collective-permute-start | bytes 3932168 | tf_op jit(solution)/shard_map/ppermute | solution.py:35
  740.5 61.9 %collective-permute-start.62 = (bf16[2,2,128,2048]{3,2,1,0:T(8,128)(2,1)}, bf16[2,2,128,2048]{3,2,1,0:T(8,128)(2,1)S(1)}, u32[]{:S(2)}, u32[]{:S(2)}) collective-permute-start(bf16[2,2,128,2048]{3,2,1,0:T(8,128)(2,1)} %bitcast_dynamic-update-slice_fusion.24), channel_id=1, source_target_pairs={{0,1},{1,0},{2,3},{3,2},{4,5},{5,4},{6,7},{7,6},{8,9},{9,8},{10,11... | collective-permute-start | bytes 6291464 | tf_op jit(solution)/shard_map/ppermute | solution.py:35
  786.0 81.5 %collective-permute-start.88 = (bf16[64,2560]{1,0:T(8,128)(2,1)}, bf16[64,2560]{1,0:T(8,128)(2,1)}, u32[]{:S(2)}, u32[]{:S(2)}) collective-permute-start(bf16[64,2560]{1,0:T(8,128)(2,1)} %get-tuple-element.122), channel_id=1, source_target_pairs={{0,32},{1,33},{2,34},{3,35},{4,36},{5,37},{6,38},{7,39},{8,40},{9,... | collective-permute-start | bytes 983048 | tf_op jit(solution)/shard_map/ppermute | solution.py:35
  790.9 76.6 %collective-permute-start.87 = (bf16[64,2560]{1,0:T(8,128)(2,1)}, bf16[64,2560]{1,0:T(8,128)(2,1)}, u32[]{:S(2)}, u32[]{:S(2)}) collective-permute-start(bf16[64,2560]{1,0:T(8,128)(2,1)} %get-tuple-element.123), channel_id=1, source_target_pairs={{0,48},{1,49},{2,50},{3,51},{4,52},{5,53},{6,54},{7,55},{8,56},{9,... | collective-permute-start | bytes 983048 | tf_op jit(solution)/shard_map/ppermute | solution.py:35
  798.6 69.0 %collective-permute-start.86 = (bf16[64,2560]{1,0:T(8,128)(2,1)}, bf16[64,2560]{1,0:T(8,128)(2,1)}, u32[]{:S(2)}, u32[]{:S(2)}) collective-permute-start(bf16[64,2560]{1,0:T(8,128)(2,1)} %get-tuple-element.121), channel_id=1, source_target_pairs={{0,16},{1,17},{2,18},{3,19},{4,20},{5,21},{6,22},{7,23},{8,24},{9,... | collective-permute-start | bytes 983048 | tf_op jit(solution)/shard_map/ppermute | solution.py:35
  800.0 76.3 %collective-permute-start.95 = (bf16[64,2560]{1,0:T(8,128)(2,1)}, bf16[64,2560]{1,0:T(8,128)(2,1)}, u32[]{:S(2)}, u32[]{:S(2)}) collective-permute-start(bf16[64,2560]{1,0:T(8,128)(2,1)} %fusion.77), channel_id=1, source_target_pairs={{0,64},{1,65},{2,66},{3,67},{4,68},{5,69},{6,70},{7,71},{8,72},{9,... | collective-permute-start | bytes 983048 | tf_op jit(solution)/shard_map/ppermute | solution.py:43
  869.1 25.0 %collective-permute-start.68 = (bf16[4,64,1152]{2,1,0:T(8,128)(2,1)}, bf16[4,64,1152]{2,1,0:T(8,128)(2,1)}, u32[]{:S(2)}, u32[]{:S(2)}) collective-permute-start(bf16[4,64,1152]{2,1,0:T(8,128)(2,1)} %get-tuple-element.98), channel_id=1, source_target_pairs={{0,12},{1,13},{2,14},{3,15},{4,0},{5,1},{6,2},{7,3},{8,4},{9,5},{1... | collective-permute-start | bytes 1769480 | tf_op jit(solution)/shard_map/ppermute | solution.py:35
  871.2 24.4 %collective-permute-start.67 = (bf16[4,64,1152]{2,1,0:T(8,128)(2,1)}, bf16[4,64,1152]{2,1,0:T(8,128)(2,1)}, u32[]{:S(2)}, u32[]{:S(2)}) collective-permute-start(bf16[4,64,1152]{2,1,0:T(8,128)(2,1)} %get-tuple-element.96), channel_id=1, source_target_pairs={{0,4},{1,5},{2,6},{3,7},{4,8},{5,9},{6,10},{7,11},{8,12},{9,13},{1... | collective-permute-start | bytes 1769480 | tf_op jit(solution)/shard_map/ppermute | solution.py:35
  876.3 25.2 %collective-permute-start.74 = (bf16[4,64,1152]{2,1,0:T(8,128)(2,1)}, bf16[4,64,1152]{2,1,0:T(8,128)(2,1)}, u32[]{:S(2)}, u32[]{:S(2)}) collective-permute-start(bf16[4,64,1152]{2,1,0:T(8,128)(2,1)} %get-tuple-element.101), channel_id=1, source_target_pairs={{0,48},{1,49},{2,50},{3,51},{4,52},{5,53},{6,54},{7,55},{8,56},{9,... | collective-permute-start | bytes 1769480 | tf_op jit(solution)/shard_map/ppermute | solution.py:35
  894.1 33.1 %collective-permute-start.63 = (bf16[2,2,128,2048]{3,2,1,0:T(8,128)(2,1)S(1)}, bf16[2,2,128,2048]{3,2,1,0:T(8,128)(2,1)S(1)}, u32[]{:S(2)}, u32[]{:S(2)}) collective-permute-start(bf16[2,2,128,2048]{3,2,1,0:T(8,128)(2,1)S(1)} %fusion.34), channel_id=1, source_target_pairs={{0,1},{1,0},{2,3},{3,2},{4,5},{5,4},{6,7},{7,6},{8,9},{9,8},{10,11... | collective-permute-start | bytes 6291464 | tf_op jit(solution)/shard_map/ppermute | solution.py:35
  (148 other events, 2324.1 us)

commit v2 on v1

v2 whole, which is shorter than its diff:
```python
import functools

import jax
import jax.numpy as jnp
import numpy as np
from jax import lax
from jax.experimental import pallas as pl
from jax.experimental.pallas import tpu as pltpu
from jax.sharding import Mesh
from jax.sharding import PartitionSpec as P

HD = 128
TOPK = 8
E = 10
D = 2048
SEQ = 512
ROWS = 1024
BLK = 128
HALF_E = 5
FFS = 256
GU = HALF_E * 2 * FFS
EW = HALF_E * 3 * FFS
AW = 1152
ROUTER_AT = 4
AXES = ("xl", "y", "z", "xh", "c")
SIZES = (2, 4, 4, 2, 2)
DP = ("xl", "y", "z")
EPS = 1e-06
THETA = 10000.0
F32 = jnp.float32
BF16 = jnp.bfloat16
MIB = 1 << 20
LOGICAL = pl.DeviceIdType.MESH
VMEM = pl.BlockSpec(memory_space=pltpu.VMEM)
ANY = pl.BlockSpec(memory_space=pl.ANY)


class Place:
    def __init__(self):
        self.xl, self.y, self.z, self.xh, self.c = (lax.axis_index(a) for a in AXES)
        self.x = self.xh * 2 + self.xl
        self.t = self.xh * 2 + self.c

    def at(self, dx=0, dy=0, dz=0, dc=0):
        x = lax.rem(self.x + (dx + 4), 4)
        return (
            lax.rem(x, 2),
            lax.rem(self.y + (dy + 4), 4),
            lax.rem(self.z + (dz + 4), 4),
            lax.div(x, 2),
            lax.rem(self.c + (dc + 2), 2),
        )

    def chip(self, dx):
        x = lax.rem(self.x + (dx + 4), 4)
        return lax.rem(x, 2), lax.div(x, 2)

    def partner(self):
        return (1 - self.xl, self.y, self.z, self.xh, self.c)


class Wires:
    def __init__(self, send, recv, near):
        self.send, self.recv, self.near = send, recv, near
        self.count, self.near_count = 0, 0

    def to(self, device, src, dst):
        k, self.count = self.count, self.count + 1
        copy = pltpu.make_async_remote_copy(
            src_ref=src,
            dst_ref=dst,
            send_sem=self.send.at[k],
            recv_sem=self.recv.at[k],
            device_id=device,
            device_id_type=LOGICAL,
        )
        copy.start()
        return copy

    def here(self, src, dst):
        k, self.near_count = self.near_count, self.near_count + 1
        copy = pltpu.make_async_copy(src, dst, self.near.at[k])
        copy.start()
        return copy


def wire_scratch(copies, local):
    return [
        pltpu.SemaphoreType.DMA((copies,)),
        pltpu.SemaphoreType.DMA((copies,)),
        pltpu.SemaphoreType.DMA((local,)),
    ]


def greet(devices):
    barrier = pltpu.get_barrier_semaphore()
    for device in devices:
        pl.semaphore_signal(barrier, inc=1, device_id=device, device_id_type=LOGICAL)
    pl.semaphore_wait(barrier, len(devices))


def params(collective_id=None, vmem=56):
    if collective_id is None:
        return pltpu.CompilerParams(vmem_limit_bytes=vmem * MIB)
    return pltpu.CompilerParams(
        collective_id=collective_id, has_side_effects=True, vmem_limit_bytes=vmem * MIB
    )


def each_rows(total, step, body):
    def run(i, carry):
        body(pl.ds(pl.multiple_of(i * step, step), step))
        return carry

    lax.fori_loop(0, total // step, run, 0)


class Spread:
    def __init__(self, wires, place, block, out):
        self.wires, self.place, self.out = wires, place, out
        mine = out.at[place.xl, place.xh, place.c]
        self.far = {k: wires.to(place.at(dx=k), block, mine) for k in (1, 3, 2)}
        self.rest = [wires.to(place.at(dc=1), block, mine)]
        self.local = wires.here(block, mine)

    def forward(self):
        for k in (1, 3, 2):
            self.far[k].wait_recv()
            xl, xh = self.place.chip(-k)
            got = self.out.at[xl, xh, self.place.c]
            self.rest.append(self.wires.to(self.place.at(dc=1), got, got))

    def finish(self):
        self.local.wait()
        for copy in self.rest:
            copy.wait()
        for copy in self.far.values():
            copy.wait_send()


class Collect:
    def __init__(self, wires, place, parts, got, own, half, arrived):
        self.wires, self.place = wires, place
        self.got, self.own, self.half, self.arrived = got, own, half, arrived
        self.swap, self.load = {}, {}
        for k in (1, 3, 2, 0):
            xl, xh = place.chip(k)
            self.swap[k] = wires.to(
                place.at(dc=1), parts.at[xl, xh, 1 - place.c], got.at[k]
            )
            self.load[k] = wires.here(parts.at[xl, xh, place.c], own.at[k])

    def pass_on(self):
        self.far = {}
        for k in (1, 3, 2):
            self.swap[k].wait_recv()
            self.load[k].wait()

            def add(rows, k=k):
                both = self.own[k, rows].astype(F32) + self.got[k, rows].astype(F32)
                self.half[k - 1, rows] = both.astype(self.half.dtype)

            each_rows(BLK, 16, add)
            self.far[k] = self.wires.to(
                self.place.at(dx=k), self.half.at[k - 1], self.arrived.at[k - 1]
            )

    def arrive(self):
        self.swap[0].wait_recv()
        self.load[0].wait()
        for k in (1, 3, 2):
            self.far[k].wait_recv()

    def total(self, rows):
        total = self.own[0, rows].astype(F32) + self.got[0, rows].astype(F32)
        for k in range(3):
            total = total + self.arrived[k, rows].astype(F32)
        return total

    def finish(self):
        for copy in self.swap.values():
            copy.wait_send()
        for copy in self.far.values():
            copy.wait_send()


def collect_scratch(width, dtype):
    return [
        pltpu.VMEM((4, BLK, width), dtype),
        pltpu.VMEM((4, BLK, width), dtype),
        pltpu.VMEM((3, BLK, width), dtype),
        pltpu.VMEM((3, BLK, width), dtype),
    ]


def cell_peers(place):
    return [place.at(dx=1), place.at(dx=2), place.at(dx=3), place.at(dc=1)]


def plane_peers(place):
    return [place.at(dy=k) for k in (1, 2, 3)] + [place.at(dz=k) for k in (1, 2, 3)]


def open_kernel(
    x_own,
    cot_own,
    att,
    small,
    exp,
    mask,
    live,
    in_all,
    cot_all,
    att_full,
    near_rows,
    far_rows,
    mask_both,
    live_both,
    send,
    recv,
    near,
):
    p = Place()
    w = Wires(send, recv, near)
    greet(cell_peers(p) + plane_peers(p) + [p.at(dx=2, dc=1)])
    xl, y, z, t = p.xl, p.y, p.z, p.t
    rows_t = pl.ds(pl.multiple_of(t * 16, 16), 16)
    mine = att_full.at[xl, y, z]
    small_mine = mine.at[rows_t, pl.ds(1024, 128)]
    smalls = [w.to(p.at(dx=a, dc=b), small, small_mine) for a, b in ((0, 1), (2, 0), (2, 1))]
    att_swap = w.to(p.partner(), att.at[1 - xl], mine.at[:, pl.ds(0, 1024)])
    local = [
        w.here(small, small_mine),
        w.here(att.at[xl], mine.at[:, pl.ds(0, 1024)]),
    ]
    tokens = Spread(w, p, x_own, in_all)
    exp_swap = w.to(p.partner(), exp.at[1 - xl], far_rows.at[z])
    masks = [
        w.to(p.partner(), mask, mask_both.at[xl]),
        w.to(p.partner(), live, live_both.at[xl]),
    ]
    later = [
        w.here(mask, mask_both.at[xl]),
        w.here(live, live_both.at[xl]),
        w.here(exp.at[xl], near_rows.at[y]),
    ]
    for copy in smalls:
        copy.wait_recv()
    for copy in local:
        copy.wait()
    strip = mine.at[:, pl.ds(1024, 128)]
    small_swap = w.to(p.partner(), strip, strip)
    att_near = [w.to(p.at(dy=k), mine, mine) for k in (1, 3, 2)]
    att_swap.wait_recv()
    small_swap.wait_recv()
    theirs = att_full.at[1 - xl, y, z]
    att_far = [w.to(p.at(dz=k), theirs, theirs) for k in (1, 3, 2)]
    exp_near = [w.to(p.at(dy=k), exp.at[xl], near_rows.at[y]) for k in (1, 3, 2)]
    exp_swap.wait_recv()
    exp_far = [w.to(p.at(dz=k), far_rows.at[z], far_rows.at[z]) for k in (1, 3, 2)]
    for copy in att_near + att_far:
        copy.wait_recv()
    whole = att_full.at[xl, :, z]
    att_end = [w.to(p.at(dz=k), whole, whole) for k in (1, 3, 2)]
    whole = att_full.at[1 - xl, y]
    att_end += [w.to(p.at(dy=k), whole, whole) for k in (1, 3, 2)]
    tokens.forward()
    cots = Spread(w, p, cot_own, cot_all)
    cots.forward()
    tokens.finish()
    cots.finish()
    for copy in masks + exp_near + exp_far + att_end + later:
        copy.wait()
    for copy in smalls + [att_swap, small_swap, exp_swap] + att_near + att_far:
        copy.wait_send()


def opening(x_own, cot_own, att, small, exp, mask, live):
    cell = jax.ShapeDtypeStruct((2, 2, 2, BLK, D), BF16)
    return pl.pallas_call(
        open_kernel,
        name="opening",
        out_shape=[
            cell,
            cell,
            jax.ShapeDtypeStruct((2, 4, 4, 64, AW), BF16),
            jax.ShapeDtypeStruct((4, 64, EW), BF16),
            jax.ShapeDtypeStruct((4, 64, EW), BF16),
            jax.ShapeDtypeStruct((2, SEQ, 128), BF16),
            jax.ShapeDtypeStruct((2, 16, SEQ), BF16),
        ],
        in_specs=[ANY] * 7,
        out_specs=[ANY] * 7,
        scratch_shapes=wire_scratch(48, 16),
        compiler_params=params(0),
    )(x_own, cot_own, att, small, exp, mask, live)


def middle_kernel(
    branch, near_rows, far_rows, x_own, gains, state, mid_all, exp_full,
    got, own, half, arrived, block, send, recv, near,
):
    p = Place()
    w = Wires(send, recv, near)
    xl, y, z = p.xl, p.y, p.z
    greet(cell_peers(p) + [p.at(dy=1), p.at(dy=3), p.at(dz=1), p.at(dz=3)])
    sums = Collect(w, p, branch, got, own, half, arrived)
    mine = exp_full.at[xl, :, z]
    theirs = exp_full.at[1 - xl, y]
    near_up = w.to(p.at(dz=1), near_rows, mine)
    near_down = w.to(p.at(dz=3), near_rows, mine)
    far_up = w.to(p.at(dy=1), far_rows, theirs)
    far_down = w.to(p.at(dy=3), far_rows, theirs)
    local = [w.here(near_rows, mine), w.here(far_rows, theirs)]
    sums.pass_on()
    sums.arrive()

    def norm(rows):
        now = x_own[rows].astype(F32) + sums.total(rows)
        state[rows] = now
        scale = lax.rsqrt(jnp.mean(now * now, axis=-1, keepdims=True) + EPS)
        block[rows] = (now * scale * gains[1:2]).astype(BF16)

    each_rows(BLK, 16, norm)
    tokens = Spread(w, p, block, mid_all)
    below = lax.rem(z + 3, 4)
    above = lax.rem(z + 1, 4)
    left = lax.rem(y + 3, 4)
    right = lax.rem(y + 1, 4)
    relays = []
    near_up.wait_recv()
    part = exp_full.at[xl, pl.ds(0, 2), below]
    relays.append(w.to(p.at(dz=1), part, part))
    far_up.wait_recv()
    part = exp_full.at[1 - xl, left, pl.ds(0, 2)]
    relays.append(w.to(p.at(dy=1), part, part))
    near_down.wait_recv()
    part = exp_full.at[xl, pl.ds(2, 2), above]
    relays.append(w.to(p.at(dz=3), part, part))
    far_down.wait_recv()
    part = exp_full.at[1 - xl, right, pl.ds(2, 2)]
    relays.append(w.to(p.at(dy=3), part, part))
    tokens.forward()
    tokens.finish()
    sums.finish()
    for copy in local + relays:
        copy.wait()
    for copy in (near_up, near_down, far_up, far_down):
        copy.wait_send()


def middle(branch, near_rows, far_rows, x_own, gains):
    return pl.pallas_call(
        middle_kernel,
        name="middle",
        out_shape=[
            jax.ShapeDtypeStruct((BLK, D), F32),
            jax.ShapeDtypeStruct((2, 2, 2, BLK, D), BF16),
            jax.ShapeDtypeStruct((2, 4, 4, 64, EW), BF16),
        ],
        in_specs=[ANY, ANY, ANY, VMEM, VMEM],
        out_specs=[VMEM, ANY, ANY],
        scratch_shapes=collect_scratch(D, BF16)
        + [pltpu.VMEM((BLK, D), BF16)]
        + wire_scratch(32, 16),
        compiler_params=params(1),
    )(branch, near_rows, far_rows, x_own, gains)


def split_dot(value, other, dims):
    high = value.astype(BF16)
    low = (value - high.astype(F32)).astype(BF16)
    dot = functools.partial(
        lax.dot_general, dimension_numbers=(dims, ((), ())), preferred_element_type=F32
    )
    return dot(high, other) + dot(low, other)


def norm_back(value, gain, grad):
    scale = lax.rsqrt(jnp.mean(value * value, axis=-1, keepdims=True) + EPS)
    shaped = grad * gain
    along = jnp.mean(shaped * value, axis=-1, keepdims=True)
    return scale * shaped - value * (scale * scale * scale * along), grad * value * scale


def turn_kernel(
    mid_part, route, gu, dn, state, cot_own, soft, small, gains,
    branch_grad, state_grad, gain_grad, logit_grad, near_rows, far_rows,
    got, own, half, arrived, rgot, rown, rhalf, rarrived, from_router, block,
    near_in, far_in, send, recv, near,
):
    p = Place()
    w = Wires(send, recv, near)
    xl, y, z = p.xl, p.y, p.z
    greet(cell_peers(p) + plane_peers(p))
    routes = Collect(w, p, route, rgot, rown, rhalf, rarrived)
    sums = Collect(w, p, mid_part, got, own, half, arrived)
    gu_cols, dn_cols = pl.ds(0, GU), pl.ds(GU, EW - GU)
    sent = []
    for k in (1, 3, 2):
        to_z, to_y = lax.rem(z + k, 4), lax.rem(y + k, 4)
        for source, cols in ((gu, gu_cols), (dn, dn_cols)):
            sent.append(
                w.to(p.at(dz=k), source.at[xl, :, to_z], near_in.at[k - 1, :, :, cols])
            )
            sent.append(
                w.to(p.at(dy=k), source.at[1 - xl, to_y], far_in.at[k - 1, :, :, cols])
            )
    local = []
    for source, cols in ((gu, gu_cols), (dn, dn_cols)):
        local.append(w.here(source.at[xl, :, z], near_rows.at[:, :, cols]))
        local.append(w.here(source.at[1 - xl, y], far_rows.at[:, :, cols]))
    routes.pass_on()
    sums.pass_on()
    routes.arrive()

    def router(rows):
        chance = soft[rows]
        grad = routes.total(rows)
        grad = chance * (grad - jnp.sum(chance * grad, axis=-1, keepdims=True))
        logit_grad[rows] = grad

    each_rows(BLK, 16, router)
    from_router[...] = split_dot(logit_grad[...], small[...], ((1,), (1,)))
    sums.arrive()
    gain_grad[...] = jnp.zeros_like(gain_grad)

    def back(rows):
        grad = sums.total(rows) + from_router[rows]
        change, gain_part = norm_back(state[rows], gains[1:2], grad)
        total = cot_own[rows].astype(F32) + change
        state_grad[rows] = total
        block[rows] = total.astype(BF16)
        gain_grad[0:1] += jnp.sum(gain_part, axis=0, keepdims=True)

    each_rows(BLK, 16, back)
    tokens = Spread(w, p, block, branch_grad)
    tokens.forward()
    for copy in local:
        copy.wait()
    for copy in sent:
        copy.wait_recv()
    for rows_ref, in_ref in ((near_rows, near_in), (far_rows, far_in)):
        for b in range(4):

            def add(rows, b=b, rows_ref=rows_ref, in_ref=in_ref):
                total = rows_ref[b, rows].astype(F32)
                for k in range(3):
                    total = total + in_ref[k, b, rows].astype(F32)
                rows_ref[b, rows] = total.astype(BF16)

            each_rows(64, 16, add)
    tokens.finish()
    sums.finish()
    routes.finish()
    for copy in sent:
        copy.wait_send()


def turn(mid_part, route, gu, dn, state, cot_own, soft, small, gains):
    part = jax.ShapeDtypeStruct((4, 64, EW), BF16)
    return pl.pallas_call(
        turn_kernel,
        name="turn",
        out_shape=[
            jax.ShapeDtypeStruct((2, 2, 2, BLK, D), BF16),
            jax.ShapeDtypeStruct((BLK, D), F32),
            jax.ShapeDtypeStruct((8, D), F32),
            jax.ShapeDtypeStruct((BLK, 128), F32),
            part,
            part,
        ],
        in_specs=[ANY] * 4 + [VMEM] * 5,
        out_specs=[ANY] + [VMEM] * 5,
        scratch_shapes=collect_scratch(D, BF16)
        + collect_scratch(128, F32)
        + [
            pltpu.VMEM((BLK, D), F32),
            pltpu.VMEM((BLK, D), BF16),
            pltpu.VMEM((3, 4, 64, EW), BF16),
            pltpu.VMEM((3, 4, 64, EW), BF16),
        ]
        + wire_scratch(48, 16),
        compiler_params=params(2),
    )(mid_part, route, gu, dn, state, cot_own, soft, small, gains)


def close_kernel(
    in_part, mixed, near_rows, far_rows, att_grad, state, state_grad, x_own, gains,
    input_grad, output, exp_sum, att_sum, small_sum,
    got, own, half, arrived, mgot, mown, mhalf, marrived,
    near_in, far_in, far_sum, att_near_in, att_far_in, att_near, att_far,
    att_near_end, att_far_end, att_far_sum, exp_got, att_got, small_all, small_in,
    send, recv, near,
):
    p = Place()
    w = Wires(send, recv, near)
    xl, y, z = p.xl, p.y, p.z
    greet(cell_peers(p) + plane_peers(p) + [p.at(dx=2, dc=1)])
    sums = Collect(w, p, in_part, got, own, half, arrived)
    sent = []
    atts = []
    exps = []
    for k in (1, 3, 2):
        to_z, to_y = lax.rem(z + k, 4), lax.rem(y + k, 4)
        atts.append(w.to(p.at(dz=k), att_grad.at[xl, :, to_z], att_near_in.at[k - 1]))
        atts.append(w.to(p.at(dy=k), att_grad.at[1 - xl, to_y], att_far_in.at[k - 1]))
    for k in (1, 3, 2):
        to_z, to_y = lax.rem(z + k, 4), lax.rem(y + k, 4)
        exps.append(w.to(p.at(dy=k), near_rows.at[to_y], near_in.at[k - 1]))
        exps.append(w.to(p.at(dz=k), far_rows.at[to_z], far_in.at[k - 1]))
    local = [
        w.here(att_grad.at[xl, :, z], att_near),
        w.here(att_grad.at[1 - xl, y], att_far),
        w.here(near_rows.at[y], near_in.at[3]),
        w.here(far_rows.at[z], far_in.at[3]),
    ]
    sums.pass_on()
    mixes = Collect(w, p, mixed, mgot, mown, mhalf, marrived)
    sums.arrive()

    def back(rows):
        change, _ = norm_back(x_own[rows].astype(F32), gains[0:1], sums.total(rows))
        input_grad[rows] = state_grad[rows] + change

    each_rows(BLK, 16, back)
    mixes.pass_on()
    for copy in local:
        copy.wait()
    for copy in atts:
        copy.wait_recv()
    for rows_ref, in_ref in ((att_near, att_near_in), (att_far, att_far_in)):
        for b in range(4):

            def add(rows, b=b, rows_ref=rows_ref, in_ref=in_ref):
                total = rows_ref[b, rows].astype(F32)
                for k in range(3):
                    total = total + in_ref[k, b, rows].astype(F32)
                rows_ref[b, rows] = total.astype(BF16)

            each_rows(64, 16, add)
    ends = []
    for k in (1, 3, 2):
        to_z, to_y = lax.rem(z + k, 4), lax.rem(y + k, 4)
        ends.append(w.to(p.at(dy=k), att_near.at[to_y], att_near_end.at[k - 1]))
        ends.append(w.to(p.at(dz=k), att_far.at[to_z], att_far_end.at[k - 1]))
    for copy in exps:
        copy.wait_recv()

    def exp_far(rows):
        total = far_in[3, rows].astype(F32)
        for k in range(3):
            total = total + far_in[k, rows].astype(F32)
        far_sum[rows] = total.astype(BF16)

    each_rows(64, 16, exp_far)
    exp_swap = w.to(p.partner(), far_sum, exp_got)

    def exp_near(rows):
        total = near_in[3, rows].astype(F32)
        for k in range(3):
            total = total + near_in[k, rows].astype(F32)
        exp_sum[0, rows] = total

    each_rows(64, 16, exp_near)
    mixes.arrive()

    def finish(rows):
        output[rows] = (state[rows] + mixes.total(rows)).astype(BF16)

    each_rows(BLK, 16, finish)
    for copy in ends:
        copy.wait_recv()

    def att_far_add(rows):
        total = att_far[z, rows].astype(F32)
        for k in range(3):
            total = total + att_far_end[k, rows].astype(F32)
        att_far_sum[rows] = total.astype(BF16)

    each_rows(64, 16, att_far_add)
    att_swap = w.to(p.partner(), att_far_sum, att_got)

    def att_near_add(rows):
        total = att_near[y, rows].astype(F32)
        for k in range(3):
            total = total + att_near_end[k, rows].astype(F32)
        att_sum[0, rows] = total

    each_rows(64, 16, att_near_add)
    exp_swap.wait_recv()
    exp_sum[1] = exp_got[...].astype(F32)
    att_swap.wait_recv()
    att_sum[1] = att_got[...].astype(F32)
    small_all[...] = att_sum[0, :, 1024:] + att_sum[1, :, 1024:]
    smalls = []
    for n, (a, b) in enumerate(((0, 1), (2, 0), (2, 1))):
        dest = lax.rem(p.xh + a // 2, 2) * 2 + lax.rem(p.c + b, 2)
        smalls.append(
            w.to(
                p.at(dx=a, dc=b),
                small_all.at[pl.ds(pl.multiple_of(dest * 16, 16), 16)],
                small_in.at[n],
            )
        )
    for copy in smalls:
        copy.wait_recv()
    total = small_all[pl.ds(pl.multiple_of(p.t * 16, 16), 16)]
    for n in range(3):
        total = total + small_in[n]
    small_sum[...] = total
    sums.finish()
    mixes.finish()
    for copy in atts + exps + ends + [exp_swap, att_swap] + smalls:
        copy.wait_send()


def closing(in_part, mixed, near_rows, far_rows, att_grad, state, state_grad, x_own, gains):
    return pl.pallas_call(
        close_kernel,
        name="closing",
        out_shape=[
            jax.ShapeDtypeStruct((BLK, D), F32),
            jax.ShapeDtypeStruct((BLK, D), BF16),
            jax.ShapeDtypeStruct((2, 64, EW), F32),
            jax.ShapeDtypeStruct((2, 64, AW), F32),
            jax.ShapeDtypeStruct((16, 128), F32),
        ],
        in_specs=[ANY] * 5 + [VMEM] * 4,
        out_specs=[VMEM] * 5,
        scratch_shapes=collect_scratch(D, BF16)
        + collect_scratch(D, BF16)
        + [
            pltpu.VMEM((4, 64, EW), BF16),
            pltpu.VMEM((4, 64, EW), BF16),
            pltpu.VMEM((64, EW), BF16),
            pltpu.VMEM((3, 4, 64, AW), BF16),
            pltpu.VMEM((3, 4, 64, AW), BF16),
            pltpu.VMEM((4, 64, AW), BF16),
            pltpu.VMEM((4, 64, AW), BF16),
            pltpu.VMEM((3, 64, AW), BF16),
            pltpu.VMEM((3, 64, AW), BF16),
            pltpu.VMEM((64, AW), BF16),
            pltpu.VMEM((64, EW), BF16),
            pltpu.VMEM((64, AW), BF16),
            pltpu.VMEM((64, 128), F32),
            pltpu.VMEM((3, 16, 128), F32),
        ]
        + wire_scratch(48, 16),
        compiler_params=params(3),
    )(in_part, mixed, near_rows, far_rows, att_grad, state, state_grad, x_own, gains)


def dot(a, b, dims=((1,), (0,))):
    return lax.dot_general(a, b, (dims, ((), ())), preferred_element_type=F32)


def turn_half(v):
    return pltpu.roll(v, HD // 2, 1)


def attend_kernel(
    x, w_att, gains, head_gains, cos, sin, live, normed, proj, qkv, attended, branch
):
    def norm(rows):
        v = x[rows].astype(F32)
        scale = lax.rsqrt(jnp.mean(v * v, axis=-1, keepdims=True) + EPS)
        normed[rows] = (v * scale * gains[0:1]).astype(BF16)

    each_rows(SEQ, 16, norm)
    for c in range(3):
        cols = pl.ds(c * 256, 256)
        proj[:, cols] = dot(normed[...], w_att[:, cols])
    for h in range(2):
        for c, factor in ((0, HD ** (-0.5)), (1, 1.0)):
            cols = pl.ds(c * 256 + h * HD, HD)
            v = proj[:, cols]
            scale = lax.rsqrt(jnp.mean(v * v, axis=-1, keepdims=True) + EPS)
            v = v * scale * head_gains[c : c + 1, h * HD : (h + 1) * HD]
            v = (v * cos[...] + turn_half(v) * sin[...]) * factor
            qkv[:, cols] = v.astype(BF16)
    qkv[:, 512:] = proj[:, 512:].astype(BF16)
    for h in range(2):
        q, k, v = (qkv[:, pl.ds(c * 256 + h * HD, HD)] for c in range(3))
        scores = dot(q, k, ((1,), (1,)))
        weights = jnp.exp(scores - jnp.max(scores, axis=-1, keepdims=True)) * live[0, 0:1]
        probs = (weights / jnp.sum(weights, axis=-1, keepdims=True)).astype(BF16)
        attended[:, pl.ds(h * HD, HD)] = dot(probs, v).astype(BF16)
    for n in range(4):
        rows = pl.ds(n * 512, 512)
        branch[:, rows] = dot(
            attended[...], w_att[rows, 768:1024], ((1,), (1,))
        ).astype(BF16)


def whole(shape):
    return pl.BlockSpec(shape, lambda s: (0,) * len(shape), pipeline_mode=pl.Buffered(1))


def by_seq(width):
    return pl.BlockSpec((SEQ, width), lambda s: (s, 0))


def attend(x, w_att, gains, head_gains, cos, sin, live):
    flops = 2 * ROWS * D * 1024 + 2 * 2 * 4 * SEQ * SEQ * HD
    return pl.pallas_call(
        attend_kernel,
        name="attend",
        grid=(2,),
        out_shape=[
            jax.ShapeDtypeStruct((ROWS, D), BF16),
            jax.ShapeDtypeStruct((ROWS, 768), F32),
            jax.ShapeDtypeStruct((ROWS, 768), BF16),
            jax.ShapeDtypeStruct((ROWS, 256), BF16),
            jax.ShapeDtypeStruct((ROWS, D), BF16),
        ],
        in_specs=[
            by_seq(D),
            whole((D, AW)),
            whole((8, D)),
            whole((8, 256)),
            whole((SEQ, HD)),
            whole((SEQ, HD)),
            pl.BlockSpec((1, 16, SEQ), lambda s: (s, 0, 0)),
        ],
        out_specs=[by_seq(D), by_seq(768), by_seq(768), by_seq(256), by_seq(D)],
        compiler_params=params(),
        cost_estimate=pl.CostEstimate(flops=flops, bytes_accessed=20 * MIB, transcendentals=0),
    )(x, w_att, gains, head_gains, cos, sin, live)


def attend_back_kernel(
    bg, x, w_att, gains, head_gains, cos, sin, live, proj, qkv,
    proj_grad, in_part, in_gain, head_gain, att_bg,
):
    first = pl.program_id(0) == 0

    @pl.when(first)
    def _():
        in_gain[...] = jnp.zeros_like(in_gain)
        head_gain[...] = jnp.zeros_like(head_gain)

    att_bg[...] = dot(bg[...], w_att[:, 768:1024]).astype(BF16)
    for h in range(2):
        head = pl.ds(h * HD, HD)
        q, k, v = (qkv[:, pl.ds(c * 256 + h * HD, HD)] for c in range(3))
        scores = dot(q, k, ((1,), (1,)))
        weights = jnp.exp(scores - jnp.max(scores, axis=-1, keepdims=True)) * live[0, 0:1]
        probs = weights / jnp.sum(weights, axis=-1, keepdims=True)
        prob_grad = dot(att_bg[:, head], v, ((1,), (1,)))
        inner = jnp.sum(probs * prob_grad, axis=-1, keepdims=True)
        score_grad = (probs * (prob_grad - inner)).astype(BF16)
        value_grad = dot(probs.astype(BF16), att_bg[:, head], ((0,), (0,)))
        proj_grad[:, pl.ds(512 + h * HD, HD)] = value_grad.astype(BF16)
        both = (
            (0, dot(score_grad, k) * HD ** (-0.5)),
            (1, dot(score_grad, q, ((0,), (0,)))),
        )
        for c, grad in both:
            cols = pl.ds(c * 256 + h * HD, HD)
            grad = grad * cos[...] - turn_half(grad) * sin[...]
            gain = head_gains[c : c + 1, h * HD : (h + 1) * HD]
            change, gain_part = norm_back(proj[:, cols], gain, grad)
            proj_grad[:, cols] = change.astype(BF16)
            head_gain[c : c + 1, h * HD : (h + 1) * HD] += jnp.sum(
                gain_part, axis=0, keepdims=True
            )
    for n in range(4):
        rows = pl.ds(n * 128, 128)
        part = dot(proj_grad[rows], w_att[:, :768], ((1,), (1,)))
        in_part[rows] = part.astype(BF16)
        v = x[rows].astype(F32)
        scale = lax.rsqrt(jnp.mean(v * v, axis=-1, keepdims=True) + EPS)
        in_gain[0:1] += jnp.sum(part * v * scale, axis=0, keepdims=True)


def attend_back(bg, x, w_att, gains, head_gains, cos, sin, live, proj, qkv):
    flops = 2 * ROWS * D * 1024 + 2 * 2 * 10 * SEQ * SEQ * HD
    return pl.pallas_call(
        attend_back_kernel,
        name="attend_back",
        grid=(2,),
        out_shape=[
            jax.ShapeDtypeStruct((ROWS, 768), BF16),
            jax.ShapeDtypeStruct((ROWS, D), BF16),
            jax.ShapeDtypeStruct((8, D), F32),
            jax.ShapeDtypeStruct((8, 256), F32),
        ],
        in_specs=[
            by_seq(D),
            by_seq(D),
            whole((D, AW)),
            whole((8, D)),
            whole((8, 256)),
            whole((SEQ, HD)),
            whole((SEQ, HD)),
            pl.BlockSpec((1, 16, SEQ), lambda s: (s, 0, 0)),
            by_seq(768),
            by_seq(768),
        ],
        out_specs=[by_seq(768), by_seq(D), whole((8, D)), whole((8, 256))],
        scratch_shapes=[pltpu.VMEM((SEQ, 256), BF16)],
        compiler_params=params(),
        cost_estimate=pl.CostEstimate(flops=flops, bytes_accessed=20 * MIB, transcendentals=0),
    )(bg, x, w_att, gains, head_gains, cos, sin, live, proj, qkv)


TILE = 256


def expert_kernel(
    mid, cot, w_exp, small, mask, pre_grad, gated, mid_part, mixed_part, soft, route, acc, acc2
):
    xl = lax.axis_index("xl")
    logits = dot(mid[...], small[...])
    on = mask[...] > 0
    peak = jnp.max(jnp.where(on, logits, -1e30), axis=-1, keepdims=True)
    chance = jnp.where(on, jnp.exp(jnp.where(on, logits - peak, 0.0)), 0.0)
    chance = chance / jnp.maximum(jnp.sum(chance, axis=-1, keepdims=True), 1.0)
    soft[...] = chance
    lane = lax.broadcasted_iota(jnp.int32, (TILE, 128), 1)
    routed = jnp.zeros((TILE, 128), F32)
    for e in range(HALF_E):
        here = lane == ROUTER_AT + xl * HALF_E + e
        gate = jnp.sum(jnp.where(here, chance, 0.0), axis=-1, keepdims=True)
        pre = dot(mid[...], w_exp[:, pl.ds(e * 512, 512)])
        hidden = dot(cot[...], w_exp[:, pl.ds(GU + e * 256, 256)])
        gate_pre, up_pre = pre[:, :FFS], pre[:, FFS:]
        sig = 1.0 / (1.0 + jnp.exp(-gate_pre))
        silu = gate_pre * sig
        inner = (silu * up_pre).astype(BF16).astype(F32)
        routed = jnp.where(here, jnp.sum(inner * hidden, axis=-1, keepdims=True), routed)
        gated[:, pl.ds(e * FFS, FFS)] = (gate * inner).astype(BF16)
        hidden = gate * hidden
        pre_grad[:, pl.ds(e * 512, FFS)] = (
            hidden * up_pre * (sig + silu * (1.0 - sig))
        ).astype(BF16)
        pre_grad[:, pl.ds(e * 512 + FFS, FFS)] = (hidden * silu).astype(BF16)
    route[...] = routed
    for n in range(4):
        rows = pl.ds(n * 512, 512)
        mid_part[:, rows] = dot(pre_grad[...], w_exp[rows, :GU], ((1,), (1,))).astype(BF16)
        mixed_part[:, rows] = dot(gated[...], w_exp[rows, GU:], ((1,), (1,))).astype(BF16)


def experts(mid, cot, w_exp, small, mask):
    def tile(width):
        return pl.BlockSpec((TILE, width), lambda s: (s, 0))

    return pl.pallas_call(
        expert_kernel,
        name="experts",
        grid=(ROWS // TILE,),
        out_shape=[
            jax.ShapeDtypeStruct((ROWS, GU), BF16),
            jax.ShapeDtypeStruct((ROWS, EW - GU), BF16),
            jax.ShapeDtypeStruct((ROWS, D), BF16),
            jax.ShapeDtypeStruct((ROWS, D), BF16),
            jax.ShapeDtypeStruct((ROWS, 128), F32),
            jax.ShapeDtypeStruct((ROWS, 128), F32),
        ],
        in_specs=[tile(D), tile(D), whole((D, EW)), whole((D, 128)), tile(128)],
        out_specs=[tile(GU), tile(EW - GU), tile(D), tile(D), tile(128), tile(128)],
        scratch_shapes=[pltpu.VMEM((8, 128), F32), pltpu.VMEM((8, 128), F32)],
        compiler_params=params(),
        cost_estimate=pl.CostEstimate(
            flops=2 * ROWS * D * 256 * 30, bytes_accessed=40 * MIB, transcendentals=0
        ),
    )(mid, cot, w_exp, small, mask)


def rotary_tables():
    half = HD // 2
    freqs = np.float32(THETA) ** (-(np.arange(half, dtype=np.float32) * np.float32(2.0 / HD)))
    angles = np.arange(SEQ, dtype=np.float32)[:, None] * freqs[None, :].astype(np.float32)
    cos, sin = np.cos(angles), np.sin(angles)
    return (
        np.concatenate([cos, cos], axis=1).astype(np.float32),
        np.concatenate([-sin, sin], axis=1).astype(np.float32),
    )


def local(
    layer_input, cotangent, lengths, expert_ids, gains, w_qkv, w_out, w_router, w_gate_up, w_down
):
    xl, xh, c = (lax.axis_index(a) for a in ("xl", "xh", "c"))
    t = xh * 2 + c

    small = jnp.concatenate([gains.T, w_router], axis=1)
    small = jnp.pad(small, ((0, 0), (0, 128 - small.shape[1])))
    out_rows = w_out.reshape(2, 256, 64).transpose(0, 2, 1)
    qkv_rows = w_qkv.reshape(3, 64, 2, 256).transpose(2, 1, 0, 3).reshape(2, 64, 768)
    att = jnp.concatenate([qkv_rows, out_rows], axis=2)
    exp = jnp.concatenate(
        [
            w_gate_up.reshape(2, HALF_E, 2, 64, FFS).transpose(0, 3, 1, 2, 4).reshape(2, 64, GU),
            w_down.reshape(2, HALF_E, FFS, 64).transpose(0, 3, 1, 2).reshape(2, 64, EW - GU),
        ],
        axis=2,
    )
    on = jnp.arange(SEQ, dtype=jnp.int32) < lengths[0]
    number = jnp.arange(128, dtype=jnp.int32) - ROUTER_AT
    named = jnp.zeros((SEQ, 128), bool)
    for k in range(TOPK):
        named = named | (expert_ids[:, k][:, None] == number[None, :])
    mask = (named & on[:, None]).astype(BF16)
    live = jnp.broadcast_to(on[None, :], (16, SEQ)).astype(BF16)

    in_all, cot_all, att_full, near_rows, far_rows, mask_both, live_both = opening(
        layer_input, cotangent, att, small, exp, mask, live
    )
    x_all = in_all.reshape(ROWS, D)
    cot_all = cot_all.reshape(ROWS, D)
    w_att = att_full.reshape(D, AW)
    w_small = w_att[:, 1024:]
    gain_rows = w_small[:, :8].astype(F32).T
    head_start = t * 512 + xl * 256
    head_gains = lax.dynamic_slice(gain_rows, (2, head_start), (2, 256))
    head_gains = jnp.pad(head_gains, ((0, 6), (0, 0)))
    live_both = live_both.astype(F32)
    cos, sin = (jnp.asarray(table) for table in rotary_tables())

    normed, proj, qkv, attended, branch = attend(
        x_all, w_att, gain_rows, head_gains, cos, sin, live_both
    )
    state, mid_all, exp_full = middle(
        branch.reshape(2, 2, 2, BLK, D), near_rows, far_rows, layer_input, gain_rows
    )
    mid = mid_all.reshape(ROWS, D)
    w_exp = exp_full.reshape(D, EW)
    pre_grad, gated, mid_part, mixed_part, soft, route = experts(
        mid, cot_all, w_exp, w_small, mask_both.reshape(ROWS, 128)
    )
    gu = jnp.einsum("sd,sf->df", mid, pre_grad, preferred_element_type=F32).astype(BF16)
    dn = jnp.einsum("sd,sf->df", cot_all, gated, preferred_element_type=F32).astype(BF16)
    own_start = xl * SEQ + t * BLK
    soft_own = lax.dynamic_slice_in_dim(soft, own_start, BLK)
    branch_grad, state_grad, mid_gain, logit_grad, near_sum, far_sum = turn(
        mid_part.reshape(2, 2, 2, BLK, D),
        route.reshape(2, 2, 2, BLK, 128),
        gu.reshape(2, 4, 4, 64, GU),
        dn.reshape(2, 4, 4, 64, EW - GU),
        state,
        cotangent,
        soft_own,
        w_small,
        gain_rows,
    )
    bg = branch_grad.reshape(ROWS, D)
    proj_grad, in_part, in_gain, head_gain = attend_back(
        bg, x_all, w_att, gain_rows, head_gains, cos, sin, live_both, proj, qkv
    )
    qkv_grad = jnp.einsum("sd,sf->df", normed, proj_grad, preferred_element_type=F32)
    out_grad = jnp.einsum("sd,sf->df", bg, attended, preferred_element_type=F32)
    mid_own = lax.dynamic_slice_in_dim(mid, own_start, BLK)
    router_grad = jnp.dot(
        mid_own.astype(F32).T, logit_grad, precision=lax.Precision.HIGHEST
    )[:, ROUTER_AT : ROUTER_AT + E]
    head_rows = lax.dynamic_update_slice(jnp.zeros((2, D), F32), head_gain[:2], (0, head_start))
    gain_part = jnp.concatenate([in_gain[:1], mid_gain[:1], head_rows]).T
    smalls = jnp.concatenate([gain_part, router_grad], axis=1)
    smalls = jnp.pad(smalls, ((0, 0), (0, 128 - smalls.shape[1])))
    att_grad = jnp.concatenate([qkv_grad, out_grad, smalls], axis=1).astype(BF16)
    input_grad, output, exp_sum, att_sum, small_sum = closing(
        in_part.reshape(2, 2, 2, BLK, D),
        mixed_part.reshape(2, 2, 2, BLK, D),
        near_sum,
        far_sum,
        att_grad.reshape(2, 4, 4, 64, AW),
        state,
        state_grad,
        layer_input,
        gain_rows,
    )

    def in_order(sums):
        return jnp.where(xl == 0, sums, sums[::-1])

    gate_up_out = in_order(exp_sum[:, :, :GU]).reshape(2, 64, HALF_E, 2, FFS)
    gate_up_out = gate_up_out.transpose(0, 2, 3, 1, 4).reshape(E, 2, 64, FFS)
    down_out = in_order(exp_sum[:, :, GU:]).reshape(2, 64, HALF_E, FFS)
    down_out = down_out.transpose(0, 2, 3, 1).reshape(E, FFS, 64)
    qkv_out = in_order(att_sum[:, :, :768]).reshape(2, 64, 3, 256)
    qkv_out = qkv_out.transpose(2, 1, 0, 3).reshape(3, 64, 512)
    out_out = in_order(att_sum[:, :, 768:1024]).transpose(0, 2, 1).reshape(512, 64)
    gains_out = small_sum[:, :4].T
    router_out = small_sum[:, ROUTER_AT : ROUTER_AT + E]
    return (output, input_grad, gains_out, qkv_out, out_out, router_out, gate_up_out, down_out)


def solution(mesh):
    split = Mesh(mesh.devices.reshape(SIZES), AXES)
    rows, tensor = P(AXES, None), ("xh", "c")
    return jax.shard_map(
        local,
        mesh=split,
        in_specs=(
            rows,
            rows,
            P(DP),
            P(DP, None),
            P(None, AXES),
            P(None, DP, tensor),
            P(tensor, DP),
            rows,
            P(None, None, DP, tensor),
            P(None, tensor, DP),
        ),
        out_specs=(
            rows,
            rows,
            P(None, AXES),
            P(None, DP, tensor),
            P(tensor, DP),
            rows,
            P(None, None, DP, tensor),
            P(None, tensor, DP),
        ),
        check_vma=False,
    )
```

time: 977 us -> 579 us (0.59)
  Pallas kernels: 0 us -> 490 us
  local copies, waits for them, and re-layouts: 329 us -> 33.4 us
  waiting for transfers between devices: 228 us -> 0 us
  starting transfers between devices: 211 us -> 0 us
  matrix products: 128 us -> 34.8 us
  other arithmetic: 62.1 us -> 11.4 us
    pallas_call x0 -> x7, Pallas kernels: none -> 490 us  [the longest x1 127 us: middle(): pl.pallas_call(middle_kernel, name='middle', out_shape=[jax.ShapeDtypeStr...]
    ppermute x109 -> x0, waiting for transfers between devices: 228 us -> none  [the longest x102 221 us: shift(): return lax.ppermute(v, AXES, perm)]
    ppermute x109 -> x0, starting transfers between devices: 211 us -> none  [the longest x102 206 us: shift(): return lax.ppermute(v, AXES, perm)]
    dot_general x20 -> x5, matrix products: 123 us -> 34.8 us  [the longest x1 13.9 us: local(): jnp.einsum('sd,sf->df', mid, pre_grad, preferred_element_type=F32)]
    dynamic_update_slice x62 -> x1, local copies, waits for them, and re-layouts: 79.3 us -> 0.71 us  [local(): lax.dynamic_update_slice(jnp.zeros((2, D), F32), head_gain[:2], (0, head_...]
    convert_element_type x12 -> x0, local copies, waits for them, and re-layouts: 63 us -> none  [the longest x3 31.7 us: local(): jnp.stack([gate_grad, up_grad], axis=2).astype(BF16).reshape(1024, 2560)]
    squeeze x23 -> x0, local copies, waits for them, and re-layouts: 46.6 us -> none  [the longest x2 17 us: local(): pre_gate = pre[:, :, 0]]
    dot_general x7 -> x1, local copies, waits for them, and re-layouts: 44.2 us -> 6.41 us  [local(): out_grad = jnp.einsum('sd,sf->df', bg, attended, preferred_element_type=F32)]
  transfers between devices with their start and end apart: 109 -> 0, of which waited for: 50 -> 0; matrix products, arithmetic and copies ran while one was open for 43% -> 0% of each run, Pallas kernels for 0% -> 0%
where the time goes in v2:
time: 579 us; the launch traced here: 572 us
  Pallas kernels  490 us (85%)
  matrix products  34.8 us (6%)
  local copies, waits for them, and re-layouts  33.4 us (6%)
  other arithmetic  11.4 us (2%)
    pallas_call x1, Pallas kernels, middle(): pl.pallas_call(middle_kernel, name='middle', out_shape=[jax.ShapeDtypeStr...  127 us
    pallas_call x1, Pallas kernels, opening(): pl.pallas_call(open_kernel, name='opening', out_shape=[cell, cell, jax.Sh...  102 us
    pallas_call x1, Pallas kernels, turn(): pl.pallas_call(turn_kernel, name='turn', out_shape=[jax.ShapeDtypeStruct(...  94.1 us
    pallas_call x1, Pallas kernels, closing(): pl.pallas_call(close_kernel, name='closing', out_shape=[jax.ShapeDtypeStr...  80.7 us
    pallas_call x1, Pallas kernels, experts(): pl.pallas_call(expert_kernel, name='experts', grid=(ROWS // TILE,), out_s...  43.9 us
    pallas_call x1, Pallas kernels, attend_back(): pl.pallas_call(attend_back_kernel, name='attend_back', grid=(2,), out_sha...  21.8 us
    pallas_call x1, Pallas kernels, attend(): pl.pallas_call(attend_kernel, name='attend', grid=(2,), out_shape=[jax.Sh...  20.9 us
    dot_general x1, matrix products, local(): jnp.einsum('sd,sf->df', mid, pre_grad, preferred_element_type=F32)  13.9 us

profile of v2, /device:TPU:1, one launch (start us, length us, event | category | flops | bytes accessed | tf_op | source)
XLA Modules:
  0.0 571.8 jit_solution(11976982476911502026)
XLA Ops:
  0.7 1.0 fusion.10
  2.4 1.9 and_convert_fusion.mask
  4.3 0.6 broadcast_in_dim.4.live
  4.9 1.8 copy.68
  6.7 0.4 reshape.123
  7.1 1.2 copy.69
  8.3 0.4 reshape.125
  8.7 1.0 pad_maximum_fusion.1.exp
  9.9 0.2 reshape.120
  10.2 0.7 pad_maximum_fusion.2.att
  11.0 0.7 fusion.6.small
  11.7 102.0 %opening.1 = (bf16[2,2,2,128,2048]{4,3,2,1,0:T(8,128)(2,1)}, bf16[2,2,2,128,2048]{4,3,2,1,0:T(8,128)(2,1)}, bf16[2,4,4,64,1152]{4,3,2,1,0:T(8,128)(2,1)}, bf16[4...) custom-call(bf16[128,2048]{1,0:T(8,128)(2,1)} %x_own.5, ...), custom_call_target="tpu_custom_call" | custom-call | tf_op jit(solution)/shard_map/opening/pallas_call | solution.py:280
  113.7 1.1 slice.84
  114.9 0.7 fusion.9
  115.7 0.6 pad.14.head_gains
  116.3 1.4 convert_element_type.30.live
  117.7 20.9 %attend.1 = (bf16[1024,2048]{1,0:T(8,128)(2,1)}, f32[1024,768]{1,0:T(8,128)}, bf16[1024,768]{1,0:T(8,128)(2,1)}, bf16[1024,256]{1,0:T(8,128)(2,1)}, bf16[1024,2048]{1,0:T(8,128)(2,1)}) custom-call(bf16[1024,2048]{1,0:T(8,128)(2,1)} %bitcast.120, bf16[2048,1152]{1,0:T(8,128)(2,1)} %bitcast.102, f32[8,2048]{1,0:T(8,128)} %get-tuple-element.105.gains, ...), custom_call_target="tpu_custom_call" | custom-call | flops 4831838208 | bytes 20971520 | tf_op jit(solution)/shard_map/attend/pallas_call | solution.py:706
  138.6 126.7 %middle.1 = (f32[128,2048]{1,0:T(8,128)}, bf16[2,2,2,128,2048]{4,3,2,1,0:T(8,128)(2,1)}, bf16[2,4,4,64,3840]{4,3,2,1,0:T(8,128)(2,1)}) custom-call(bf16[2,2,2,128,2048]{4,3,2,1,0:T(8,128)(2,1)} %bitcast.85, bf16[4,64,3840]{2,1,0:T(8,128)(2,1)} %get-tuple-element.48.near_rows, bf16[4,64,3840]{2,1,0:T(8,128)(2,1)} %get-tuple-element.49.far_rows, ...), custom_call_target="tpu_custom_call" | custom-call | tf_op jit(solution)/shard_map/middle/pallas_call | solution.py:353
  265.3 1.9 slice.85.small
  267.2 43.9 %experts.1 = (bf16[1024,2560]{1,0:T(8,128)(2,1)}, bf16[1024,1280]{1,0:T(8,128)(2,1)}, bf16[1024,2048]{1,0:T(8,128)(2,1)}, bf16[1024,2048]{1,0:T(8,128)(2,1)}, f32[1024,128]{1,0:T(8,128)}, /*index=5*/f32[1024,128]{1,0:T(8,128)}) custom-call(bf16[1024,2048]{1,0:T(8,128)(2,1)} %bitcast.106, bf16[1024,2048]{1,0:T(8,128)(2,1)} %bitcast.122, ...), custom_call_target="tpu_custom_call" | custom-call | flops 32212254720 | bytes 41943040 | tf_op jit(solution)/shard_map/experts/pallas_call | solution.py:850
  311.1 9.3 %convolution_convert_fusion.1 = bf16[2048,1280]{1,0:T(8,128)(2,1)} fusion(bf16[1024,2048]{1,0:T(8,128)(2,1)S(1)} %bitcast.123, bf16[1024,1280]{1,0:T(8,128)(2,1)} %get-tuple-element.57), kind=kOutput, calls=%fused_computation.1 | convolution fusion | flops 5371330560 | bytes 12058624 | tf_op jit(solution)/shard_map/sd,sf->df/dot_general | solution.py:935
  320.4 13.9 %convolution_convert_fusion = bf16[2048,2560]{1,0:T(8,128)(2,1)} fusion(bf16[1024,2048]{1,0:T(8,128)(2,1)S(1)} %bitcast.108, bf16[1024,2560]{1,0:T(8,128)(2,1)S(1)} %copy-done.12), kind=kOutput, calls=%fused_computation | convolution fusion | flops 10742661120 | bytes 19922944 | tf_op jit(solution)/shard_map/sd,sf->df/dot_general | solution.py:934
  334.3 1.5 constant_dynamic-slice_fusion.soft
  335.7 94.1 %turn.1 = (bf16[2,2,2,128,2048]{4,3,2,1,0:T(8,128)(2,1)}, f32[128,2048]{1,0:T(8,128)}, f32[8,2048]{1,0:T(8,128)}, f32[128,128]{1,0:T(8,128)}, bf16[4,64,3840]{2,...) custom-call(bf16[2,2,2,128,2048]{4,3,2,1,0:T(8,128)(2,1)} %bitcast.88, f32[2,2,2,128,128]{4,3,2,1,0:T(8,128)} %bitcast.98, ...), custom_call_target="tpu_custom_call" | custom-call | tf_op jit(solution)/shard_map/turn/pallas_call | solution.py:462
  429.9 21.8 %attend_back.1 = (bf16[1024,768]{1,0:T(8,128)(2,1)}, bf16[1024,2048]{1,0:T(8,128)(2,1)}, f32[8,2048]{1,0:T(8,128)}, f32[8,256]{1,0:T(8,128)}) custom-call(bf16[1024,2048]{1,0:T(8,128)(2,1)} %bitcast.83, bf16[1024,2048]{1,0:T(8,128)(2,1)} %bitcast.121, bf16[2048,1152]{1,0:T(8,128)(2,1)} %bitcast.104, f32[8,2048]{1,0:T(8,128)} %get-tuple-element.105.gains, ...), custom_call_target="tpu_custom_call" | custom-call | flops 5637144576 | bytes 20971520 | tf_op jit(solution)/shard_map/attend_back/pallas_call | solution.py:779
  451.6 5.4 convolution_convert_fusion.2
  457.1 6.4 %copy.52 = bf16[2048,1024]{1,0:T(8,128)(2,1)} copy(bf16[2048,1024]{0,1:T(8,128)(2,1)} %bitcast.84) | data formatting | bytes 8388608 | tf_op jit(solution)/shard_map/sd,sf->df/dot_general | solution.py:954
  463.5 4.6 convolution_convert_fusion.3
  468.1 0.7 slice_dynamic-update-slice_fusion
  468.8 0.8 slice.96
  469.6 0.8 slice.95
  470.5 1.7 fusion.1
  472.2 1.0 copy.61
  473.3 1.1 pad.15.clone
  474.4 4.7 pad_maximum_fusion.att_grad
  479.1 80.7 %closing.1 = (f32[128,2048]{1,0:T(8,128)}, bf16[128,2048]{1,0:T(8,128)(2,1)}, f32[2,64,3840]{2,1,0:T(8,128)}, f32[2,64,1152]{2,1,0:T(8,128)}, f32[16,128]{1,0:T(8,128)}) custom-call(bf16[2,2,2,128,2048]{4,3,2,1,0:T(8,128)(2,1)} %bitcast.82, bf16[2,2,2,128,2048]{4,3,2,1,0:T(8,128)(2,1)} %bitcast.81, bf16[4,64,3840]{2,1,0:T(8,128)(2,1)} %get-tuple-element.65.near_rows, ...), custom_call_target="tpu_custom_call" | custom-call | tf_op jit(solution)/shard_map/closing/pallas_call | solution.py:619
  559.8 1.4 slice.82
  561.3 0.8 reshape.143
  562.2 1.2 copy.56
  563.4 1.1 slice.83
  564.8 1.0 copy.57
  566.2 0.3 copy.54
  566.5 1.1 reshape.141
  567.6 0.7 copy.63
  568.2 0.7 copy.58
  568.9 0.7 slice.81
  569.6 0.8 copy.76
  570.4 1.0 copy.77
  (47 shorter events, 1.4 us)
Async XLA Ops:
  0.6 9.0 %copy-start.3 = (bf16[3,64,512]{2,1,0:T(8,128)(2,1)S(1)}, bf16[3,64,512]{2,1,0:T(8,128)(2,1)}, u32[]{:S(2)}) copy-start(bf16[3,64,512]{2,1,0:T(8,128)(2,1)} %param.17) | copy-start | bytes 589828
  0.6 9.5 %copy-start.6 = (bf16[512,64]{0,1:T(8,128)(2,1)S(1)}, bf16[512,64]{0,1:T(8,128)(2,1)}, u32[]{:S(2)}) copy-start(bf16[512,64]{0,1:T(8,128)(2,1)} %param.18) | copy-start | bytes 196612
  2.4 8.5 %copy-start.9 = (bf16[4,16]{1,0:T(4,128)(2,1)S(1)}, bf16[4,16]{1,0:T(4,128)(2,1)}, u32[]{:S(2)}) copy-start(bf16[4,16]{1,0:T(4,128)(2,1)} %param.16) | copy-start | bytes 388
  2.4 8.6 %copy-start.8 = (bf16[16,10]{1,0:T(8,128)(2,1)S(1)}, bf16[16,10]{1,0:T(8,128)(2,1)}, u32[]{:S(2)}) copy-start(bf16[16,10]{1,0:T(8,128)(2,1)} %param.19) | copy-start | bytes 964
  267.2 43.9 %copy-start.10 = (bf16[2,2,2,128,2048]{4,3,2,1,0:T(8,128)(2,1)S(1)}, bf16[2,2,2,128,2048]{4,3,2,1,0:T(8,128)(2,1)}, u32[]{:S(2)}) copy-start(bf16[2,2,2,128,2048]{4,3,2,1,0:T(8,128)(2,1)} %get-tuple-element.51) | copy-start | bytes 12582916
  311.1 9.3 %copy-start.5 = (bf16[2,2,2,128,2048]{4,3,2,1,0:T(8,128)(2,1)S(1)}, bf16[2,2,2,128,2048]{4,3,2,1,0:T(8,128)(2,1)}, u32[]{:S(2)}) copy-start(bf16[2,2,2,128,2048]{4,3,2,1,0:T(8,128)(2,1)} %get-tuple-element.50) | copy-start | bytes 12582916
  311.1 9.3 %copy-start.12 = (bf16[1024,2560]{1,0:T(8,128)(2,1)S(1)}, bf16[1024,2560]{1,0:T(8,128)(2,1)}, u32[]{:S(2)}) copy-start(bf16[1024,2560]{1,0:T(8,128)(2,1)} %get-tuple-element.56) | copy-start | bytes 15728644
  429.9 21.8 %copy-start.11 = (bf16[1024,2048]{1,0:T(8,128)(2,1)S(1)}, bf16[1024,2048]{1,0:T(8,128)(2,1)}, u32[]{:S(2)}) copy-start(bf16[1024,2048]{1,0:T(8,128)(2,1)} %get-tuple-element.67) | copy-start | bytes 12582916
  463.5 7.0 %copy-start.4 = (f32[128,128]{1,0:T(8,128)S(1)}, f32[128,128]{1,0:T(8,128)}, u32[]{:S(2)}) copy-start(f32[128,128]{1,0:T(8,128)} %get-tuple-element.73) | copy-start | bytes 196612
  562.2 3.7 copy-start.2
  564.6 3.6 copy-start.7
  564.6 4.9 copy-start.1
  564.8 5.5 copy-start

commit v3 on v2

--- a/solution.py
+++ b/solution.py
@@ -130,34 +130,47 @@
             got = self.out.at[xl, xh, self.place.c]
             self.rest.append(self.wires.to(self.place.at(dc=1), got, got))
 
-    def finish(self):
+    def arrived(self):
         self.local.wait()
         for copy in self.rest:
-            copy.wait()
-        for copy in self.far.values():
+            copy.wait_recv()
+
+    def finish(self):
+        for copy in self.rest + list(self.far.values()):
             copy.wait_send()
 
 
 class Collect:
     def __init__(self, wires, place, parts, got, own, half, arrived):
-        self.wires, self.place = wires, place
+        self.wires, self.place, self.parts = wires, place, parts
         self.got, self.own, self.half, self.arrived = got, own, half, arrived
-        self.swap, self.load = {}, {}
-        for k in (1, 3, 2, 0):
-            xl, xh = place.chip(k)
-            self.swap[k] = wires.to(
-                place.at(dc=1), parts.at[xl, xh, 1 - place.c], got.at[k]
+        self.swap, self.load, self.far = {}, {}, {}
+
+    def begin(self, steps=(1, 3, 2, 0)):
+        for k in steps:
+            xl, xh = self.place.chip(k)
+            self.swap[k] = self.wires.to(
+                self.place.at(dc=1), self.parts.at[xl, xh, 1 - self.place.c], self.got.at[k]
             )
-            self.load[k] = wires.here(parts.at[xl, xh, place.c], own.at[k])
-
-    def pass_on(self):
-        self.far = {}
-        for k in (1, 3, 2):
+            if self.own is not None:
+                self.load[k] = self.wires.here(
+                    self.parts.at[xl, xh, self.place.c], self.own.at[k]
+                )
+
+    def mine(self, k, rows):
+        if self.own is not None:
+            return self.own[k, rows]
+        xl, xh = self.place.chip(k)
+        return self.parts[xl, xh, self.place.c, rows]
+
+    def pass_on(self, steps=(1, 3, 2)):
+        for k in steps:
             self.swap[k].wait_recv()
-            self.load[k].wait()
+            if self.own is not None:
+                self.load[k].wait()
 
             def add(rows, k=k):
-                both = self.own[k, rows].astype(F32) + self.got[k, rows].astype(F32)
+                both = self.mine(k, rows).astype(F32) + self.got[k, rows].astype(F32)
                 self.half[k - 1, rows] = both.astype(self.half.dtype)
 
             each_rows(BLK, 16, add)
@@ -167,12 +180,13 @@
 
     def arrive(self):
         self.swap[0].wait_recv()
-        self.load[0].wait()
+        if self.own is not None:
+            self.load[0].wait()
         for k in (1, 3, 2):
             self.far[k].wait_recv()
 
     def total(self, rows):
-        total = self.own[0, rows].astype(F32) + self.got[0, rows].astype(F32)
+        total = self.mine(0, rows).astype(F32) + self.got[0, rows].astype(F32)
         for k in range(3):
             total = total + self.arrived[k, rows].astype(F32)
         return total
@@ -193,6 +207,14 @@
     ]
 
 
+def dot(a, b, dims=((1,), (0,))):
+    return lax.dot_general(a, b, (dims, ((), ())), preferred_element_type=F32)
+
+
+def turn_half(v):
+    return pltpu.roll(v, HD // 2, 1)
+
+
 def cell_peers(place):
     return [place.at(dx=1), place.at(dx=2), place.at(dx=3), place.at(dc=1)]
 
@@ -201,53 +223,29 @@
     return [place.at(dy=k) for k in (1, 2, 3)] + [place.at(dz=k) for k in (1, 2, 3)]
 
 
-def open_kernel(
-    x_own,
-    cot_own,
-    att,
-    small,
-    exp,
-    mask,
-    live,
-    in_all,
-    cot_all,
-    att_full,
-    near_rows,
-    far_rows,
-    mask_both,
-    live_both,
-    send,
-    recv,
-    near,
+def forward_kernel(
+    x_own, cot_own, att, small, exp, mask, live, cos, sin,
+    cot_all, mid_all, exp_full, att_out, normed_out, proj_out, qkv, attended, state, gains,
+    head_gains, mask_both, live_out,
+    x_all, att_full, live_both, near_rows, far_rows, normed, proj, branch,
+    got, half, arrived, block, send, recv, near,
 ):
     p = Place()
     w = Wires(send, recv, near)
     greet(cell_peers(p) + plane_peers(p) + [p.at(dx=2, dc=1)])
     xl, y, z, t = p.xl, p.y, p.z, p.t
+
     rows_t = pl.ds(pl.multiple_of(t * 16, 16), 16)
     mine = att_full.at[xl, y, z]
     small_mine = mine.at[rows_t, pl.ds(1024, 128)]
     smalls = [w.to(p.at(dx=a, dc=b), small, small_mine) for a, b in ((0, 1), (2, 0), (2, 1))]
     att_swap = w.to(p.partner(), att.at[1 - xl], mine.at[:, pl.ds(0, 1024)])
-    local = [
-        w.here(small, small_mine),
-        w.here(att.at[xl], mine.at[:, pl.ds(0, 1024)]),
-    ]
-    tokens = Spread(w, p, x_own, in_all)
-    exp_swap = w.to(p.partner(), exp.at[1 - xl], far_rows.at[z])
-    masks = [
-        w.to(p.partner(), mask, mask_both.at[xl]),
-        w.to(p.partner(), live, live_both.at[xl]),
-    ]
-    later = [
-        w.here(mask, mask_both.at[xl]),
-        w.here(live, live_both.at[xl]),
-        w.here(exp.at[xl], near_rows.at[y]),
-    ]
+    tokens = Spread(w, p, x_own, x_all)
+    mine[:, 0:1024] = att[xl]
+    mine[rows_t, 1024:1152] = small[...]
+    live_both[xl] = live[...]
     for copy in smalls:
         copy.wait_recv()
-    for copy in local:
-        copy.wait()
     strip = mine.at[:, pl.ds(1024, 128)]
     small_swap = w.to(p.partner(), strip, strip)
     att_near = [w.to(p.at(dy=k), mine, mine) for k in (1, 3, 2)]
@@ -255,9 +253,13 @@
     small_swap.wait_recv()
     theirs = att_full.at[1 - xl, y, z]
     att_far = [w.to(p.at(dz=k), theirs, theirs) for k in (1, 3, 2)]
-    exp_near = [w.to(p.at(dy=k), exp.at[xl], near_rows.at[y]) for k in (1, 3, 2)]
-    exp_swap.wait_recv()
-    exp_far = [w.to(p.at(dz=k), far_rows.at[z], far_rows.at[z]) for k in (1, 3, 2)]
+    exp_swap = w.to(p.partner(), exp.at[1 - xl], far_rows.at[z])
+    masks = [
+        w.to(p.partner(), live, live_both.at[xl]),
+        w.to(p.partner(), mask, mask_both.at[xl]),
+    ]
+    local = [w.here(mask, mask_both.at[xl])]
+    near_rows[y] = exp[xl]
     for copy in att_near + att_far:
         copy.wait_recv()
     whole = att_full.at[xl, :, z]
@@ -265,54 +267,84 @@
     whole = att_full.at[1 - xl, y]
     att_end += [w.to(p.at(dy=k), whole, whole) for k in (1, 3, 2)]
     tokens.forward()
+    exp_near = [w.to(p.at(dy=k), exp.at[xl], near_rows.at[y]) for k in (1, 3, 2)]
+    exp_swap.wait_recv()
+    exp_far = [w.to(p.at(dz=k), far_rows.at[z], far_rows.at[z]) for k in (1, 3, 2)]
     cots = Spread(w, p, cot_own, cot_all)
+    for copy in att_end:
+        copy.wait_recv()
+    tokens.arrived()
+
+    for n in range(16):
+        column = att_full[n // 8, n % 8 // 2, pl.ds(n % 2 * 2, 2), :, 1024:1152]
+        column = jnp.transpose(column.astype(F32).reshape(128, 128))
+        gains[:, n * 128 : (n + 1) * 128] = column[:8]
+    start = pl.multiple_of(t * 512 + xl * 256, 256)
+    head_gains[...] = jnp.zeros_like(head_gains)
+    head_gains[0:2] = gains[2:4, pl.ds(start, 256)]
+    masks[0].wait_recv()
+    local.append(w.here(att_full, att_out))
+    local.append(w.here(live_both, live_out))
+
+    sums = Collect(w, p, branch, got, None, half, arrived)
+
+    def project(s):
+        for b in range(4):
+
+            def norm(rows, b=b):
+                v = x_all[s, b // 2, b % 2, rows].astype(F32)
+                scale = lax.rsqrt(jnp.mean(v * v, axis=-1, keepdims=True) + EPS)
+                value = (v * scale * gains[0:1]).astype(BF16)
+                normed[s, pl.ds(pl.multiple_of(b * BLK + rows.start, 16), 16)] = value
+
+            each_rows(BLK, 16, norm)
+        for c in range(3):
+            cols = pl.ds(c * 256, 256)
+            weight = att_full[:, :, :, :, cols].reshape(D, 256)
+            proj[s, :, cols] = dot(normed[s], weight)
+
+    def attend(s):
+        for h in range(2):
+            for c, factor in ((0, HD ** (-0.5)), (1, 1.0)):
+                cols = pl.ds(c * 256 + h * HD, HD)
+                v = proj[s, :, cols]
+                scale = lax.rsqrt(jnp.mean(v * v, axis=-1, keepdims=True) + EPS)
+                v = v * scale * head_gains[c : c + 1, h * HD : (h + 1) * HD]
+                v = (v * cos[...] + turn_half(v) * sin[...]) * factor
+                qkv[s, :, cols] = v.astype(BF16)
+        qkv[s, :, 512:768] = proj[s, :, 512:768].astype(BF16)
+        for h in range(2):
+            q, k, v = (qkv[s, :, pl.ds(c * 256 + h * HD, HD)] for c in range(3))
+            scores = dot(q, k, ((1,), (1,)))
+            weights = jnp.exp(scores - jnp.max(scores, axis=-1, keepdims=True))
+            weights = weights * live_both[s, 0:1].astype(F32)
+            probs = (weights / jnp.sum(weights, axis=-1, keepdims=True)).astype(BF16)
+            attended[s, :, pl.ds(h * HD, HD)] = dot(probs, v).astype(BF16)
+        for n in range(4):
+            weight = att_full[n // 2, pl.ds(n % 2 * 2, 2), :, :, 768:1024].reshape(512, 256)
+            part = dot(attended[s], weight, ((1,), (1,))).astype(BF16)
+            branch[s, :, :, :, pl.ds(n * 512, 512)] = part.reshape(2, 2, BLK, 512)
+
+    first, second = 1 - xl, xl
+    project(first)
+    attend(first)
+    sums.begin((1, 3))
     cots.forward()
-    tokens.finish()
-    cots.finish()
-    for copy in masks + exp_near + exp_far + att_end + later:
-        copy.wait()
-    for copy in smalls + [att_swap, small_swap, exp_swap] + att_near + att_far:
-        copy.wait_send()
-
-
-def opening(x_own, cot_own, att, small, exp, mask, live):
-    cell = jax.ShapeDtypeStruct((2, 2, 2, BLK, D), BF16)
-    return pl.pallas_call(
-        open_kernel,
-        name="opening",
-        out_shape=[
-            cell,
-            cell,
-            jax.ShapeDtypeStruct((2, 4, 4, 64, AW), BF16),
-            jax.ShapeDtypeStruct((4, 64, EW), BF16),
-            jax.ShapeDtypeStruct((4, 64, EW), BF16),
-            jax.ShapeDtypeStruct((2, SEQ, 128), BF16),
-            jax.ShapeDtypeStruct((2, 16, SEQ), BF16),
-        ],
-        in_specs=[ANY] * 7,
-        out_specs=[ANY] * 7,
-        scratch_shapes=wire_scratch(48, 16),
-        compiler_params=params(0),
-    )(x_own, cot_own, att, small, exp, mask, live)
-
-
-def middle_kernel(
-    branch, near_rows, far_rows, x_own, gains, state, mid_all, exp_full,
-    got, own, half, arrived, block, send, recv, near,
-):
-    p = Place()
-    w = Wires(send, recv, near)
-    xl, y, z = p.xl, p.y, p.z
-    greet(cell_peers(p) + [p.at(dy=1), p.at(dy=3), p.at(dz=1), p.at(dz=3)])
-    sums = Collect(w, p, branch, got, own, half, arrived)
-    mine = exp_full.at[xl, :, z]
-    theirs = exp_full.at[1 - xl, y]
-    near_up = w.to(p.at(dz=1), near_rows, mine)
-    near_down = w.to(p.at(dz=3), near_rows, mine)
-    far_up = w.to(p.at(dy=1), far_rows, theirs)
-    far_down = w.to(p.at(dy=3), far_rows, theirs)
-    local = [w.here(near_rows, mine), w.here(far_rows, theirs)]
-    sums.pass_on()
+    for copy in exp_near + exp_far:
+        copy.wait_recv()
+    mine_z = exp_full.at[xl, :, z]
+    mine_y = exp_full.at[1 - xl, y]
+    near_up = w.to(p.at(dz=1), near_rows, mine_z)
+    near_down = w.to(p.at(dz=3), near_rows, mine_z)
+    far_up = w.to(p.at(dy=1), far_rows, mine_y)
+    far_down = w.to(p.at(dy=3), far_rows, mine_y)
+    local += [w.here(near_rows, mine_z), w.here(far_rows, mine_y)]
+    sums.pass_on((1, 3))
+    project(second)
+    attend(second)
+    sums.begin((2, 0))
+    local += [w.here(normed, normed_out), w.here(proj, proj_out)]
+    sums.pass_on((2,))
     sums.arrive()
 
     def norm(rows):
@@ -322,11 +354,9 @@
         block[rows] = (now * scale * gains[1:2]).astype(BF16)
 
     each_rows(BLK, 16, norm)
-    tokens = Spread(w, p, block, mid_all)
-    below = lax.rem(z + 3, 4)
-    above = lax.rem(z + 1, 4)
-    left = lax.rem(y + 3, 4)
-    right = lax.rem(y + 1, 4)
+    mids = Spread(w, p, block, mid_all)
+    below, above = lax.rem(z + 3, 4), lax.rem(z + 1, 4)
+    left, right = lax.rem(y + 3, 4), lax.rem(y + 1, 4)
     relays = []
     near_up.wait_recv()
     part = exp_full.at[xl, pl.ds(0, 2), below]
@@ -340,31 +370,63 @@
     far_down.wait_recv()
     part = exp_full.at[1 - xl, right, pl.ds(2, 2)]
     relays.append(w.to(p.at(dy=3), part, part))
-    tokens.forward()
-    tokens.finish()
-    sums.finish()
-    for copy in local + relays:
+    mids.forward()
+    mids.arrived()
+    cots.arrived()
+    for copy in masks[1:]:
+        copy.wait_recv()
+    for copy in relays:
+        copy.wait_recv()
+    for copy in local:
         copy.wait()
-    for copy in (near_up, near_down, far_up, far_down):
+    for group in (tokens, cots, mids, sums):
+        group.finish()
+    for copy in (
+        smalls + [att_swap, small_swap, exp_swap] + masks + att_near + att_far + att_end
+        + exp_near + exp_far + relays + [near_up, near_down, far_up, far_down]
+    ):
         copy.wait_send()
 
 
-def middle(branch, near_rows, far_rows, x_own, gains):
+def forward(x_own, cot_own, att, small, exp, mask, live, cos, sin):
+    cell = jax.ShapeDtypeStruct((2, 2, 2, BLK, D), BF16)
     return pl.pallas_call(
-        middle_kernel,
-        name="middle",
+        forward_kernel,
+        name="forward",
         out_shape=[
+            cell,
+            cell,
+            jax.ShapeDtypeStruct((2, 4, 4, 64, EW), BF16),
+            jax.ShapeDtypeStruct((2, 4, 4, 64, AW), BF16),
+            jax.ShapeDtypeStruct((2, SEQ, D), BF16),
+            jax.ShapeDtypeStruct((2, SEQ, 768), F32),
+            jax.ShapeDtypeStruct((2, SEQ, 768), BF16),
+            jax.ShapeDtypeStruct((2, SEQ, 256), BF16),
             jax.ShapeDtypeStruct((BLK, D), F32),
-            jax.ShapeDtypeStruct((2, 2, 2, BLK, D), BF16),
-            jax.ShapeDtypeStruct((2, 4, 4, 64, EW), BF16),
+            jax.ShapeDtypeStruct((8, D), F32),
+            jax.ShapeDtypeStruct((8, 256), F32),
+            jax.ShapeDtypeStruct((2, SEQ, 128), BF16),
+            jax.ShapeDtypeStruct((2, 16, SEQ), BF16),
         ],
-        in_specs=[ANY, ANY, ANY, VMEM, VMEM],
-        out_specs=[VMEM, ANY, ANY],
-        scratch_shapes=collect_scratch(D, BF16)
-        + [pltpu.VMEM((BLK, D), BF16)]
-        + wire_scratch(32, 16),
-        compiler_params=params(1),
-    )(branch, near_rows, far_rows, x_own, gains)
+        in_specs=[VMEM] * 9,
+        out_specs=[ANY] * 6 + [VMEM] * 5 + [ANY] * 2,
+        scratch_shapes=[
+            pltpu.VMEM((2, 2, 2, BLK, D), BF16),
+            pltpu.VMEM((2, 4, 4, 64, AW), BF16),
+            pltpu.VMEM((2, 16, SEQ), BF16),
+            pltpu.VMEM((4, 64, EW), BF16),
+            pltpu.VMEM((4, 64, EW), BF16),
+            pltpu.VMEM((2, SEQ, D), BF16),
+            pltpu.VMEM((2, SEQ, 768), F32),
+            pltpu.VMEM((2, 2, 2, BLK, D), BF16),
+            pltpu.VMEM((4, BLK, D), BF16),
+            pltpu.VMEM((3, BLK, D), BF16),
+            pltpu.VMEM((3, BLK, D), BF16),
+            pltpu.VMEM((BLK, D), BF16),
+        ]
+        + wire_scratch(80, 16),
+        compiler_params=params(0, 60),
+    )(x_own, cot_own, att, small, exp, mask, live, cos, sin)
 
 
 def split_dot(value, other, dims):
@@ -383,35 +445,115 @@
     return scale * shaped - value * (scale * scale * scale * along), grad * value * scale
 
 
+class Reduce:
+    def __init__(self, wires, up, down, blocks, here, halves, mains):
+        self.wires, self.up, self.down = wires, up, down
+        self.blocks, self.here, self.halves, self.mains = blocks, here, halves, mains
+        self.first, self.second = {}, {}
+
+    def begin(self, cols):
+        opposite = self.blocks(lax.rem(self.here + 2, 4))
+        low, high = pl.ds(0, 2), pl.ds(2, 2)
+        self.first[cols] = (
+            self.wires.to(self.up, opposite.at[low, :, self.span(cols)], self.half(0, cols)),
+            self.wires.to(self.down, opposite.at[high, :, self.span(cols)], self.half(1, cols)),
+        )
+
+    @staticmethod
+    def span(cols):
+        return pl.ds(*cols)
+
+    def half(self, side, cols):
+        return self.halves.at[side, :, :, self.span(cols)]
+
+    def relay(self, cols):
+        span = self.span(cols)
+        sent = []
+        for side, device in ((0, self.up), (1, self.down)):
+            self.first[cols][side].wait_recv()
+            block = self.blocks(lax.rem(self.here + (1 if side == 0 else 3), 4))
+            for b in range(2):
+                at = (side * 2 + b, slice(None), span)
+                total = block[at].astype(F32) + self.halves[side, b, :, span].astype(F32)
+                block[at] = total.astype(BF16)
+            sent.append(
+                self.wires.to(device, block.at[:, :, span], self.mains.at[side, :, :, span])
+            )
+        self.second[cols] = sent
+
+    def total(self, cols, store):
+        span = self.span(cols)
+        for copy in self.second[cols]:
+            copy.wait_recv()
+        own = self.blocks(self.here)
+        for b in range(4):
+            total = own[b, :, span].astype(F32)
+            for side in range(2):
+                total = total + self.mains[side, b, :, span].astype(F32)
+            store(b, span, total)
+
+    def finish(self):
+        for copies in list(self.first.values()) + list(self.second.values()):
+            for copy in copies:
+                copy.wait_send()
+
+
 def turn_kernel(
-    mid_part, route, gu, dn, state, cot_own, soft, small, gains,
+    mid_part, route, mid, cot, pre_grad, gated, state, cot_own, soft, small, gains,
     branch_grad, state_grad, gain_grad, logit_grad, near_rows, far_rows,
     got, own, half, arrived, rgot, rown, rhalf, rarrived, from_router, block,
-    near_in, far_in, send, recv, near,
+    mid_here, cot_here, pre_here, gated_here, dw, near_half, far_half, near_main, far_main,
+    send, recv, near,
 ):
     p = Place()
     w = Wires(send, recv, near)
     xl, y, z = p.xl, p.y, p.z
-    greet(cell_peers(p) + plane_peers(p))
+    greet(cell_peers(p) + [p.at(dy=1), p.at(dy=3), p.at(dz=1), p.at(dz=3)])
     routes = Collect(w, p, route, rgot, rown, rhalf, rarrived)
     sums = Collect(w, p, mid_part, got, own, half, arrived)
-    gu_cols, dn_cols = pl.ds(0, GU), pl.ds(GU, EW - GU)
-    sent = []
-    for k in (1, 3, 2):
-        to_z, to_y = lax.rem(z + k, 4), lax.rem(y + k, 4)
-        for source, cols in ((gu, gu_cols), (dn, dn_cols)):
-            sent.append(
-                w.to(p.at(dz=k), source.at[xl, :, to_z], near_in.at[k - 1, :, :, cols])
-            )
-            sent.append(
-                w.to(p.at(dy=k), source.at[1 - xl, to_y], far_in.at[k - 1, :, :, cols])
-            )
-    local = []
-    for source, cols in ((gu, gu_cols), (dn, dn_cols)):
-        local.append(w.here(source.at[xl, :, z], near_rows.at[:, :, cols]))
-        local.append(w.here(source.at[1 - xl, y], far_rows.at[:, :, cols]))
+    routes.begin()
+    sums.begin()
+    loads = [w.here(mid, mid_here), w.here(cot, cot_here)]
+
+    def fetch(e):
+        return (
+            w.here(pre_grad.at[:, pl.ds(e * 512, 512)], pre_here.at[e % 2]),
+            w.here(gated.at[:, pl.ds(e * FFS, FFS)], gated_here.at[e % 2]),
+        )
+
+    ready = {0: fetch(0), 1: fetch(1)}
+    along_z = Reduce(
+        w, p.at(dz=1), p.at(dz=3), lambda k: dw.at[xl, :, k], z, near_half, near_main
+    )
+    along_y = Reduce(
+        w, p.at(dy=1), p.at(dy=3), lambda k: dw.at[1 - xl, k], y, far_half, far_main
+    )
     routes.pass_on()
     sums.pass_on()
+    for copy in loads:
+        copy.wait()
+    groups = [(e * 768, 768) for e in range(HALF_E)]
+    for e in range(HALF_E):
+        for copy in ready[e]:
+            copy.wait()
+        for n in range(4):
+            at = pl.ds(n * 512, 512)
+            to = (n // 2, pl.ds(n % 2 * 2, 2))
+            grad = dot(mid_here[:, at], pre_here[e % 2], ((0,), (0,)))
+            dw[(*to, slice(None), slice(None), pl.ds(e * 768, 512))] = grad.astype(
+                BF16
+            ).reshape(2, 4, 64, 512)
+            grad = dot(cot_here[:, at], gated_here[e % 2], ((0,), (0,)))
+            dw[(*to, slice(None), slice(None), pl.ds(e * 768 + 512, 256))] = grad.astype(
+                BF16
+            ).reshape(2, 4, 64, 256)
+        along_z.begin(groups[e])
+        along_y.begin(groups[e])
+        if e + 2 < HALF_E:
+            ready[e + 2] = fetch(e + 2)
+        if e > 0:
+            along_z.relay(groups[e - 1])
+            along_y.relay(groups[e - 1])
     routes.arrive()
 
     def router(rows):
@@ -422,6 +564,8 @@
 
     each_rows(BLK, 16, router)
     from_router[...] = split_dot(logit_grad[...], small[...], ((1,), (1,)))
+    along_z.relay(groups[-1])
+    along_y.relay(groups[-1])
     sums.arrive()
     gain_grad[...] = jnp.zeros_like(gain_grad)
 
@@ -435,29 +579,27 @@
 
     each_rows(BLK, 16, back)
     tokens = Spread(w, p, block, branch_grad)
-    tokens.forward()
-    for copy in local:
-        copy.wait()
-    for copy in sent:
-        copy.wait_recv()
-    for rows_ref, in_ref in ((near_rows, near_in), (far_rows, far_in)):
-        for b in range(4):
-
-            def add(rows, b=b, rows_ref=rows_ref, in_ref=in_ref):
-                total = rows_ref[b, rows].astype(F32)
-                for k in range(3):
-                    total = total + in_ref[k, b, rows].astype(F32)
-                rows_ref[b, rows] = total.astype(BF16)
-
-            each_rows(64, 16, add)
+
+    def keep(rows_ref):
+        def store(b, span, total):
+            rows_ref[b, :, span] = total.astype(BF16)
+
+        return store
+
+    for e in range(HALF_E):
+        if e == 3:
+            tokens.forward()
+        along_z.total(groups[e], keep(near_rows))
+        along_y.total(groups[e], keep(far_rows))
+    tokens.arrived()
     tokens.finish()
     sums.finish()
     routes.finish()
-    for copy in sent:
-        copy.wait_send()
-
-
-def turn(mid_part, route, gu, dn, state, cot_own, soft, small, gains):
+    along_z.finish()
+    along_y.finish()
+
+
+def turn(mid_part, route, mid, cot, pre_grad, gated, state, cot_own, soft, small, gains):
     part = jax.ShapeDtypeStruct((4, 64, EW), BF16)
     return pl.pallas_call(
         turn_kernel,
@@ -470,19 +612,26 @@
             part,
             part,
         ],
-        in_specs=[ANY] * 4 + [VMEM] * 5,
+        in_specs=[ANY] * 6 + [VMEM] * 5,
         out_specs=[ANY] + [VMEM] * 5,
         scratch_shapes=collect_scratch(D, BF16)
         + collect_scratch(128, F32)
         + [
             pltpu.VMEM((BLK, D), F32),
             pltpu.VMEM((BLK, D), BF16),
-            pltpu.VMEM((3, 4, 64, EW), BF16),
-            pltpu.VMEM((3, 4, 64, EW), BF16),
+            pltpu.VMEM((ROWS, D), BF16),
+            pltpu.VMEM((ROWS, D), BF16),
+            pltpu.VMEM((2, ROWS, 512), BF16),
+            pltpu.VMEM((2, ROWS, FFS), BF16),
+            pltpu.VMEM((2, 4, 4, 64, EW), BF16),
+            pltpu.VMEM((2, 2, 64, EW), BF16),
+            pltpu.VMEM((2, 2, 64, EW), BF16),
+            pltpu.VMEM((2, 4, 64, EW), BF16),
+            pltpu.VMEM((2, 4, 64, EW), BF16),
         ]
-        + wire_scratch(48, 16),
-        compiler_params=params(2),
-    )(mid_part, route, gu, dn, state, cot_own, soft, small, gains)
+        + wire_scratch(72, 40),
+        compiler_params=params(2, 60),
+    )(mid_part, route, mid, cot, pre_grad, gated, state, cot_own, soft, small, gains)
 
 
 def close_kernel(
@@ -498,6 +647,7 @@
     xl, y, z = p.xl, p.y, p.z
     greet(cell_peers(p) + plane_peers(p) + [p.at(dx=2, dc=1)])
     sums = Collect(w, p, in_part, got, own, half, arrived)
+    sums.begin()
     sent = []
     atts = []
     exps = []
@@ -517,6 +667,7 @@
     ]
     sums.pass_on()
     mixes = Collect(w, p, mixed, mgot, mown, mhalf, marrived)
+    mixes.begin()
     sums.arrive()
 
     def back(rows):
@@ -651,48 +802,6 @@
     )(in_part, mixed, near_rows, far_rows, att_grad, state, state_grad, x_own, gains)
 
 
-def dot(a, b, dims=((1,), (0,))):
-    return lax.dot_general(a, b, (dims, ((), ())), preferred_element_type=F32)
-
-
-def turn_half(v):
-    return pltpu.roll(v, HD // 2, 1)
-
-
-def attend_kernel(
-    x, w_att, gains, head_gains, cos, sin, live, normed, proj, qkv, attended, branch
-):
-    def norm(rows):
-        v = x[rows].astype(F32)
-        scale = lax.rsqrt(jnp.mean(v * v, axis=-1, keepdims=True) + EPS)
-        normed[rows] = (v * scale * gains[0:1]).astype(BF16)
-
-    each_rows(SEQ, 16, norm)
-    for c in range(3):
-        cols = pl.ds(c * 256, 256)
-        proj[:, cols] = dot(normed[...], w_att[:, cols])
-    for h in range(2):
-        for c, factor in ((0, HD ** (-0.5)), (1, 1.0)):
-            cols = pl.ds(c * 256 + h * HD, HD)
-            v = proj[:, cols]
-            scale = lax.rsqrt(jnp.mean(v * v, axis=-1, keepdims=True) + EPS)
-            v = v * scale * head_gains[c : c + 1, h * HD : (h + 1) * HD]
-            v = (v * cos[...] + turn_half(v) * sin[...]) * factor
-            qkv[:, cols] = v.astype(BF16)
-    qkv[:, 512:] = proj[:, 512:].astype(BF16)
-    for h in range(2):
-        q, k, v = (qkv[:, pl.ds(c * 256 + h * HD, HD)] for c in range(3))
-        scores = dot(q, k, ((1,), (1,)))
-        weights = jnp.exp(scores - jnp.max(scores, axis=-1, keepdims=True)) * live[0, 0:1]
-        probs = (weights / jnp.sum(weights, axis=-1, keepdims=True)).astype(BF16)
-        attended[:, pl.ds(h * HD, HD)] = dot(probs, v).astype(BF16)
-    for n in range(4):
-        rows = pl.ds(n * 512, 512)
-        branch[:, rows] = dot(
-            attended[...], w_att[rows, 768:1024], ((1,), (1,))
-        ).astype(BF16)
-
-
 def whole(shape):
     return pl.BlockSpec(shape, lambda s: (0,) * len(shape), pipeline_mode=pl.Buffered(1))
 
@@ -701,36 +810,8 @@
     return pl.BlockSpec((SEQ, width), lambda s: (s, 0))
 
 
-def attend(x, w_att, gains, head_gains, cos, sin, live):
-    flops = 2 * ROWS * D * 1024 + 2 * 2 * 4 * SEQ * SEQ * HD
-    return pl.pallas_call(
-        attend_kernel,
-        name="attend",
-        grid=(2,),
-        out_shape=[
-            jax.ShapeDtypeStruct((ROWS, D), BF16),
-            jax.ShapeDtypeStruct((ROWS, 768), F32),
-            jax.ShapeDtypeStruct((ROWS, 768), BF16),
-            jax.ShapeDtypeStruct((ROWS, 256), BF16),
-            jax.ShapeDtypeStruct((ROWS, D), BF16),
-        ],
-        in_specs=[
-            by_seq(D),
-            whole((D, AW)),
-            whole((8, D)),
-            whole((8, 256)),
-            whole((SEQ, HD)),
-            whole((SEQ, HD)),
-            pl.BlockSpec((1, 16, SEQ), lambda s: (s, 0, 0)),
-        ],
-        out_specs=[by_seq(D), by_seq(768), by_seq(768), by_seq(256), by_seq(D)],
-        compiler_params=params(),
-        cost_estimate=pl.CostEstimate(flops=flops, bytes_accessed=20 * MIB, transcendentals=0),
-    )(x, w_att, gains, head_gains, cos, sin, live)
-
-
 def attend_back_kernel(
-    bg, x, w_att, gains, head_gains, cos, sin, live, proj, qkv,
+    bg, normed, w_att, gains, head_gains, cos, sin, live, proj, qkv,
     proj_grad, in_part, in_gain, head_gain, att_bg,
 ):
     first = pl.program_id(0) == 0
@@ -745,7 +826,7 @@
         head = pl.ds(h * HD, HD)
         q, k, v = (qkv[:, pl.ds(c * 256 + h * HD, HD)] for c in range(3))
         scores = dot(q, k, ((1,), (1,)))
-        weights = jnp.exp(scores - jnp.max(scores, axis=-1, keepdims=True)) * live[0, 0:1]
+        weights = jnp.exp(scores - jnp.max(scores, axis=-1, keepdims=True)) * live[0, 0:1].astype(F32)
         probs = weights / jnp.sum(weights, axis=-1, keepdims=True)
         prob_grad = dot(att_bg[:, head], v, ((1,), (1,)))
         inner = jnp.sum(probs * prob_grad, axis=-1, keepdims=True)
@@ -769,12 +850,14 @@
         rows = pl.ds(n * 128, 128)
         part = dot(proj_grad[rows], w_att[:, :768], ((1,), (1,)))
         in_part[rows] = part.astype(BF16)
-        v = x[rows].astype(F32)
-        scale = lax.rsqrt(jnp.mean(v * v, axis=-1, keepdims=True) + EPS)
-        in_gain[0:1] += jnp.sum(part * v * scale, axis=0, keepdims=True)
-
-
-def attend_back(bg, x, w_att, gains, head_gains, cos, sin, live, proj, qkv):
+        in_gain[0:1] += jnp.sum(part * normed[rows].astype(F32), axis=0, keepdims=True)
+
+    @pl.when(jnp.logical_not(first))
+    def _():
+        in_gain[0:1] = in_gain[0:1] / gains[0:1]
+
+
+def attend_back(bg, normed, w_att, gains, head_gains, cos, sin, live, proj, qkv):
     flops = 2 * ROWS * D * 1024 + 2 * 2 * 10 * SEQ * SEQ * HD
     return pl.pallas_call(
         attend_back_kernel,
@@ -802,7 +885,7 @@
         scratch_shapes=[pltpu.VMEM((SEQ, 256), BF16)],
         compiler_params=params(),
         cost_estimate=pl.CostEstimate(flops=flops, bytes_accessed=20 * MIB, transcendentals=0),
-    )(bg, x, w_att, gains, head_gains, cos, sin, live, proj, qkv)
+    )(bg, normed, w_att, gains, head_gains, cos, sin, live, proj, qkv)
 
 
 TILE = 256
@@ -906,40 +989,31 @@
     mask = (named & on[:, None]).astype(BF16)
     live = jnp.broadcast_to(on[None, :], (16, SEQ)).astype(BF16)
 
-    in_all, cot_all, att_full, near_rows, far_rows, mask_both, live_both = opening(
-        layer_input, cotangent, att, small, exp, mask, live
-    )
-    x_all = in_all.reshape(ROWS, D)
+    cos, sin = (jnp.asarray(table) for table in rotary_tables())
+    (
+        cot_all, mid_all, exp_full, att_full, normed, proj, qkv, attended, state, gain_rows,
+        head_gains, mask_both, live_both,
+    ) = forward(layer_input, cotangent, att, small, exp, mask, live, cos, sin)
     cot_all = cot_all.reshape(ROWS, D)
     w_att = att_full.reshape(D, AW)
     w_small = w_att[:, 1024:]
-    gain_rows = w_small[:, :8].astype(F32).T
-    head_start = t * 512 + xl * 256
-    head_gains = lax.dynamic_slice(gain_rows, (2, head_start), (2, 256))
-    head_gains = jnp.pad(head_gains, ((0, 6), (0, 0)))
-    live_both = live_both.astype(F32)
-    cos, sin = (jnp.asarray(table) for table in rotary_tables())
-
-    normed, proj, qkv, attended, branch = attend(
-        x_all, w_att, gain_rows, head_gains, cos, sin, live_both
-    )
-    state, mid_all, exp_full = middle(
-        branch.reshape(2, 2, 2, BLK, D), near_rows, far_rows, layer_input, gain_rows
-    )
+    normed = normed.reshape(ROWS, D)
+    attended = attended.reshape(ROWS, 256)
     mid = mid_all.reshape(ROWS, D)
     w_exp = exp_full.reshape(D, EW)
+    head_start = t * 512 + xl * 256
     pre_grad, gated, mid_part, mixed_part, soft, route = experts(
         mid, cot_all, w_exp, w_small, mask_both.reshape(ROWS, 128)
     )
-    gu = jnp.einsum("sd,sf->df", mid, pre_grad, preferred_element_type=F32).astype(BF16)
-    dn = jnp.einsum("sd,sf->df", cot_all, gated, preferred_element_type=F32).astype(BF16)
     own_start = xl * SEQ + t * BLK
     soft_own = lax.dynamic_slice_in_dim(soft, own_start, BLK)
     branch_grad, state_grad, mid_gain, logit_grad, near_sum, far_sum = turn(
         mid_part.reshape(2, 2, 2, BLK, D),
         route.reshape(2, 2, 2, BLK, 128),
-        gu.reshape(2, 4, 4, 64, GU),
-        dn.reshape(2, 4, 4, 64, EW - GU),
+        mid,
+        cot_all,
+        pre_grad,
+        gated,
         state,
         cotangent,
         soft_own,
@@ -948,7 +1022,8 @@
     )
     bg = branch_grad.reshape(ROWS, D)
     proj_grad, in_part, in_gain, head_gain = attend_back(
-        bg, x_all, w_att, gain_rows, head_gains, cos, sin, live_both, proj, qkv
+        bg, normed, w_att, gain_rows, head_gains, cos, sin, live_both,
+        proj.reshape(ROWS, 768), qkv.reshape(ROWS, 768),
     )
     qkv_grad = jnp.einsum("sd,sf->df", normed, proj_grad, preferred_element_type=F32)
     out_grad = jnp.einsum("sd,sf->df", bg, attended, preferred_element_type=F32)
@@ -976,10 +1051,9 @@
     def in_order(sums):
         return jnp.where(xl == 0, sums, sums[::-1])
 
-    gate_up_out = in_order(exp_sum[:, :, :GU]).reshape(2, 64, HALF_E, 2, FFS)
-    gate_up_out = gate_up_out.transpose(0, 2, 3, 1, 4).reshape(E, 2, 64, FFS)
-    down_out = in_order(exp_sum[:, :, GU:]).reshape(2, 64, HALF_E, FFS)
-    down_out = down_out.transpose(0, 2, 3, 1).reshape(E, FFS, 64)
+    exp_sum = in_order(exp_sum).reshape(2, 64, HALF_E, 3, FFS)
+    gate_up_out = exp_sum[:, :, :, :2].transpose(0, 2, 3, 1, 4).reshape(E, 2, 64, FFS)
+    down_out = exp_sum[:, :, :, 2].transpose(0, 2, 3, 1).reshape(E, FFS, 64)
     qkv_out = in_order(att_sum[:, :, :768]).reshape(2, 64, 3, 256)
     qkv_out = qkv_out.transpose(2, 1, 0, 3).reshape(3, 64, 512)
     out_out = in_order(att_sum[:, :, 768:1024]).transpose(0, 2, 1).reshape(512, 64)

time: 579 us -> 475 us (0.82)
  Pallas kernels: 490 us -> 399 us
  matrix products: 34.8 us -> 12.3 us
  local copies, waits for them, and re-layouts: 33.4 us -> 39.5 us
    pallas_call x3 -> x1, Pallas kernels: 250 us -> 159 us  [forward(): pl.pallas_call(forward_kernel, name='forward', out_shape=[cell, cell, jax...]
    dot_general x2 -> x0, matrix products: 23.1 us -> none  [the longest x1 13.9 us: local(): jnp.einsum('sd,sf->df', mid, pre_grad, preferred_element_type=F32)]
    dot_general x0 -> x1, local copies, waits for them, and re-layouts: none -> 6.68 us  [local(): jnp.einsum('sd,sf->df', normed, proj_grad, preferred_element_type=F32)]
where the time goes in v3:
time: 475 us; the launch traced here: 466 us
  Pallas kernels  399 us (84%)
  local copies, waits for them, and re-layouts  39.5 us (8%)
  other arithmetic  12.8 us (3%)
  matrix products  12.3 us (3%)
    pallas_call x1, Pallas kernels, forward(): pl.pallas_call(forward_kernel, name='forward', out_shape=[cell, cell, jax...  159 us
    pallas_call x1, Pallas kernels, turn(): pl.pallas_call(turn_kernel, name='turn', out_shape=[jax.ShapeDtypeStruct(...  96.9 us
    pallas_call x1, Pallas kernels, closing(): pl.pallas_call(close_kernel, name='closing', out_shape=[jax.ShapeDtypeStr...  77.8 us
    pallas_call x1, Pallas kernels, experts(): pl.pallas_call(expert_kernel, name='experts', grid=(ROWS // TILE,), out_s...  44.1 us
    pallas_call x1, Pallas kernels, attend_back(): pl.pallas_call(attend_back_kernel, name='attend_back', grid=(2,), out_sha...  21.5 us

profile of v3, /device:TPU:1, one launch (start us, length us, event | category | flops | bytes accessed | tf_op | source)
XLA Modules:
  0.0 465.7 jit_solution(7620121583061641369)
XLA Ops:
  0.7 1.0 fusion.9
  2.4 0.0 copy-start.7
  2.4 1.9 and_convert_fusion.mask
  4.3 0.6 broadcast_in_dim.4.live
  4.9 1.8 copy.64
  6.7 0.4 reshape.120
  7.1 1.2 copy.65
  8.3 0.4 reshape.122
  8.7 1.0 pad_maximum_fusion.1.exp
  9.7 0.1 reshape.116
  9.7 0.2 copy.66
  9.9 0.2 reshape.117
  10.2 0.7 pad_maximum_fusion.2.att
  10.9 0.1 copy.44
  11.0 0.7 fusion.6.small
  11.7 158.8 %forward.1 = (bf16[2,2,2,128,2048]{4,3,2,1,0:T(8,128)(2,1)}, bf16[2,2,2,128,2048]{4,3,2,1,0:T(8,128)(2,1)}, bf16[2,4,4,64,3840]{4,3,2,1,0:T(8,128)(2,1)}, bf16[2...) custom-call(bf16[128,2048]{1,0:T(8,128)(2,1)} %x_own.3, ...), custom_call_target="tpu_custom_call" | custom-call | tf_op jit(solution)/shard_map/forward/pallas_call | solution.py:393
  170.4 1.9 slice.79.small
  172.3 44.1 %experts.1 = (bf16[1024,2560]{1,0:T(8,128)(2,1)}, bf16[1024,1280]{1,0:T(8,128)(2,1)}, bf16[1024,2048]{1,0:T(8,128)(2,1)}, bf16[1024,2048]{1,0:T(8,128)(2,1)}, f32[1024,128]{1,0:T(8,128)}, /*index=5*/f32[1024,128]{1,0:T(8,128)}) custom-call(bf16[1024,2048]{1,0:T(8,128)(2,1)} %bitcast.80, bf16[1024,2048]{1,0:T(8,128)(2,1)} %bitcast.91, ...), custom_call_target="tpu_custom_call" | custom-call | flops 32212254720 | bytes 41943040 | tf_op jit(solution)/shard_map/experts/pallas_call | solution.py:933
  216.4 1.5 constant_dynamic-slice_fusion.soft
  217.9 96.9 %turn.1 = (bf16[2,2,2,128,2048]{4,3,2,1,0:T(8,128)(2,1)}, f32[128,2048]{1,0:T(8,128)}, f32[8,2048]{1,0:T(8,128)}, f32[128,128]{1,0:T(8,128)}, bf16[4,64,3840]{2,...) custom-call(bf16[2,2,2,128,2048]{4,3,2,1,0:T(8,128)(2,1)} %bitcast.93, f32[2,2,2,128,128]{4,3,2,1,0:T(8,128)} %bitcast.102, ...), custom_call_target="tpu_custom_call" | custom-call | tf_op jit(solution)/shard_map/turn/pallas_call | solution.py:604
  314.8 21.5 %attend_back.1 = (bf16[1024,768]{1,0:T(8,128)(2,1)}, bf16[1024,2048]{1,0:T(8,128)(2,1)}, f32[8,2048]{1,0:T(8,128)}, f32[8,256]{1,0:T(8,128)}) custom-call(bf16[1024,2048]{1,0:T(8,128)(2,1)} %bitcast.87, bf16[1024,2048]{1,0:T(8,128)(2,1)} %bitcast.85, bf16[2048,1152]{1,0:T(8,128)(2,1)} %bitcast.108, f32[8,2048]{1,0:T(8,128)} %get-tuple-element.53.gains, ...), custom_call_target="tpu_custom_call" | custom-call | flops 5637144576 | bytes 20971520 | tf_op jit(solution)/shard_map/attend_back/pallas_call | solution.py:862
  336.3 6.7 %copy.47 = bf16[2048,1024]{1,0:T(8,128)(2,1)} copy(bf16[2048,1024]{0,1:T(8,128)(2,1)} %bitcast.86) | data formatting | bytes 8388608 | tf_op jit(solution)/shard_map/sd,sf->df/dot_general | solution.py:1028
  343.0 6.1 %convolution_convert_fusion = bf16[2,4,4,64,768]{4,3,2,1,0:T(8,128)(2,1)S(1)} fusion(bf16[2,4,4,64,1024]{4,3,2,1,0:T(8,128)(2,1)} %bitcast.90, bf16[1024,768]{1,0:T(8,128)(2,1)} %get-tuple-element.64), kind=kOutput, calls=%fused_computation.2 | convolution fusion | flops 3222798336 | bytes 8912896 | tf_op jit(solution)/shard_map/sd,sf->df/dot_general | solution.py:1028
  349.1 6.4 %copy.48 = bf16[2048,1024]{1,0:T(8,128)(2,1)} copy(bf16[2048,1024]{0,1:T(8,128)(2,1)} %bitcast.88) | data formatting | bytes 8388608 | tf_op jit(solution)/shard_map/sd,sf->df/dot_general | solution.py:1029
  355.6 4.6 convolution_convert_fusion.1
  360.1 0.7 slice_dynamic-update-slice_fusion
  360.8 0.8 slice.93
  361.7 0.8 slice.92
  362.6 1.7 fusion.1
  364.3 1.0 copy.57
  365.3 1.1 pad.10.clone
  366.5 4.7 %pad_maximum_fusion.att_grad = bf16[2,4,4,64,1152]{4,3,2,1,0:T(8,128)(2,1)} fusion(bf16[2,4,4,64,128]{4,3,2,1,0:T(8,128)(2,1)S(1)} %bitcast.96, bf16[2,4,4,64,256]{4,3,2,1,0:T(8,128)(2,1)} %convolution_convert_fusion.1, bf16[2,4,4,64,768]{4,3,2,1,0:T(8,128)(2,1)S(1)} %convolution_convert_fusion), kind=kLoop, calls=%fused_computation | loop fusion | flops 14155776 | bytes 9437184 | tf_op jit(solution)/shard_map/concatenate | solution.py:1038
  371.2 77.8 %closing.1 = (f32[128,2048]{1,0:T(8,128)}, bf16[128,2048]{1,0:T(8,128)(2,1)}, f32[2,64,3840]{2,1,0:T(8,128)}, f32[2,64,1152]{2,1,0:T(8,128)}, f32[16,128]{1,0:T(8,128)}) custom-call(bf16[2,2,2,128,2048]{4,3,2,1,0:T(8,128)(2,1)} %bitcast.84, bf16[2,2,2,128,2048]{4,3,2,1,0:T(8,128)(2,1)} %bitcast.83, bf16[4,64,3840]{2,1,0:T(8,128)(2,1)} %get-tuple-element.62.near_rows, ...), custom_call_target="tpu_custom_call" | custom-call | tf_op jit(solution)/shard_map/closing/pallas_call | solution.py:770
  449.0 3.6 reverse_select_fusion
  452.7 2.9 reshape.140
  455.6 0.5 slice_bitcast_fusion
  456.1 1.2 copy.52
  457.3 0.7 slice.84
  458.0 0.9 copy.53
  459.0 0.2 reshape.137
  459.2 0.3 copy.50
  459.5 1.1 reshape.138
  460.6 0.9 slice.75
  461.5 0.7 copy.59
  462.2 0.7 copy.54
  462.8 0.7 slice.76
  463.5 0.8 copy.72
  464.3 1.0 copy.73
  (28 shorter events, 0.2 us)
Async XLA Ops:
  0.6 9.0 %copy-start.3 = (bf16[3,64,512]{2,1,0:T(8,128)(2,1)S(1)}, bf16[3,64,512]{2,1,0:T(8,128)(2,1)}, u32[]{:S(2)}) copy-start(bf16[3,64,512]{2,1,0:T(8,128)(2,1)} %param.17) | copy-start | bytes 589828
  0.6 9.5 %copy-start.5 = (bf16[512,64]{0,1:T(8,128)(2,1)S(1)}, bf16[512,64]{0,1:T(8,128)(2,1)}, u32[]{:S(2)}) copy-start(bf16[512,64]{0,1:T(8,128)(2,1)} %param.18) | copy-start | bytes 196612
  2.4 8.5 %copy-start.8 = (bf16[4,16]{1,0:T(4,128)(2,1)S(1)}, bf16[4,16]{1,0:T(4,128)(2,1)}, u32[]{:S(2)}) copy-start(bf16[4,16]{1,0:T(4,128)(2,1)} %param.16) | copy-start | bytes 388
  2.4 8.6 %copy-start.7 = (bf16[16,10]{1,0:T(8,128)(2,1)S(1)}, bf16[16,10]{1,0:T(8,128)(2,1)}, u32[]{:S(2)}) copy-start(bf16[16,10]{1,0:T(8,128)(2,1)} %param.19) | copy-start | bytes 964
  355.6 7.0 %copy-start.4 = (f32[128,128]{1,0:T(8,128)S(1)}, f32[128,128]{1,0:T(8,128)}, u32[]{:S(2)}) copy-start(f32[128,128]{1,0:T(8,128)} %get-tuple-element.69) | copy-start | bytes 196612
  455.6 3.3 copy-start.2
  457.3 4.9 %copy-start.6 = (f32[16,128]{1,0:T(8,128)S(1)}, f32[16,128]{1,0:T(8,128)}, u32[]{:S(2)}) copy-start(f32[16,128]{1,0:T(8,128)} %get-tuple-element.73) | copy-start | bytes 24580
  457.3 6.2 %copy-start.1 = (bf16[128,2048]{1,0:T(8,128)(2,1)S(1)}, bf16[128,2048]{1,0:T(8,128)(2,1)}, u32[]{:S(2)}) copy-start(bf16[128,2048]{1,0:T(8,128)(2,1)} %get-tuple-element.118) | copy-start | bytes 1572868
  458.0 6.3 %copy-start = (f32[128,2048]{1,0:T(8,128)S(1)}, f32[128,2048]{1,0:T(8,128)}, u32[]{:S(2)}) copy-start(f32[128,2048]{1,0:T(8,128)} %get-tuple-element.119) | copy-start | bytes 3145732
